TPU v7x, 1024 devices: a whole 4x4x32 slice. The times are simulated.
1024 devices in a mesh: ep: 32 (over x, y, core), dp: 32 (over z).
Axes of the slice: x: 4, y: 4, z: 32, core: 2. Of those that a mesh axis runs over, the one named last changes fastest.
Arguments:
- cotangent: bfloat16 [131072, 2048], P(('ep', 'dp')), may hold values from -6 to 6
- route_ids: int32 [131072, 2], P(('ep', 'dp')), may hold values from 0 to 31, all different within a row; in each aligned block of 128 rows (0 to 127, 128 to 255, ...) at most 10 rows name the same one
- route_probs: float32 [131072, 2], P(('ep', 'dp')), may hold values from 0.05 to 0.8
- expert_hidden: bfloat16 [327680, 768], P(('ep', 'dp')), may hold values from -6 to 6
- down_weight: bfloat16 [32, 768, 2048], P('ep'), may hold values from -0.21875 to 0.21875
Outputs:
- layer_out: bfloat16 [131072, 2048], P(('ep', 'dp'))
- router_grad: float32 [131072, 2], P(('ep', 'dp'))
- hidden_grad: bfloat16 [327680, 768], P(('ep', 'dp'))
- weight_grad: float32 [32, 768, 2048], P('ep', 'dp')
Inputs may be any that keep to these rules, and one draw needn't show every extreme that they name: `route_ids`: A token's 2 experts differ. Among the routes of one device's tokens no expert is named more than 10 times, and some device names some expert exactly 10 times.
All inputs are finite; a program needn't handle non-finite values.
Results may differ from a plain program's by a relative error of at most 0.0049.
Values may be sent and summed in bfloat16 or wider, within the bound.
No kernel may reach another device: no remote copies, remote signals or barrier semaphores. Data moves between devices by JAX's collectives and lax.ppermute only.
A program may use at most 64 MiB of HBM per device.

v0:
```python
import jax
import jax.numpy as jnp
from jax import lax
from jax.sharding import PartitionSpec as P


def send_grads(cotangent, route_probs, positions, row_count, capacity, peer_count):
    features = cotangent.shape[1]
    scaled_rows = (route_probs[:, :, None] * cotangent[:, None, :].astype(jnp.float32)).astype(
        jnp.bfloat16
    )
    buffer = (
        jnp.zeros((row_count, features), jnp.bfloat16)
        .at[positions]
        .set(scaled_rows.reshape(-1, features))
    )
    arrived = lax.all_to_all(
        buffer.reshape(peer_count, capacity, features),
        "ep",
        split_axis=0,
        concat_axis=0,
        tiled=True,
    )
    return arrived.reshape(row_count, features)


def forward(
    expert_hidden, weight, cotangent, route_probs, positions, row_count, capacity, peer_count
):
    token_count, features = cotangent.shape
    route_count = route_probs.shape[1]
    local_rows = jnp.dot(expert_hidden, weight, preferred_element_type=jnp.float32).astype(
        jnp.bfloat16
    )
    returned = lax.all_to_all(
        local_rows.reshape(peer_count, capacity, features),
        "ep",
        split_axis=0,
        concat_axis=0,
        tiled=True,
    )
    returned = returned.reshape(row_count, features)
    picked = returned[positions].reshape(token_count, route_count, features)
    layer_out = jnp.sum(route_probs[..., None] * picked.astype(jnp.float32), axis=1).astype(
        jnp.bfloat16
    )
    router_grad = jnp.einsum("td,trd->tr", cotangent, picked, preferred_element_type=jnp.float32)
    router_grad = router_grad * features ** (-0.5)
    return (layer_out, router_grad)


def shards(cotangent, route_ids, route_probs, expert_hidden, down_weight):
    peer_count = lax.axis_size("ep")
    group_count = lax.axis_size("dp")
    row_count = expert_hidden.shape[0]
    capacity = row_count // peer_count
    weight = down_weight[0]
    flat_ids = route_ids.reshape(-1)
    onehot = (flat_ids[:, None] == jnp.arange(peer_count, dtype=jnp.int32)[None, :]).astype(
        jnp.int32
    )
    earlier = jnp.cumsum(onehot, axis=0) - onehot
    positions = flat_ids * capacity + jnp.sum(earlier * onehot, axis=1)
    layer_out, router_grad = forward(
        expert_hidden, weight, cotangent, route_probs, positions, row_count, capacity, peer_count
    )
    arrived = send_grads(cotangent, route_probs, positions, row_count, capacity, peer_count)
    hidden_grad = lax.dot_general(
        arrived, weight, (((1,), (1,)), ((), ())), preferred_element_type=jnp.float32
    )
    hidden_grad = hidden_grad.astype(jnp.bfloat16)
    grad_scale = (group_count * row_count) ** (-0.5)
    full_term = lax.dot_general(
        expert_hidden, arrived, (((0,), (0,)), ((), ())), preferred_element_type=jnp.float32
    )
    weight_grad = lax.psum_scatter(full_term * grad_scale, "dp", scatter_dimension=0, tiled=True)
    return (layer_out, router_grad, hidden_grad, weight_grad[None])


def solution(mesh):
    in_specs = (
        P(("ep", "dp"), None),
        P(("ep", "dp"), None),
        P(("ep", "dp"), None),
        P(("ep", "dp"), None),
        P("ep", None, None),
    )
    out_specs = (
        P(("ep", "dp"), None),
        P(("ep", "dp"), None),
        P(("ep", "dp"), None),
        P("ep", "dp", None),
    )
    return jax.shard_map(shards, mesh=mesh, in_specs=in_specs, out_specs=out_specs, check_vma=False)
```

profile of v0, /device:TPU:8, one launch (start us, length us, event | category | flops | bytes accessed | tf_op | source)
XLA Modules:
  0.0 242.5 jit_solution(8145609890090959237)
XLA Ops:
  7.2 0.8 broadcast_multiply_fusion
  8.1 0.9 copy.20
  8.9 0.1 eq.29
  9.1 0.1 eq.25
  9.2 0.1 copy.19
  9.3 0.1 mul.63
  9.5 0.8 copy.18
  10.2 0.1 mul.68
  10.4 0.6 reduce-window.6
  11.0 0.2 slice_reduce_fusion
  11.2 3.4 %mul.70 = f32[128,2,2048]{2,1,0:T(2,128)} broadcast(bf16[128,2048]{1,0:T(8,128)(2,1)} %param.5), dimensions={0,2} | broadcast | bytes 2621440 | tf_op jit(solution)/shard_map/mul | solution.py:9
  14.6 3.7 %mul.71 = f32[256,2048]{1,0:T(8,128)} reshape(f32[128,2,2048]{2,1,0:T(2,128)} %mul.70) | data formatting | bytes 4194304 | tf_op jit(solution)/shard_map/mul | solution.py:9
  18.4 4.4 %scatter_custom_fusion = bf16[320,2048]{1,0:T(8,128)(2,1)} fusion(s32[256]{0:T(256)S(1)} %bitcast.45, f32[256,2048]{1,0:T(8,128)} %mul.71, f32[256]{0:T(256)S(1)} %mul.68, bf16[]{:T(256)} %constant.6.clone.1), kind=kCustom, calls=%fused_computation.11 | custom fusion | flops 1048576 | bytes 3408898 | tf_op jit(solution)/shard_map/scatter | solution.py:15
  22.8 3.3 %reshape.79 = bf16[32,10,2048]{2,1,0:T(8,128)(2,1)} reshape(bf16[320,2048]{1,0:T(8,128)(2,1)} %scatter_custom_fusion) | data formatting | bytes 2621440 | tf_op jit(solution)/shard_map/reshape | solution.py:18
  26.2 44.4 %all_to_all.10 = bf16[32,10,2048]{2,1,0:T(8,128)(2,1)} all-to-all(bf16[32,10,2048]{2,1,0:T(8,128)(2,1)} %reshape.79), channel_id=1, replica_groups=mesh['ep'=32,'dp'=32] {'ep'}, dimensions={0} | all-to-all | bytes 2621440 | tf_op jit(solution)/shard_map/all_to_all | solution.py:17
  70.5 3.6 %reshape.80 = bf16[320,2048]{1,0:T(8,128)(2,1)} reshape(bf16[32,10,2048]{2,1,0:T(8,128)(2,1)} %all_to_all.10) | data formatting | bytes 2621440 | tf_op jit(solution)/shard_map/reshape | solution.py:24
  74.1 5.9 %multiply_bitcast_fusion = f32[768,2048]{0,1:T(8,128)} fusion(bf16[320,2048]{1,0:T(8,128)(2,1)} %reshape.80, bf16[320,768]{1,0:T(8,128)(2,1)} %param.8), kind=kOutput, calls=%fused_computation.2 | convolution fusion | flops 1008205824 | bytes 8093696 | tf_op jit(solution)/shard_map/dot_general | solution.py:73
  80.0 6.6 %copy.27 = f32[768,2048]{1,0:T(8,128)} copy(f32[768,2048]{0,1:T(8,128)} %multiply_bitcast_fusion) | data formatting | bytes 12582912
  86.7 3.3 %fusion.4 = bf16[320,2048]{1,0:T(8,128)(2,1)} fusion(bf16[320,768]{1,0:T(8,128)(2,1)} %param.8, bf16[1,768,2048]{2,1,0:T(8,128)(2,1)S(1)} %copy-done), kind=kOutput, calls=%fused_computation.7 | convolution fusion | flops 1007288320 | bytes 4947968 | tf_op jit(solution)/shard_map/dot_general | solution.py:32
  90.0 3.3 %reshape.75 = bf16[32,10,2048]{2,1,0:T(8,128)(2,1)} reshape(bf16[320,2048]{1,0:T(8,128)(2,1)} %fusion.4) | data formatting | bytes 2621440 | tf_op jit(solution)/shard_map/reshape | solution.py:36
  93.3 5.8 %all-to-all-start = ((bf16[32,10,2048]{2,1,0:T(8,128)(2,1)}), bf16[32,10,2048]{2,1,0:T(8,128)(2,1)}, u32[]{:S(2)}, u32[]{:S(2)}) async-start(bf16[32,10,2048]{2,1,0:T(8,128)(2,1)} %reshape.75), calls=%async_computation | async-start | bytes 4194304 | tf_op jit(solution)/shard_map/all_to_all | solution.py:35
  99.2 27.1 %all-to-all-done = bf16[32,10,2048]{2,1,0:T(8,128)(2,1)} async-done(((bf16[32,10,2048]{2,1,0:T(8,128)(2,1)}), bf16[32,10,2048]{2,1,0:T(8,128)(2,1)}, u32[]{:S(2)}, u32[]{:S(2)}) %all-to-all-start) | async-done | bytes 1310752 | tf_op jit(solution)/shard_map/all_to_all | solution.py:35
  126.3 3.6 %reshape.76 = bf16[320,2048]{1,0:T(8,128)(2,1)} reshape(bf16[32,10,2048]{2,1,0:T(8,128)(2,1)} %all-to-all-done) | data formatting | bytes 2621440 | tf_op jit(solution)/shard_map/reshape | solution.py:42
  129.9 4.9 %gather_fusion = bf16[256,2048]{1,0:T(8,128)(2,1)} fusion(bf16[320,2048]{1,0:T(8,128)(2,1)} %reshape.76, s32[1024]{0:T(1024)S(1)} %pad_clamp_fusion), kind=kCustom, calls=%fused_computation | custom fusion | bytes 2098176 | tf_op jit(solution)/shard_map/gather | solution.py:43
  134.7 2.6 %reshape.78 = bf16[128,2,2048]{2,1,0:T(2,128)(2,1)} reshape(bf16[256,2048]{1,0:T(8,128)(2,1)} %gather_fusion) | data formatting | bytes 2097152 | tf_op jit(solution)/shard_map/reshape | solution.py:43
  137.3 3.7 %fusion.12 = f32[128,1,2]{2,1,0:T(1,128)S(1)} fusion(bf16[128,2,2048]{2,1,0:T(2,128)(2,1)} %reshape.78, bf16[128,2048,1]{1,0,2:T(8,128)(2,1)} %bitcast.44), kind=kOutput, calls=%fused_computation.13 | convolution fusion | flops 1048576 | bytes 1573888 | tf_op jit(solution)/shard_map/td,trd->tr/dot_general | solution.py:47
  141.0 0.6 bitcast_multiply_fusion
  141.6 5.1 %multiply_reduce_fusion = bf16[128,2048]{1,0:T(8,128)(2,1)} fusion(bf16[128,2,2048]{2,1,0:T(2,128)(2,1)} %reshape.78, f32[128,2]{1,0:T(8,128)S(1)} %copy.18), kind=kLoop, calls=%fused_computation.9 | loop fusion | flops 1310720 | bytes 1573888 | tf_op jit(solution)/shard_map/reduce_sum | solution.py:44
  146.7 3.3 %fusion.7 = bf16[320,768]{1,0:T(8,128)(2,1)} fusion(bf16[320,2048]{1,0:T(8,128)(2,1)} %reshape.80, bf16[1,768,2048]{2,1,0:T(8,128)(2,1)S(1)} %copy-done), kind=kOutput, calls=%fused_computation.10 | convolution fusion | flops 1006878720 | bytes 4947968 | tf_op jit(solution)/shard_map/dot_general | solution.py:68
  150.0 81.2 %reduce-scatter.4.cloned.1.call-done = f32[24,2048]{1,0:T(8,128)} async-done(((f32[768,2048]{1,0:T(8,128)}), f32[24,2048]{1,0:T(8,128)}) %reduce-scatter.4.cloned.1.call-update) | async-done | bytes 196624
  231.2 2.3 copy.28
  233.5 2.2 copy.24
  (11 shorter events, 0.3 us)
Async XLA Ops:
  7.2 79.5 %copy-start = (bf16[1,768,2048]{2,1,0:T(8,128)(2,1)S(1)}, bf16[1,768,2048]{2,1,0:T(8,128)(2,1)}, u32[]{:S(2)}) copy-start(bf16[1,768,2048]{2,1,0:T(8,128)(2,1)} %param.9) | copy-start | bytes 9437188
  7.2 224.0 %reduce-scatter.4.cloned.1.call-start = ((), (), s32[]{:S(2)}) async-start(), calls=%async_computation.3 | async-start | bytes 6488064
  93.3 32.9 %all-to-all-start = ((bf16[32,10,2048]{2,1,0:T(8,128)(2,1)}), bf16[32,10,2048]{2,1,0:T(8,128)(2,1)}, u32[]{:S(2)}, u32[]{:S(2)}) async-start(bf16[32,10,2048]{2,1,0:T(8,128)(2,1)} %reshape.75), calls=%async_computation | async-start | bytes 4194304 | tf_op jit(solution)/shard_map/all_to_all | solution.py:35
Sparse Core Ops, SparseCore 0:
  86.8 144.3 reduce-scatter.3
where the time goes:
time: 244 us; the launch traced here: 243 us
  waiting for transfers between devices  108 us (44%)
  blocking collectives  44.4 us (18%)
  local copies, waits for them, and re-layouts  42 us (17%)
  matrix products  16.2 us (7%)
  between operations  14.1 us (6%)
  other arithmetic  11.7 us (5%)
  starting transfers between devices  5.87 us (2%)
    unnamed x2, waiting for transfers between devices  81.2 us
    all_to_all x1, blocking collectives, send_grads(): lax.all_to_all(buffer.reshape(peer_count, capacity, features), 'ep', spli...  44.4 us
    all_to_all x1, waiting for transfers between devices, forward(): lax.all_to_all(local_rows.reshape(peer_count, capacity, features), 'ep',...  27.1 us
    unnamed x7, local copies, waits for them, and re-layouts  12.7 us
    mul x2, local copies, waits for them, and re-layouts, send_grads(): route_probs[:, :, None] * cotangent[:, None, :].astype(jnp.float32)  7.11 us
    dot_general x1, matrix products, shards(): lax.dot_general(expert_hidden, arrived, (((0,), (0,)), ((), ())), preferr...  5.92 us
    all_to_all x1, starting transfers between devices, forward(): lax.all_to_all(local_rows.reshape(peer_count, capacity, features), 'ep',...  5.83 us
    reduce_sum x1, other arithmetic, forward(): jnp.sum(route_probs[..., None] * picked.astype(jnp.float32), axis=1)  5.12 us
  transfers between devices with their start and end apart: 2, of which 2 were waited for; matrix products, arithmetic and copies ran while one was open for 13% of the time, Pallas kernels for 0%

commit v1 on v0

v1 whole, which is shorter than its diff:
```python
import jax
import jax.numpy as jnp
from jax import lax
from jax.experimental import pallas as pl
from jax.experimental.pallas import tpu as pltpu
from jax.sharding import PartitionSpec as P

BF16 = jnp.bfloat16
F32 = jnp.float32
QUARTERS = 4
VMEM_BYTES = 48 * 1024 * 1024


def iota(shape, dim):
    return lax.broadcasted_iota(jnp.int32, shape, dim)


def dot(a, b, a_dim=1, b_dim=0):
    return lax.dot_general(a, b, (((a_dim,), (b_dim,)), ((), ())), preferred_element_type=F32)


def onehot(condition):
    return condition.astype(F32).astype(BF16)


def quarter_mask(rows, columns, quarter):
    return (iota((rows, columns), 0) & 3) == quarter


def route_slots(ids):
    tokens = ids.shape[1]
    experts = iota((32, tokens), 0)
    hits = [jnp.where(experts == ids[r : r + 1, :], 1.0, 0.0) for r in range(2)]
    before = onehot(iota((tokens, tokens), 0) < iota((tokens, tokens), 1))
    earlier = dot((hits[0] + hits[1]).astype(BF16), before)
    return [jnp.sum(earlier * hit, axis=0, keepdims=True).astype(jnp.int32) for hit in hits]


def route_masks(ids):
    tokens = ids.shape[1]
    row = iota((256, tokens), 0)
    low, high = [], []
    for r, slot in enumerate(route_slots(ids)):
        expert = ids[r : r + 1, :]
        low.append((row == expert * 8 + slot) & (slot < 8))
        high.append(((row >> 2) == expert * 2 + slot - 8) & (slot >= 8))
    return low, high


def send_kernel(ids_ref, probs_ref, cot_ref, out_ref):
    low, high = route_masks(ids_ref[...])
    probs = probs_ref[...]

    def weigh(masks):
        weights = [jnp.where(mask, probs[r : r + 1, :], 0.0) for r, mask in enumerate(masks)]
        return jnp.sum(weights[0] + weights[1], axis=1, keepdims=True)

    low_select = onehot(low[0] | low[1])
    high_select = onehot(high[0] | high[1])
    low_weight, high_weight = weigh(low), weigh(high)
    width = cot_ref.shape[1] // QUARTERS
    left = jnp.zeros((256, width), F32)
    for q in range(QUARTERS):
        part = cot_ref[:, q * width : (q + 1) * width]
        out_ref[:, q * width : (q + 1) * width] = (low_weight * dot(low_select, part)).astype(BF16)
        left = jnp.where(quarter_mask(256, width, q), dot(high_select, part), left)
    out_ref[:, QUARTERS * width :] = (high_weight * left).astype(BF16)


def expert_kernel(hidden_ref, weight_ref, out_ref, packed_ref, left_ref):
    step = pl.program_id(0)
    rows = hidden_ref.shape[0]
    width = weight_ref.shape[1]

    @pl.when(step == 0)
    def _():
        row, column = iota((256, rows), 0), iota((256, rows), 1)
        peer, place = row >> 3, row & 7
        hidden = hidden_ref[...]
        packed_ref[0:256, :] = dot(onehot(column == peer * 10 + place), hidden).astype(BF16)
        packed_ref[256:512, :] = dot(onehot(column == peer * 10 + 8 + (place >> 2)), hidden).astype(BF16)
        left_ref[...] = jnp.zeros_like(left_ref)

    both = dot(packed_ref[...], weight_ref[...])
    left_ref[...] = jnp.where(quarter_mask(256, width, step), both[256:512, :], left_ref[...])
    out_ref[:, pl.ds(pl.multiple_of(step * width, width), width)] = both[0:256, :].astype(BF16)

    @pl.when(step == QUARTERS - 1)
    def _():
        out_ref[:, QUARTERS * width :] = left_ref[...].astype(BF16)


def natural_rows(low, left, step, rows):
    row, column = iota((rows, 512), 0), iota((rows, 512), 1)
    peer, place = (column & 255) >> 3, column & 7
    in_low = (column < 256) & (row == peer * 10 + place)
    in_left = (column >= 256) & (row == peer * 10 + 8 + (place >> 2)) & ((place & 3) == step)
    return dot(onehot(in_low | in_left), jnp.concatenate([low, left], axis=0)).astype(BF16)


def partial_kernel(scale, hidden_ref, low_ref, left_ref, out_ref, turned_ref):
    step = pl.program_id(0)

    @pl.when(step == 0)
    def _():
        turned_ref[...] = hidden_ref[...].T

    rows = natural_rows(low_ref[...], left_ref[...], step, hidden_ref.shape[0])
    out_ref[...] = dot(turned_ref[...], rows) * scale


def hidden_grad_kernel(low_ref, left_ref, weight_ref, out_ref, total_ref):
    step = pl.program_id(0)
    rows = natural_rows(low_ref[...], left_ref[...], step, out_ref.shape[0])
    term = dot(rows, weight_ref[...], 1, 1)

    @pl.when(step == 0)
    def _():
        total_ref[...] = term

    @pl.when(step > 0)
    def _():
        total_ref[...] += term

    @pl.when(step == QUARTERS - 1)
    def _():
        out_ref[...] = total_ref[...].astype(BF16)


def combine_kernel(ids_ref, probs_ref, cot_ref, rows_ref, out_ref, grad_ref):
    tokens, features = cot_ref.shape
    width = features // QUARTERS
    low, high = route_masks(ids_ref[...])
    diagonal = iota((tokens, tokens), 0) == iota((tokens, tokens), 1)
    probs = [
        jnp.sum(jnp.where(diagonal, probs_ref[r : r + 1, :], 0.0), axis=1, keepdims=True)
        for r in range(2)
    ]
    left = rows_ref[:, QUARTERS * width :]
    sums = [jnp.zeros((tokens, 1), F32) for _ in range(2)]
    for q in range(QUARTERS):
        part = slice(q * width, (q + 1) * width)
        held = jnp.concatenate([rows_ref[:, part], left], axis=0)
        mine = quarter_mask(256, tokens, q)
        cot = cot_ref[:, part].astype(F32)
        total = jnp.zeros((tokens, width), F32)
        for r in range(2):
            select = jnp.concatenate([onehot(low[r]), onehot(high[r] & mine)], axis=0)
            picked = dot(select, held, 0, 0)
            total += probs[r] * picked
            sums[r] += jnp.sum(cot * picked, axis=1, keepdims=True)
        out_ref[:, part] = total.astype(BF16)
    for r in range(2):
        grad_ref[r : r + 1, :] = (
            jnp.sum(jnp.where(diagonal, sums[r], 0.0), axis=0, keepdims=True) * features ** (-0.5)
        )


def call(kernel, out_shape, flops, bytes_accessed, **options):
    return pl.pallas_call(
        kernel,
        out_shape=out_shape,
        compiler_params=pltpu.CompilerParams(vmem_limit_bytes=VMEM_BYTES),
        cost_estimate=pl.CostEstimate(
            flops=flops, bytes_accessed=bytes_accessed, transcendentals=0
        ),
        **options,
    )


def exchange(packed, peers):
    blocks = packed.reshape(peers, packed.shape[0] // peers, packed.shape[1])
    return lax.all_to_all(blocks, "ep", split_axis=0, concat_axis=0, tiled=True).reshape(packed.shape)


def shards(cotangent, route_ids, route_probs, expert_hidden, down_weight):
    peers, groups = lax.axis_size("ep"), lax.axis_size("dp")
    tokens, features = cotangent.shape
    rows, inner = expert_hidden.shape
    weight = down_weight[0]
    ids, probs = route_ids.T, route_probs.T
    width = features // QUARTERS
    packed = jax.ShapeDtypeStruct((256, features + width), BF16)
    product = 2 * rows * inner * features
    whole = lambda shape: pl.BlockSpec(shape, lambda q: (0,) * len(shape))
    column = lambda height: pl.BlockSpec((height, width), lambda q: (0, q))
    last = pl.BlockSpec((256, width), lambda q: (0, QUARTERS))

    outgoing = call(send_kernel, packed, 4 * 256 * tokens * features, 2 * 10**6)(ids, probs, cotangent)
    arrived = exchange(outgoing, peers)
    expert_rows = call(
        expert_kernel,
        packed,
        2 * product,
        6 * 10**6,
        grid=(QUARTERS,),
        in_specs=[whole((rows, inner)), column(inner)],
        out_specs=whole(packed.shape),
        scratch_shapes=[pltpu.VMEM((512, inner), BF16), pltpu.VMEM((256, width), F32)],
    )(expert_hidden, weight)
    partial = call(
        lambda *refs: partial_kernel((groups * rows) ** (-0.5), *refs),
        jax.ShapeDtypeStruct((inner, features), F32),
        2 * product,
        8 * 10**6,
        grid=(QUARTERS,),
        in_specs=[whole((rows, inner)), column(256), last],
        out_specs=column(inner),
        scratch_shapes=[pltpu.VMEM((inner, rows), BF16)],
    )(expert_hidden, arrived, arrived)
    weight_grad = lax.psum_scatter(partial, "dp", scatter_dimension=0, tiled=True)
    returned = exchange(expert_rows, peers)
    hidden_grad = call(
        hidden_grad_kernel,
        jax.ShapeDtypeStruct((rows, inner), BF16),
        2 * product,
        6 * 10**6,
        grid=(QUARTERS,),
        in_specs=[column(256), last, column(inner)],
        out_specs=whole((rows, inner)),
        scratch_shapes=[pltpu.VMEM((rows, inner), F32)],
    )(arrived, arrived, weight)
    layer_out, router_grad = call(
        combine_kernel,
        (
            jax.ShapeDtypeStruct((tokens, features), BF16),
            jax.ShapeDtypeStruct((2, tokens), F32),
        ),
        8 * 256 * tokens * features,
        3 * 10**6,
    )(ids, probs, cotangent, returned)
    return (layer_out, router_grad.T, hidden_grad, weight_grad[None])


def solution(mesh):
    in_specs = (
        P(("ep", "dp"), None),
        P(("ep", "dp"), None),
        P(("ep", "dp"), None),
        P(("ep", "dp"), None),
        P("ep", None, None),
    )
    out_specs = (
        P(("ep", "dp"), None),
        P(("ep", "dp"), None),
        P(("ep", "dp"), None),
        P("ep", "dp", None),
    )
    return jax.shard_map(shards, mesh=mesh, in_specs=in_specs, out_specs=out_specs, check_vma=False)
```

time: 244 us -> 204 us (0.84)
  local copies, waits for them, and re-layouts: 42 us -> 4.31 us
  matrix products: 16.2 us -> 0 us
  Pallas kernels: 0 us -> 15.6 us
  blocking collectives: 44.4 us -> 58.5 us
  other arithmetic: 11.7 us -> 0 us
  starting transfers between devices: 5.87 us -> 0.04 us
    reduce_scatter x0 -> x1, waiting for transfers between devices: none -> 110 us  [shards(): lax.psum_scatter(partial, 'dp', scatter_dimension=0, tiled=True)]
    unnamed x2 -> x1, waiting for transfers between devices: 81.2 us -> 0.02 us
    all_to_all x1 -> x0, waiting for transfers between devices: 27.1 us -> none  [forward(): lax.all_to_all(local_rows.reshape(peer_count, capacity, features), 'ep',...]
    reshape x5 -> x0, local copies, waits for them, and re-layouts: 16.4 us -> none  [the longest x1 3.6 us: forward(): returned = returned.reshape(row_count, features)]
    dot_general x4 -> x0, matrix products: 16.2 us -> none  [the longest x1 5.92 us: shards(): lax.dot_general(expert_hidden, arrived, (((0,), (0,)), ((), ())), preferr...]
    pallas_call x0 -> x5, Pallas kernels: none -> 15.6 us  [the longest x1 5.26 us: shards(): call(lambda *refs: partial_kernel((groups * rows) ** (-0.5), *refs), jax....]
    all_to_all x1 -> x2, blocking collectives: 44.4 us -> 58.5 us  [exchange(): lax.all_to_all(blocks, 'ep', split_axis=0, concat_axis=0, tiled=True)]
    unnamed x7 -> x18, local copies, waits for them, and re-layouts: 12.7 us -> 4.31 us
  transfers between devices with their start and end apart: 2 -> 1, of which waited for: 2 -> 1; matrix products, arithmetic and copies ran while one was open for 13% -> 0% of each run, Pallas kernels for 0% -> 5%
where the time goes in v1:
time: 204 us; the launch traced here: 203 us
  waiting for transfers between devices  110 us (54%)
  blocking collectives  58.5 us (29%)
  Pallas kernels  15.6 us (8%)
  between operations  14.1 us (7%)
  local copies, waits for them, and re-layouts  4.31 us (2%)
    reduce_scatter x1, waiting for transfers between devices, shards(): lax.psum_scatter(partial, 'dp', scatter_dimension=0, tiled=True)  110 us
    all_to_all x2, blocking collectives, exchange(): lax.all_to_all(blocks, 'ep', split_axis=0, concat_axis=0, tiled=True)  58.5 us
    pallas_call x1, Pallas kernels, shards(): call(lambda *refs: partial_kernel((groups * rows) ** (-0.5), *refs), jax....  5.26 us
    pallas_call x1, Pallas kernels, shards(): call(hidden_grad_kernel, jax.ShapeDtypeStruct((rows, inner), BF16), 2 * p...  4.43 us
    unnamed x18, local copies, waits for them, and re-layouts  4.31 us
  transfers between devices with their start and end apart: 1, of which 1 were waited for; matrix products, arithmetic and copies ran while one was open for 0% of the time, Pallas kernels for 5%

profile of v1, /device:TPU:8, one launch (start us, length us, event | category | flops | bytes accessed | tf_op | source)
XLA Modules:
  0.0 203.0 jit_solution(799244746169800101)
XLA Ops:
  7.2 0.0 reduce-scatter.2.cloned.1.call-start
  7.2 0.0 copy-start
  7.2 1.0 copy-done
  8.3 0.0 copy-start.3
  8.3 0.7 copy-done.3
  8.9 0.0 copy-start.5
  8.9 0.7 copy-done.5
  9.6 0.9 shard_map.86
  10.5 0.0 copy-start.2
  10.5 34.6 %all_to_all.10 = bf16[32,8,2560]{2,1,0:T(8,128)(2,1)S(1)} all-to-all(bf16[32,8,2560]{2,1,0:T(8,128)(2,1)S(1)} %bitcast.13), channel_id=1, replica_groups=mesh['ep'=32,'dp'=32] {'ep'}, dimensions={0} | all-to-all | bytes 2621440 | tf_op jit(solution)/shard_map/all_to_all | solution.py:173
  45.1 0.0 copy-done.2
  45.1 5.3 %shard_map.88 = f32[768,2048]{1,0:T(8,128)} custom-call(bf16[320,768]{1,0:T(8,128)(2,1)S(1)} %copy-done.2, bf16[256,2560]{1,0:T(8,128)(2,1)S(1)} %bitcast.9, bf16[256,2560]{1,0:T(8,128)(2,1)S(1)} %bitcast.10), custom_call_target="tpu_custom_call" | custom-call | flops 2013265920 | bytes 8000000 | tf_op jit(solution)/shard_map/pallas_call | solution.py:201
  50.3 0.0 reduce-scatter.2.cloned.1.call-update
  50.4 0.0 copy-start.7
  50.4 1.9 copy-done.7
  52.3 3.2 %shard_map.84 = bf16[256,2560]{1,0:T(8,128)(2,1)S(1)} custom-call(bf16[320,768]{1,0:T(8,128)(2,1)S(1)} %copy-done.2, bf16[768,2048]{1,0:T(8,128)(2,1)S(1)} %bitcast.20), custom_call_target="tpu_custom_call" | custom-call | flops 2013265920 | bytes 6000000 | tf_op jit(solution)/shard_map/pallas_call | solution.py:191
  55.5 0.0 copy-start.1
  55.5 0.0 copy-start.4
  55.5 0.0 copy-start.6
  55.5 0.0 copy-start.8
  55.5 24.0 %all_to_all.11 = bf16[32,8,2560]{2,1,0:T(8,128)(2,1)S(1)} all-to-all(bf16[32,8,2560]{2,1,0:T(8,128)(2,1)S(1)} %bitcast.15), channel_id=1, replica_groups=mesh['ep'=32,'dp'=32] {'ep'}, dimensions={0} | all-to-all | bytes 2621440 | tf_op jit(solution)/shard_map/all_to_all | solution.py:173
  79.5 0.0 copy-done.1
  79.5 0.0 copy-done.4
  79.5 0.0 copy-done.6
  79.5 1.8 shard_map.85
  81.3 0.0 copy-done.8
  81.3 4.4 %shard_map.87 = bf16[320,768]{1,0:T(8,128)(2,1)} custom-call(bf16[256,2560]{1,0:T(8,128)(2,1)S(1)} %bitcast.11, bf16[256,2560]{1,0:T(8,128)(2,1)S(1)} %bitcast.12, bf16[768,2048]{1,0:T(8,128)(2,1)S(1)} %bitcast.21), custom_call_target="tpu_custom_call" | custom-call | flops 2013265920 | bytes 6000000 | tf_op jit(solution)/shard_map/pallas_call | solution.py:213
  85.7 110.4 %reduce-scatter.2.cloned.1.call-done = f32[24,2048]{1,0:T(8,128)} async-done(((f32[768,2048]{1,0:T(8,128)}), f32[24,2048]{1,0:T(8,128)}) %reduce-scatter.2.cloned.1.call-update) | async-done | bytes 196624 | tf_op jit(solution)/shard_map/reduce_scatter | solution.py:211
Async XLA Ops:
  7.2 189.0 %reduce-scatter.2.cloned.1.call-start = ((), (), s32[]{:S(2)}) async-start(), calls=%async_computation.3 | async-start | bytes 6488064 | tf_op jit(solution)/shard_map/reduce_scatter | solution.py:211
  7.2 1.0 copy-start
  8.3 0.7 copy-start.3
  8.9 0.7 copy-start.5
  10.5 34.6 %copy-start.2 = (bf16[320,768]{1,0:T(8,128)(2,1)S(1)}, bf16[320,768]{1,0:T(8,128)(2,1)}, u32[]{:S(2)}) copy-start(bf16[320,768]{1,0:T(8,128)(2,1)} %refs_0_.1) | copy-start | bytes 1474564
  50.4 1.9 copy-start.7
  55.5 24.0 %copy-start.1 = (bf16[128,2048]{1,0:T(8,128)(2,1)S(1)}, bf16[128,2048]{1,0:T(8,128)(2,1)}, u32[]{:S(2)}) copy-start(bf16[128,2048]{1,0:T(8,128)(2,1)} %cot_ref.3) | copy-start | bytes 1572868
  55.5 24.0 %copy-start.4 = (s32[128,2]{0,1:T(2,128)S(1)}, s32[128,2]{0,1:T(2,128)}, u32[]{:S(2)}) copy-start(s32[128,2]{0,1:T(2,128)} %param.6) | copy-start | bytes 3076
  55.5 24.0 %copy-start.6 = (f32[128,2]{0,1:T(2,128)S(1)}, f32[128,2]{0,1:T(2,128)}, u32[]{:S(2)}) copy-start(f32[128,2]{0,1:T(2,128)} %param.7) | copy-start | bytes 3076
  55.5 25.8 %copy-start.8 = (bf16[1,768,2048]{2,1,0:T(8,128)(2,1)S(1)}, bf16[1,768,2048]{2,1,0:T(8,128)(2,1)}, u32[]{:S(2)}) copy-start(bf16[1,768,2048]{2,1,0:T(8,128)(2,1)} %param.9) | copy-start | bytes 9437188
Sparse Core Ops, SparseCore 0:
  50.5 145.6 reduce-scatter.1

commit v2 on v1

--- a/solution.py
+++ b/solution.py
@@ -8,6 +8,7 @@
 BF16 = jnp.bfloat16
 F32 = jnp.float32
 QUARTERS = 4
+CHUNK = 24
 VMEM_BYTES = 48 * 1024 * 1024
 
 
@@ -98,15 +99,46 @@
     return dot(onehot(in_low | in_left), jnp.concatenate([low, left], axis=0)).astype(BF16)
 
 
-def partial_kernel(scale, hidden_ref, low_ref, left_ref, out_ref, turned_ref):
+def chunk_order(group, rows):
+    block = (rows * 2731) >> 16
+    offset = jnp.where(block < 11, 14 - 3 * block, jnp.where(block < 21, 46 - 3 * block, 78 - 3 * block))
+    return ((group + offset) & 31) * CHUNK + rows - block * CHUNK
+
+
+def partial_kernel(scale, group_ref, hidden_ref, low_ref, left_ref, down_ref, up_ref, own_ref, turned_ref):
     step = pl.program_id(0)
+    inner = hidden_ref.shape[1]
 
     @pl.when(step == 0)
     def _():
-        turned_ref[...] = hidden_ref[...].T
+        source = chunk_order(group_ref[0], iota((1, inner), 1))
+        select = onehot(iota((inner, inner), 0) == source)
+        turned_ref[...] = dot(select, hidden_ref[...], 0, 1).astype(BF16)
 
     rows = natural_rows(low_ref[...], left_ref[...], step, hidden_ref.shape[0])
-    out_ref[...] = dot(turned_ref[...], rows) * scale
+    product = dot(turned_ref[...], rows) * scale
+    down_ref[...] = product[: 11 * CHUNK].astype(BF16)
+    up_ref[...] = product[11 * CHUNK : 21 * CHUNK].astype(BF16)
+    own_ref[...] = product[21 * CHUNK :]
+
+
+def shift(block, distance):
+    groups = lax.axis_size("dp")
+    return lax.ppermute(block, "dp", [(i, (i + distance) % groups) for i in range(groups)])
+
+
+def sum_over_groups(from_above, from_below, own):
+    def term(k):
+        place = slice(k * CHUNK, (k + 1) * CHUNK)
+        total = own[place] + from_above[place].astype(F32)
+        return total if k == 0 else total + from_below[(k - 1) * CHUNK : k * CHUNK].astype(F32)
+
+    rising, falling = term(0), term(10)
+    for k in range(1, 5):
+        rising = shift(rising.astype(BF16), 3).astype(F32) + term(k)
+        falling = shift(falling.astype(BF16), -3).astype(F32) + term(10 - k)
+    rising, falling = shift(rising.astype(BF16), 3), shift(falling.astype(BF16), -3)
+    return term(5) + rising.astype(F32) + falling.astype(F32)
 
 
 def hidden_grad_kernel(low_ref, left_ref, weight_ref, out_ref, total_ref):
@@ -198,18 +230,31 @@
         out_specs=whole(packed.shape),
         scratch_shapes=[pltpu.VMEM((512, inner), BF16), pltpu.VMEM((256, width), F32)],
     )(expert_hidden, weight)
-    partial = call(
+    group = lax.axis_index("dp").astype(jnp.int32).reshape(1)
+    down, up, own = call(
         lambda *refs: partial_kernel((groups * rows) ** (-0.5), *refs),
-        jax.ShapeDtypeStruct((inner, features), F32),
+        (
+            jax.ShapeDtypeStruct((11 * CHUNK, features), BF16),
+            jax.ShapeDtypeStruct((10 * CHUNK, features), BF16),
+            jax.ShapeDtypeStruct((11 * CHUNK, features), F32),
+        ),
         2 * product,
         8 * 10**6,
         grid=(QUARTERS,),
-        in_specs=[whole((rows, inner)), column(256), last],
-        out_specs=column(inner),
+        in_specs=[
+            pl.BlockSpec(memory_space=pltpu.SMEM),
+            whole((rows, inner)),
+            column(256),
+            last,
+        ],
+        out_specs=(column(11 * CHUNK), column(10 * CHUNK), column(11 * CHUNK)),
         scratch_shapes=[pltpu.VMEM((inner, rows), BF16)],
-    )(expert_hidden, arrived, arrived)
-    weight_grad = lax.psum_scatter(partial, "dp", scatter_dimension=0, tiled=True)
+    )(group, expert_hidden, arrived, arrived)
+    expert_rows, down, up = lax.optimization_barrier((expert_rows, down, up))
+    from_above, from_below = shift(down, -1), shift(up, 1)
     returned = exchange(expert_rows, peers)
+    returned, from_above, from_below = lax.optimization_barrier((returned, from_above, from_below))
+    weight_grad = sum_over_groups(from_above, from_below, own)
     hidden_grad = call(
         hidden_grad_kernel,
         jax.ShapeDtypeStruct((rows, inner), BF16),

time: 204 us -> 175 us (0.86)
  the two profiles are of different devices: /device:TPU:8 before, /device:TPU:38 now
where the time goes in v2:
time: 175 us; the launch traced here: 174 us
  starting transfers between devices  72.3 us (41%)
  waiting for transfers between devices  67.9 us (39%)
  Pallas kernels  17.4 us (10%)
  local copies, waits for them, and re-layouts  8.36 us (5%)
  other arithmetic  7.38 us (4%)
    ppermute x12, starting transfers between devices, shift(): lax.ppermute(block, 'dp', [(i, (i + distance) % groups) for i in range(gr...  58.1 us
    ppermute x12, waiting for transfers between devices, shift(): lax.ppermute(block, 'dp', [(i, (i + distance) % groups) for i in range(gr...  56 us
    all_to_all x2, starting transfers between devices, exchange(): lax.all_to_all(blocks, 'ep', split_axis=0, concat_axis=0, tiled=True)  14.2 us
    all_to_all x2, waiting for transfers between devices, exchange(): lax.all_to_all(blocks, 'ep', split_axis=0, concat_axis=0, tiled=True)  11.9 us
    unnamed x26, local copies, waits for them, and re-layouts  8.36 us
    pallas_call x1, Pallas kernels, shards(): call(lambda *refs: partial_kernel((groups * rows) ** (-0.5), *refs), (jax...  4.73 us
    convert_element_type x4, other arithmetic, sum_over_groups(): rising = shift(rising.astype(BF16), 3).astype(F32) + term(k)  4.58 us
    pallas_call x1, Pallas kernels, shards(): call(hidden_grad_kernel, jax.ShapeDtypeStruct((rows, inner), BF16), 2 * p...  4.44 us
  transfers between devices with their start and end apart: 14, of which 10 were waited for; matrix products, arithmetic and copies ran while one was open for 0% of the time, Pallas kernels for 6%

profile of v2, /device:TPU:38, one launch (start us, length us, event | category | flops | bytes accessed | tf_op | source)
XLA Modules:
  0.0 174.2 jit_solution(10655294819804828267)
XLA Ops:
  3.0 1.9 %shard_map.85 = bf16[256,2560]{1,0:T(8,128)(2,1)} custom-call(s32[2,128]{1,0:T(2,128)S(1)} %bitcast.16, f32[2,128]{1,0:T(2,128)S(1)} %bitcast.18, bf16[128,2048]{1,0:T(8,128)(2,1)S(1)} %copy-done.1), custom_call_target="tpu_custom_call" | custom-call | flops 268435456 | bytes 2000000 | tf_op jit(solution)/shard_map/pallas_call | solution.py:221
  5.0 7.7 %all-to-all-start = ((bf16[32,8,2560]{2,1,0:T(8,128)(2,1)}), bf16[32,8,2560]{2,1,0:T(8,128)(2,1)S(1)}, u32[]{:S(2)}, u32[]{:S(2)}) async-start(bf16[32,8,2560]{2,1,0:T(8,128)(2,1)} %bitcast.4), calls=%async_computation | async-start | bytes 2621440 | tf_op jit(solution)/shard_map/all_to_all | solution.py:205
  12.7 1.9 %copy-done.7 = bf16[1,768,2048]{2,1,0:T(8,128)(2,1)S(1)} copy-done((bf16[1,768,2048]{2,1,0:T(8,128)(2,1)S(1)}, bf16[1,768,2048]{2,1,0:T(8,128)(2,1)}, u32[]{:S(2)}) %copy-start.7) | copy-done | bytes 3145752
  14.6 3.2 %shard_map.84 = bf16[256,2560]{1,0:T(8,128)(2,1)S(1)} custom-call(bf16[320,768]{1,0:T(8,128)(2,1)S(1)} %copy-done.11, bf16[768,2048]{1,0:T(8,128)(2,1)S(1)} %bitcast.20), custom_call_target="tpu_custom_call" | custom-call | flops 2013265920 | bytes 6000000 | tf_op jit(solution)/shard_map/pallas_call | solution.py:223
  18.9 11.9 %all-to-all-done = bf16[32,8,2560]{2,1,0:T(8,128)(2,1)S(1)} async-done(((bf16[32,8,2560]{2,1,0:T(8,128)(2,1)}), bf16[32,8,2560]{2,1,0:T(8,128)(2,1)S(1)}, u32[]{:S(2)}, u32[]{:S(2)}) %all-to-all-start) | async-done | bytes 1310752 | tf_op jit(solution)/shard_map/all_to_all | solution.py:205
  31.8 4.7 %shard_map.86 = (bf16[264,2048]{1,0:T(8,128)(2,1)S(1)}, bf16[240,2048]{1,0:T(8,128)(2,1)S(1)}, f32[264,2048]{1,0:T(8,128)S(1)}) custom-call(s32[1]{0:T(128)} %bitcast.3.refs_0_, bf16[320,768]{1,0:T(8,128)(2,1)S(1)} %copy-done.12, bf16[256,2560]{1,0:T(8,128)(2,1)S(1)} %bitcast.11, bf16[256,2560]{1,0:T(8,128)(2,1)S(1)} %bitcast.12), custom_call_target="tpu_custom_call" | custom-call | flops 2013265920 | bytes 8000000 | tf_op jit(solution)/shard_map/pallas_call | solution.py:234
  38.5 6.5 %all-to-all-start.1 = ((bf16[32,8,2560]{2,1,0:T(8,128)(2,1)}), bf16[32,8,2560]{2,1,0:T(8,128)(2,1)}, u32[]{:S(2)}, u32[]{:S(2)}) async-start(bf16[32,8,2560]{2,1,0:T(8,128)(2,1)} %bitcast.15), calls=%async_computation.1 | async-start | bytes 2621440 | tf_op jit(solution)/shard_map/all_to_all | solution.py:205
  45.0 11.3 %collective-permute-start = (bf16[264,2048]{1,0:T(8,128)(2,1)}, bf16[264,2048]{1,0:T(8,128)(2,1)}, u32[]{:S(2)}, u32[]{:S(2)}) collective-permute-start(bf16[264,2048]{1,0:T(8,128)(2,1)} %copy-done.9), channel_id=1, source_target_pairs={{0,31},{1,0},{2,1},{3,2},{4,3},{5,4},{6,5},{7,6},{8,7},{9,8},{10,9... | collective-permute-start | bytes 3244040 | tf_op jit(solution)/shard_map/ppermute | solution.py:127
  56.3 1.9 %collective-permute-start.1 = (bf16[240,2048]{1,0:T(8,128)(2,1)}, bf16[240,2048]{1,0:T(8,128)(2,1)}, u32[]{:S(2)}, u32[]{:S(2)}) collective-permute-start(bf16[240,2048]{1,0:T(8,128)(2,1)} %copy-done.10), channel_id=1, source_target_pairs={{0,1},{1,2},{2,3},{3,4},{4,5},{5,6},{6,7},{7,8},{8,9},{9,10},{10,1... | collective-permute-start | bytes 2949128 | tf_op jit(solution)/shard_map/ppermute | solution.py:127
  58.2 29.6 %collective-permute-done.1 = bf16[240,2048]{1,0:T(8,128)(2,1)} collective-permute-done((bf16[240,2048]{1,0:T(8,128)(2,1)}, bf16[240,2048]{1,0:T(8,128)(2,1)}, u32[]{:S(2)}, u32[]{:S(2)}) %collective-permute-start.1) | collective-permute-done | bytes 983072 | tf_op jit(solution)/shard_map/ppermute | solution.py:127
  88.9 1.9 %collective-permute-start.2 = (bf16[24,2048]{1,0:T(8,128)(2,1)S(1)}, bf16[24,2048]{1,0:T(8,128)(2,1)S(1)}, u32[]{:S(2)}, u32[]{:S(2)}) collective-permute-start(bf16[24,2048]{1,0:T(8,128)(2,1)S(1)} %get-tuple-element.34), channel_id=1, source_target_pairs={{0,3},{1,4},{2,5},{3,6},{4,7},{5,8},{6,9},{7,10},{8,11},{9,12},{10... | collective-permute-start | bytes 294920 | tf_op jit(solution)/shard_map/ppermute | solution.py:127
  90.8 6.9 %collective-permute-start.7 = (bf16[24,2048]{1,0:T(8,128)(2,1)S(1)}, bf16[24,2048]{1,0:T(8,128)(2,1)S(1)}, u32[]{:S(2)}, u32[]{:S(2)}) collective-permute-start(bf16[24,2048]{1,0:T(8,128)(2,1)S(1)} %get-tuple-element.35), channel_id=1, source_target_pairs={{0,29},{1,30},{2,31},{3,0},{4,1},{5,2},{6,3},{7,4},{8,5},{9,6},{10... | collective-permute-start | bytes 294920 | tf_op jit(solution)/shard_map/ppermute | solution.py:127
  97.7 1.9 %collective-permute-done.2 = bf16[24,2048]{1,0:T(8,128)(2,1)S(1)} collective-permute-done((bf16[24,2048]{1,0:T(8,128)(2,1)S(1)}, bf16[24,2048]{1,0:T(8,128)(2,1)S(1)}, u32[]{:S(2)}, u32[]{:S(2)}) %collective-permute-start.2) | collective-permute-done | bytes 98336 | tf_op jit(solution)/shard_map/ppermute | solution.py:127
  99.6 3.1 %collective-permute-done.7 = bf16[24,2048]{1,0:T(8,128)(2,1)S(1)} collective-permute-done((bf16[24,2048]{1,0:T(8,128)(2,1)S(1)}, bf16[24,2048]{1,0:T(8,128)(2,1)S(1)}, u32[]{:S(2)}, u32[]{:S(2)}) %collective-permute-start.7) | collective-permute-done | bytes 98336 | tf_op jit(solution)/shard_map/ppermute | solution.py:127
  102.8 1.1 add_convert_fusion.8
  103.9 1.9 %collective-permute-start.3 = (bf16[24,2048]{1,0:T(8,128)(2,1)S(1)}, bf16[24,2048]{1,0:T(8,128)(2,1)S(1)}, u32[]{:S(2)}, u32[]{:S(2)}) collective-permute-start(bf16[24,2048]{1,0:T(8,128)(2,1)S(1)} %get-tuple-element.32), channel_id=1, source_target_pairs={{0,3},{1,4},{2,5},{3,6},{4,7},{5,8},{6,9},{7,10},{8,11},{9,12},{10... | collective-permute-start | bytes 294920 | tf_op jit(solution)/shard_map/ppermute | solution.py:127
  105.8 7.4 %collective-permute-start.8 = (bf16[24,2048]{1,0:T(8,128)(2,1)S(1)}, bf16[24,2048]{1,0:T(8,128)(2,1)S(1)}, u32[]{:S(2)}, u32[]{:S(2)}) collective-permute-start(bf16[24,2048]{1,0:T(8,128)(2,1)S(1)} %get-tuple-element.33), channel_id=1, source_target_pairs={{0,29},{1,30},{2,31},{3,0},{4,1},{5,2},{6,3},{7,4},{8,5},{9,6},{10... | collective-permute-start | bytes 294920 | tf_op jit(solution)/shard_map/ppermute | solution.py:127
  113.3 3.8 %collective-permute-done.3 = bf16[24,2048]{1,0:T(8,128)(2,1)S(1)} collective-permute-done((bf16[24,2048]{1,0:T(8,128)(2,1)S(1)}, bf16[24,2048]{1,0:T(8,128)(2,1)S(1)}, u32[]{:S(2)}, u32[]{:S(2)}) %collective-permute-start.3) | collective-permute-done | bytes 98336 | tf_op jit(solution)/shard_map/ppermute | solution.py:127
  117.7 1.3 add_convert_fusion.7
  119.0 6.0 %collective-permute-start.4 = (bf16[24,2048]{1,0:T(8,128)(2,1)S(1)}, bf16[24,2048]{1,0:T(8,128)(2,1)S(1)}, u32[]{:S(2)}, u32[]{:S(2)}) collective-permute-start(bf16[24,2048]{1,0:T(8,128)(2,1)S(1)} %get-tuple-element.30), channel_id=1, source_target_pairs={{0,3},{1,4},{2,5},{3,6},{4,7},{5,8},{6,9},{7,10},{8,11},{9,12},{10... | collective-permute-start | bytes 294920 | tf_op jit(solution)/shard_map/ppermute | solution.py:127
  125.0 2.8 %collective-permute-start.9 = (bf16[24,2048]{1,0:T(8,128)(2,1)S(1)}, bf16[24,2048]{1,0:T(8,128)(2,1)S(1)}, u32[]{:S(2)}, u32[]{:S(2)}) collective-permute-start(bf16[24,2048]{1,0:T(8,128)(2,1)S(1)} %get-tuple-element.31), channel_id=1, source_target_pairs={{0,29},{1,30},{2,31},{3,0},{4,1},{5,2},{6,3},{7,4},{8,5},{9,6},{10... | collective-permute-start | bytes 294920 | tf_op jit(solution)/shard_map/ppermute | solution.py:127
  128.5 8.8 %collective-permute-done.9 = bf16[24,2048]{1,0:T(8,128)(2,1)S(1)} collective-permute-done((bf16[24,2048]{1,0:T(8,128)(2,1)S(1)}, bf16[24,2048]{1,0:T(8,128)(2,1)S(1)}, u32[]{:S(2)}, u32[]{:S(2)}) %collective-permute-start.9) | collective-permute-done | bytes 98336 | tf_op jit(solution)/shard_map/ppermute | solution.py:127
  137.3 1.1 add_convert_fusion.6
  138.5 5.3 %collective-permute-start.5 = (bf16[24,2048]{1,0:T(8,128)(2,1)S(1)}, bf16[24,2048]{1,0:T(8,128)(2,1)S(1)}, u32[]{:S(2)}, u32[]{:S(2)}) collective-permute-start(bf16[24,2048]{1,0:T(8,128)(2,1)S(1)} %get-tuple-element.28), channel_id=1, source_target_pairs={{0,3},{1,4},{2,5},{3,6},{4,7},{5,8},{6,9},{7,10},{8,11},{9,12},{10... | collective-permute-start | bytes 294920 | tf_op jit(solution)/shard_map/ppermute | solution.py:127
  143.7 3.6 %collective-permute-start.10 = (bf16[24,2048]{1,0:T(8,128)(2,1)S(1)}, bf16[24,2048]{1,0:T(8,128)(2,1)S(1)}, u32[]{:S(2)}, u32[]{:S(2)}) collective-permute-start(bf16[24,2048]{1,0:T(8,128)(2,1)S(1)} %get-tuple-element.29), channel_id=1, source_target_pairs={{0,29},{1,30},{2,31},{3,0},{4,1},{5,2},{6,3},{7,4},{8,5},{9,6},{10... | collective-permute-start | bytes 294920 | tf_op jit(solution)/shard_map/ppermute | solution.py:127
  148.1 6.7 %collective-permute-done.10 = bf16[24,2048]{1,0:T(8,128)(2,1)S(1)} collective-permute-done((bf16[24,2048]{1,0:T(8,128)(2,1)S(1)}, bf16[24,2048]{1,0:T(8,128)(2,1)S(1)}, u32[]{:S(2)}, u32[]{:S(2)}) %collective-permute-start.10) | collective-permute-done | bytes 98336 | tf_op jit(solution)/shard_map/ppermute | solution.py:127
  154.8 1.1 add_convert_fusion.5
  155.9 1.9 %collective-permute-start.6 = (bf16[24,2048]{1,0:T(8,128)(2,1)S(1)}, bf16[24,2048]{1,0:T(8,128)(2,1)S(1)}, u32[]{:S(2)}, u32[]{:S(2)}) collective-permute-start(bf16[24,2048]{1,0:T(8,128)(2,1)S(1)} %get-tuple-element.26), channel_id=1, source_target_pairs={{0,3},{1,4},{2,5},{3,6},{4,7},{5,8},{6,9},{7,10},{8,11},{9,12},{10... | collective-permute-start | bytes 294920 | tf_op jit(solution)/shard_map/ppermute | solution.py:127
  157.9 7.1 %collective-permute-start.11 = (bf16[24,2048]{1,0:T(8,128)(2,1)S(1)}, bf16[24,2048]{1,0:T(8,128)(2,1)S(1)}, u32[]{:S(2)}, u32[]{:S(2)}) collective-permute-start(bf16[24,2048]{1,0:T(8,128)(2,1)S(1)} %get-tuple-element.27), channel_id=1, source_target_pairs={{0,29},{1,30},{2,31},{3,0},{4,1},{5,2},{6,3},{7,4},{8,5},{9,6},{10... | collective-permute-start | bytes 294920 | tf_op jit(solution)/shard_map/ppermute | solution.py:127
  165.0 4.4 %shard_map.88 = bf16[320,768]{1,0:T(8,128)(2,1)} custom-call(bf16[256,2560]{1,0:T(8,128)(2,1)S(1)} %bitcast.13, bf16[256,2560]{1,0:T(8,128)(2,1)S(1)} %bitcast.14, bf16[768,2048]{1,0:T(8,128)(2,1)S(1)} %bitcast.21), custom_call_target="tpu_custom_call" | custom-call | flops 2013265920 | bytes 6000000 | tf_op jit(solution)/shard_map/pallas_call | solution.py:258
  169.4 3.1 %shard_map.87 = (bf16[128,2048]{1,0:T(8,128)(2,1)}, f32[2,128]{1,0:T(2,128)}) custom-call(s32[2,128]{1,0:T(2,128)S(1)} %bitcast.17, f32[2,128]{1,0:T(2,128)S(1)} %bitcast.19, bf16[128,2048]{1,0:T(8,128)(2,1)S(1)} %copy-done.2, bf16[256,2560]{1,0:T(8,128)(2,1)} %bitcast.7.rows_ref), custom_call_target="tpu_custom_call" | custom-call | flops 536870912 | bytes 3000000 | tf_op jit(solution)/shard_map/pallas_call | solution.py:268
  172.5 1.7 add_bitcast_fusion
  (33 shorter events, 9.6 us)
Async XLA Ops:
  0.6 1.0 copy-start.1
  1.7 0.7 copy-start.3
  2.4 0.7 copy-start.5
  5.0 7.8 %copy-start.11 = (bf16[320,768]{1,0:T(8,128)(2,1)S(1)}, bf16[320,768]{1,0:T(8,128)(2,1)}, u32[]{:S(2)}) copy-start(bf16[320,768]{1,0:T(8,128)(2,1)} %refs_1_.1) | copy-start | bytes 1474564
  5.0 25.8 %all-to-all-start = ((bf16[32,8,2560]{2,1,0:T(8,128)(2,1)}), bf16[32,8,2560]{2,1,0:T(8,128)(2,1)S(1)}, u32[]{:S(2)}, u32[]{:S(2)}) async-start(bf16[32,8,2560]{2,1,0:T(8,128)(2,1)} %bitcast.4), calls=%async_computation | async-start | bytes 2621440 | tf_op jit(solution)/shard_map/all_to_all | solution.py:205
  12.7 1.9 %copy-start.7 = (bf16[1,768,2048]{2,1,0:T(8,128)(2,1)S(1)}, bf16[1,768,2048]{2,1,0:T(8,128)(2,1)}, u32[]{:S(2)}) copy-start(bf16[1,768,2048]{2,1,0:T(8,128)(2,1)} %param.9) | copy-start | bytes 9437188
  17.8 1.1 copy-start
  30.8 1.0 copy-start.12
  36.6 1.0 copy-start.9
  37.5 1.0 copy-start.10
  38.5 49.3 %all-to-all-start.1 = ((bf16[32,8,2560]{2,1,0:T(8,128)(2,1)}), bf16[32,8,2560]{2,1,0:T(8,128)(2,1)}, u32[]{:S(2)}, u32[]{:S(2)}) async-start(bf16[32,8,2560]{2,1,0:T(8,128)(2,1)} %bitcast.15), calls=%async_computation.1 | async-start | bytes 2621440 | tf_op jit(solution)/shard_map/all_to_all | solution.py:205
  45.0 42.8 %collective-permute-start = (bf16[264,2048]{1,0:T(8,128)(2,1)}, bf16[264,2048]{1,0:T(8,128)(2,1)}, u32[]{:S(2)}, u32[]{:S(2)}) collective-permute-start(bf16[264,2048]{1,0:T(8,128)(2,1)} %copy-done.9), channel_id=1, source_target_pairs={{0,31},{1,0},{2,1},{3,2},{4,3},{5,4},{6,5},{7,6},{8,7},{9,8},{10,9... | collective-permute-start | bytes 3244040 | tf_op jit(solution)/shard_map/ppermute | solution.py:127
  56.3 31.5 %collective-permute-start.1 = (bf16[240,2048]{1,0:T(8,128)(2,1)}, bf16[240,2048]{1,0:T(8,128)(2,1)}, u32[]{:S(2)}, u32[]{:S(2)}) collective-permute-start(bf16[240,2048]{1,0:T(8,128)(2,1)} %copy-done.10), channel_id=1, source_target_pairs={{0,1},{1,2},{2,3},{3,4},{4,5},{5,6},{6,7},{7,8},{8,9},{9,10},{10,1... | collective-permute-start | bytes 2949128 | tf_op jit(solution)/shard_map/ppermute | solution.py:127
  88.9 10.8 %collective-permute-start.2 = (bf16[24,2048]{1,0:T(8,128)(2,1)S(1)}, bf16[24,2048]{1,0:T(8,128)(2,1)S(1)}, u32[]{:S(2)}, u32[]{:S(2)}) collective-permute-start(bf16[24,2048]{1,0:T(8,128)(2,1)S(1)} %get-tuple-element.34), channel_id=1, source_target_pairs={{0,3},{1,4},{2,5},{3,6},{4,7},{5,8},{6,9},{7,10},{8,11},{9,12},{10... | collective-permute-start | bytes 294920 | tf_op jit(solution)/shard_map/ppermute | solution.py:127
  90.8 12.0 %collective-permute-start.7 = (bf16[24,2048]{1,0:T(8,128)(2,1)S(1)}, bf16[24,2048]{1,0:T(8,128)(2,1)S(1)}, u32[]{:S(2)}, u32[]{:S(2)}) collective-permute-start(bf16[24,2048]{1,0:T(8,128)(2,1)S(1)} %get-tuple-element.35), channel_id=1, source_target_pairs={{0,29},{1,30},{2,31},{3,0},{4,1},{5,2},{6,3},{7,4},{8,5},{9,6},{10... | collective-permute-start | bytes 294920 | tf_op jit(solution)/shard_map/ppermute | solution.py:127
  103.9 13.2 %collective-permute-start.3 = (bf16[24,2048]{1,0:T(8,128)(2,1)S(1)}, bf16[24,2048]{1,0:T(8,128)(2,1)S(1)}, u32[]{:S(2)}, u32[]{:S(2)}) collective-permute-start(bf16[24,2048]{1,0:T(8,128)(2,1)S(1)} %get-tuple-element.32), channel_id=1, source_target_pairs={{0,3},{1,4},{2,5},{3,6},{4,7},{5,8},{6,9},{7,10},{8,11},{9,12},{10... | collective-permute-start | bytes 294920 | tf_op jit(solution)/shard_map/ppermute | solution.py:127
  105.8 11.8 %collective-permute-start.8 = (bf16[24,2048]{1,0:T(8,128)(2,1)S(1)}, bf16[24,2048]{1,0:T(8,128)(2,1)S(1)}, u32[]{:S(2)}, u32[]{:S(2)}) collective-permute-start(bf16[24,2048]{1,0:T(8,128)(2,1)S(1)} %get-tuple-element.33), channel_id=1, source_target_pairs={{0,29},{1,30},{2,31},{3,0},{4,1},{5,2},{6,3},{7,4},{8,5},{9,6},{10... | collective-permute-start | bytes 294920 | tf_op jit(solution)/shard_map/ppermute | solution.py:127
  117.7 47.3 %copy-start.8 = (bf16[1,768,2048]{2,1,0:T(8,128)(2,1)S(1)}, bf16[1,768,2048]{2,1,0:T(8,128)(2,1)}, u32[]{:S(2)}) copy-start(bf16[1,768,2048]{2,1,0:T(8,128)(2,1)} %param.9) | copy-start | bytes 9437188
  119.0 9.5 %collective-permute-start.4 = (bf16[24,2048]{1,0:T(8,128)(2,1)S(1)}, bf16[24,2048]{1,0:T(8,128)(2,1)S(1)}, u32[]{:S(2)}, u32[]{:S(2)}) collective-permute-start(bf16[24,2048]{1,0:T(8,128)(2,1)S(1)} %get-tuple-element.30), channel_id=1, source_target_pairs={{0,3},{1,4},{2,5},{3,6},{4,7},{5,8},{6,9},{7,10},{8,11},{9,12},{10... | collective-permute-start | bytes 294920 | tf_op jit(solution)/shard_map/ppermute | solution.py:127
  125.0 12.3 %collective-permute-start.9 = (bf16[24,2048]{1,0:T(8,128)(2,1)S(1)}, bf16[24,2048]{1,0:T(8,128)(2,1)S(1)}, u32[]{:S(2)}, u32[]{:S(2)}) collective-permute-start(bf16[24,2048]{1,0:T(8,128)(2,1)S(1)} %get-tuple-element.31), channel_id=1, source_target_pairs={{0,29},{1,30},{2,31},{3,0},{4,1},{5,2},{6,3},{7,4},{8,5},{9,6},{10... | collective-permute-start | bytes 294920 | tf_op jit(solution)/shard_map/ppermute | solution.py:127
  138.5 9.6 %collective-permute-start.5 = (bf16[24,2048]{1,0:T(8,128)(2,1)S(1)}, bf16[24,2048]{1,0:T(8,128)(2,1)S(1)}, u32[]{:S(2)}, u32[]{:S(2)}) collective-permute-start(bf16[24,2048]{1,0:T(8,128)(2,1)S(1)} %get-tuple-element.28), channel_id=1, source_target_pairs={{0,3},{1,4},{2,5},{3,6},{4,7},{5,8},{6,9},{7,10},{8,11},{9,12},{10... | collective-permute-start | bytes 294920 | tf_op jit(solution)/shard_map/ppermute | solution.py:127
  143.7 11.0 %collective-permute-start.10 = (bf16[24,2048]{1,0:T(8,128)(2,1)S(1)}, bf16[24,2048]{1,0:T(8,128)(2,1)S(1)}, u32[]{:S(2)}, u32[]{:S(2)}) collective-permute-start(bf16[24,2048]{1,0:T(8,128)(2,1)S(1)} %get-tuple-element.29), channel_id=1, source_target_pairs={{0,29},{1,30},{2,31},{3,0},{4,1},{5,2},{6,3},{7,4},{8,5},{9,6},{10... | collective-permute-start | bytes 294920 | tf_op jit(solution)/shard_map/ppermute | solution.py:127
  155.9 16.6 %collective-permute-start.6 = (bf16[24,2048]{1,0:T(8,128)(2,1)S(1)}, bf16[24,2048]{1,0:T(8,128)(2,1)S(1)}, u32[]{:S(2)}, u32[]{:S(2)}) collective-permute-start(bf16[24,2048]{1,0:T(8,128)(2,1)S(1)} %get-tuple-element.26), channel_id=1, source_target_pairs={{0,3},{1,4},{2,5},{3,6},{4,7},{5,8},{6,9},{7,10},{8,11},{9,12},{10... | collective-permute-start | bytes 294920 | tf_op jit(solution)/shard_map/ppermute | solution.py:127
  157.8 11.6 %copy-start.2 = (bf16[128,2048]{1,0:T(8,128)(2,1)S(1)}, bf16[128,2048]{1,0:T(8,128)(2,1)}, u32[]{:S(2)}) copy-start(bf16[128,2048]{1,0:T(8,128)(2,1)} %cot_ref.3) | copy-start | bytes 1572868
  157.8 11.6 %copy-start.4 = (s32[128,2]{0,1:T(2,128)S(1)}, s32[128,2]{0,1:T(2,128)}, u32[]{:S(2)}) copy-start(s32[128,2]{0,1:T(2,128)} %param.6) | copy-start | bytes 3076
  157.9 11.5 %copy-start.6 = (f32[128,2]{0,1:T(2,128)S(1)}, f32[128,2]{0,1:T(2,128)}, u32[]{:S(2)}) copy-start(f32[128,2]{0,1:T(2,128)} %param.7) | copy-start | bytes 3076
  157.9 14.7 %collective-permute-start.11 = (bf16[24,2048]{1,0:T(8,128)(2,1)S(1)}, bf16[24,2048]{1,0:T(8,128)(2,1)S(1)}, u32[]{:S(2)}, u32[]{:S(2)}) collective-permute-start(bf16[24,2048]{1,0:T(8,128)(2,1)S(1)} %get-tuple-element.27), channel_id=1, source_target_pairs={{0,29},{1,30},{2,31},{3,0},{4,1},{5,2},{6,3},{7,4},{8,5},{9,6},{10... | collective-permute-start | bytes 294920 | tf_op jit(solution)/shard_map/ppermute | solution.py:127

commit v3 on v1

--- a/solution.py
+++ b/solution.py
@@ -8,6 +8,8 @@
 BF16 = jnp.bfloat16
 F32 = jnp.float32
 QUARTERS = 4
+HALVES = 2
+CHUNK = 24
 VMEM_BYTES = 48 * 1024 * 1024
 
 
@@ -47,7 +49,7 @@
     return low, high
 
 
-def send_kernel(ids_ref, probs_ref, cot_ref, out_ref):
+def send_kernel(ids_ref, probs_ref, cot_ref, *out_refs):
     low, high = route_masks(ids_ref[...])
     probs = probs_ref[...]
 
@@ -58,13 +60,16 @@
     low_select = onehot(low[0] | low[1])
     high_select = onehot(high[0] | high[1])
     low_weight, high_weight = weigh(low), weigh(high)
-    width = cot_ref.shape[1] // QUARTERS
-    left = jnp.zeros((256, width), F32)
-    for q in range(QUARTERS):
-        part = cot_ref[:, q * width : (q + 1) * width]
-        out_ref[:, q * width : (q + 1) * width] = (low_weight * dot(low_select, part)).astype(BF16)
-        left = jnp.where(quarter_mask(256, width, q), dot(high_select, part), left)
-    out_ref[:, QUARTERS * width :] = (high_weight * left).astype(BF16)
+    width = cot_ref.shape[1] // (HALVES * QUARTERS)
+    for h, out_ref in enumerate(out_refs):
+        left = jnp.zeros((256, width), F32)
+        for q in range(QUARTERS):
+            start = (h * QUARTERS + q) * width
+            part = cot_ref[:, start : start + width]
+            rows = low_weight * dot(low_select, part)
+            out_ref[:, q * width : (q + 1) * width] = rows.astype(BF16)
+            left = jnp.where(quarter_mask(256, width, q), dot(high_select, part), left)
+        out_ref[:, QUARTERS * width :] = (high_weight * left).astype(BF16)
 
 
 def expert_kernel(hidden_ref, weight_ref, out_ref, packed_ref, left_ref):
@@ -98,21 +103,63 @@
     return dot(onehot(in_low | in_left), jnp.concatenate([low, left], axis=0)).astype(BF16)
 
 
-def partial_kernel(scale, hidden_ref, low_ref, left_ref, out_ref, turned_ref):
+def chunk_order(group, rows):
+    block = (rows * 2731) >> 16
+    offset = jnp.where(block < 11, 14 - 3 * block, jnp.where(block < 21, 46 - 3 * block, 78 - 3 * block))
+    return ((group + offset) & 31) * CHUNK + rows - block * CHUNK
+
+
+def turn_kernel(group_ref, hidden_ref, turned_ref):
+    inner = hidden_ref.shape[1]
+    source = chunk_order(group_ref[0], iota((1, inner), 1))
+    select = onehot(iota((inner, inner), 0) == source)
+    turned_ref[...] = dot(select, hidden_ref[...], 0, 1).astype(BF16)
+
+
+def partial_kernel(scale, turned_ref, low_ref, left_ref, down_ref, up_ref, own_ref):
+    rows = natural_rows(low_ref[...], left_ref[...], pl.program_id(0), turned_ref.shape[1])
+    product = dot(turned_ref[...], rows) * scale
+    down_ref[...] = product[: 11 * CHUNK].astype(BF16)
+    up_ref[...] = product[11 * CHUNK : 21 * CHUNK].astype(BF16)
+    own_ref[...] = product[21 * CHUNK :]
+
+
+def shift(block, distance):
+    groups = lax.axis_size("dp")
+    return lax.ppermute(block, "dp", [(i, (i + distance) % groups) for i in range(groups)])
+
+
+def sum_over_groups(halves, expert_rows, combine):
+    def term(k):
+        parts = []
+        for from_above, from_below, own in halves:
+            place = slice(k * CHUNK, (k + 1) * CHUNK)
+            total = own[place] + from_above[place].astype(F32)
+            if k > 0:
+                total += from_below[(k - 1) * CHUNK : k * CHUNK].astype(F32)
+            parts.append(total)
+        return jnp.concatenate(parts, axis=1)
+
+    rising, falling = term(0), term(10)
+    for k in range(1, 5):
+        rising, falling = shift(rising.astype(BF16), 3), shift(falling.astype(BF16), -3)
+        if k == 1:
+            rising, expert_rows = lax.optimization_barrier((rising, expert_rows))
+            combined = combine(expert_rows)
+        if k == 4:
+            rising, falling, combined = lax.optimization_barrier((rising, falling, combined))
+        rising, falling = rising.astype(F32) + term(k), falling.astype(F32) + term(10 - k)
+    rising, falling = shift(rising.astype(BF16), 3), shift(falling.astype(BF16), -3)
+    return term(5) + rising.astype(F32) + falling.astype(F32), combined
+
+
+def hidden_grad_kernel(*refs):
+    inputs, (out_ref, total_ref) = refs[:-2], refs[-2:]
     step = pl.program_id(0)
-
-    @pl.when(step == 0)
-    def _():
-        turned_ref[...] = hidden_ref[...].T
-
-    rows = natural_rows(low_ref[...], left_ref[...], step, hidden_ref.shape[0])
-    out_ref[...] = dot(turned_ref[...], rows) * scale
-
-
-def hidden_grad_kernel(low_ref, left_ref, weight_ref, out_ref, total_ref):
-    step = pl.program_id(0)
-    rows = natural_rows(low_ref[...], left_ref[...], step, out_ref.shape[0])
-    term = dot(rows, weight_ref[...], 1, 1)
+    term = 0.0
+    for low_ref, left_ref, weight_ref in zip(inputs[0::3], inputs[1::3], inputs[2::3]):
+        rows = natural_rows(low_ref[...], left_ref[...], step, out_ref.shape[0])
+        term += dot(rows, weight_ref[...], 1, 1)
 
     @pl.when(step == 0)
     def _():
@@ -184,10 +231,23 @@
     product = 2 * rows * inner * features
     whole = lambda shape: pl.BlockSpec(shape, lambda q: (0,) * len(shape))
     column = lambda height: pl.BlockSpec((height, width), lambda q: (0, q))
-    last = pl.BlockSpec((256, width), lambda q: (0, QUARTERS))
-
-    outgoing = call(send_kernel, packed, 4 * 256 * tokens * features, 2 * 10**6)(ids, probs, cotangent)
-    arrived = exchange(outgoing, peers)
+
+    half = features // HALVES
+    narrow = half // QUARTERS
+    half_packed = jax.ShapeDtypeStruct((256, half + narrow), BF16)
+    block = lambda height, at: pl.BlockSpec((height, narrow), lambda q: (0, at(q)))
+    half_low, half_left = block(256, lambda q: q), block(256, lambda q: QUARTERS)
+    outgoing = call(send_kernel, (half_packed,) * HALVES, 4 * 256 * tokens * features, 2 * 10**6)(
+        ids, probs, cotangent
+    )
+    group = lax.axis_index("dp").astype(jnp.int32).reshape(1)
+    turned = call(
+        turn_kernel,
+        jax.ShapeDtypeStruct((inner, rows), BF16),
+        2 * inner * inner * rows,
+        10**6,
+        in_specs=[pl.BlockSpec(memory_space=pltpu.SMEM), pl.BlockSpec(memory_space=pltpu.VMEM)],
+    )(group, expert_hidden)
     expert_rows = call(
         expert_kernel,
         packed,
@@ -198,37 +258,56 @@
         out_specs=whole(packed.shape),
         scratch_shapes=[pltpu.VMEM((512, inner), BF16), pltpu.VMEM((256, width), F32)],
     )(expert_hidden, weight)
-    partial = call(
-        lambda *refs: partial_kernel((groups * rows) ** (-0.5), *refs),
-        jax.ShapeDtypeStruct((inner, features), F32),
-        2 * product,
-        8 * 10**6,
-        grid=(QUARTERS,),
-        in_specs=[whole((rows, inner)), column(256), last],
-        out_specs=column(inner),
-        scratch_shapes=[pltpu.VMEM((inner, rows), BF16)],
-    )(expert_hidden, arrived, arrived)
-    weight_grad = lax.psum_scatter(partial, "dp", scatter_dimension=0, tiled=True)
-    returned = exchange(expert_rows, peers)
+
+    def partial(arrived):
+        return call(
+            lambda *refs: partial_kernel((groups * rows) ** (-0.5), *refs),
+            (
+                jax.ShapeDtypeStruct((11 * CHUNK, half), BF16),
+                jax.ShapeDtypeStruct((10 * CHUNK, half), BF16),
+                jax.ShapeDtypeStruct((11 * CHUNK, half), F32),
+            ),
+            product,
+            4 * 10**6,
+            grid=(QUARTERS,),
+            in_specs=[whole((inner, rows)), half_low, half_left],
+            out_specs=tuple(block(n * CHUNK, lambda q: q) for n in (11, 10, 11)),
+        )(turned, arrived, arrived)
+
+    first = exchange(outgoing[0], peers)
+    first, behind = lax.optimization_barrier((first, outgoing[1]))
+    second = exchange(behind, peers)
+    down_0, up_0, own_0 = partial(first)
+    above_0, below_0 = shift(down_0, -1), shift(up_0, 1)
+    down_1, up_1, own_1 = partial(second)
+    above_1, below_1 = shift(down_1, -1), shift(up_1, 1)
     hidden_grad = call(
         hidden_grad_kernel,
         jax.ShapeDtypeStruct((rows, inner), BF16),
         2 * product,
         6 * 10**6,
         grid=(QUARTERS,),
-        in_specs=[column(256), last, column(inner)],
+        in_specs=[half_low, half_left, block(inner, lambda q: q)]
+        + [half_low, half_left, block(inner, lambda q: QUARTERS + q)],
         out_specs=whole((rows, inner)),
         scratch_shapes=[pltpu.VMEM((rows, inner), F32)],
-    )(arrived, arrived, weight)
-    layer_out, router_grad = call(
-        combine_kernel,
-        (
-            jax.ShapeDtypeStruct((tokens, features), BF16),
-            jax.ShapeDtypeStruct((2, tokens), F32),
-        ),
-        8 * 256 * tokens * features,
-        3 * 10**6,
-    )(ids, probs, cotangent, returned)
+    )(first, first, weight, second, second, weight)
+    above_1, below_1, hidden_grad = lax.optimization_barrier((above_1, below_1, hidden_grad))
+
+    def combine(packed_rows):
+        return call(
+            combine_kernel,
+            (
+                jax.ShapeDtypeStruct((tokens, features), BF16),
+                jax.ShapeDtypeStruct((2, tokens), F32),
+            ),
+            8 * 256 * tokens * features,
+            3 * 10**6,
+        )(ids, probs, cotangent, exchange(packed_rows, peers))
+
+    weight_grad, (layer_out, router_grad) = sum_over_groups(
+        ((above_0, below_0, own_0), (above_1, below_1, own_1)), expert_rows, combine
+    )
     return (layer_out, router_grad.T, hidden_grad, weight_grad[None])
 
 

time: 204 us -> 161 us (0.79)
  the two profiles are of different devices: /device:TPU:8 before, /device:TPU:2 now
where the time goes in v3:
time: 161 us; the launch traced here: 159 us
  starting transfers between devices  78 us (48%)
  blocking collectives  27.6 us (17%)
  Pallas kernels  22.5 us (14%)
  waiting for transfers between devices  18.5 us (11%)
  other arithmetic  6.31 us (4%)
  local copies, waits for them, and re-layouts  5.59 us (3%)
    ppermute x14, starting transfers between devices, shift(): lax.ppermute(block, 'dp', [(i, (i + distance) % groups) for i in range(gr...  64.3 us
    all_to_all x1, blocking collectives, exchange(): lax.all_to_all(blocks, 'ep', split_axis=0, concat_axis=0, tiled=True)  27.6 us
    ppermute x14, waiting for transfers between devices, shift(): lax.ppermute(block, 'dp', [(i, (i + distance) % groups) for i in range(gr...  18.5 us
    all_to_all x2, starting transfers between devices, exchange(): lax.all_to_all(blocks, 'ep', split_axis=0, concat_axis=0, tiled=True)  13.7 us
    pallas_call x2, Pallas kernels, partial(): call(lambda *refs: partial_kernel((groups * rows) ** (-0.5), *refs), (jax...  7.93 us
    pallas_call x1, Pallas kernels, shards(): call(hidden_grad_kernel, jax.ShapeDtypeStruct((rows, inner), BF16), 2 * p...  5.87 us
    unnamed x40, local copies, waits for them, and re-layouts  5.59 us
    pallas_call x1, Pallas kernels, shards(): call(expert_kernel, packed, 2 * product, 6 * 10 ** 6, grid=(QUARTERS,), i...  4.31 us
  transfers between devices with their start and end apart: 16, of which 9 were waited for; matrix products, arithmetic and copies ran while one was open for 3% of the time, Pallas kernels for 13%

profile of v3, /device:TPU:2, one launch (start us, length us, event | category | flops | bytes accessed | tf_op | source)
XLA Modules:
  0.0 159.5 jit_solution(8204782502211548076)
XLA Ops:
  3.0 1.8 %shard_map.85 = (bf16[256,1280]{1,0:T(8,128)(2,1)S(1)}, bf16[256,1280]{1,0:T(8,128)(2,1)}) custom-call(s32[2,128]{1,0:T(2,128)S(1)} %bitcast.22, f32[2,128]{1,0:T(2,128)S(1)} %bitcast.24, bf16[128,2048]{1,0:T(8,128)(2,1)S(1)} %copy-done.5), custom_call_target="tpu_custom_call" | custom-call | flops 268435456 | bytes 2000000 | tf_op jit(solution)/shard_map/pallas_call | solution.py:240
  4.8 27.6 %all_to_all.15 = bf16[32,8,1280]{2,1,0:T(8,128)(2,1)} all-to-all(bf16[32,8,1280]{2,1,0:T(8,128)(2,1)S(1)} %bitcast.21), channel_id=1, replica_groups=mesh['ep'=32,'dp'=32] {'ep'}, dimensions={0} | all-to-all | bytes 1310720 | tf_op jit(solution)/shard_map/all_to_all | solution.py:220
  32.4 6.1 %all-to-all-start.1 = ((bf16[32,8,1280]{2,1,0:T(8,128)(2,1)}), bf16[32,8,1280]{2,1,0:T(8,128)(2,1)}, u32[]{:S(2)}, u32[]{:S(2)}) async-start(bf16[32,8,1280]{2,1,0:T(8,128)(2,1)} %bitcast.5), calls=%async_computation.1 | async-start | bytes 1310720 | tf_op jit(solution)/shard_map/all_to_all | solution.py:220
  40.4 3.6 %shard_map.86 = (bf16[264,1024]{1,0:T(8,128)(2,1)}, bf16[240,1024]{1,0:T(8,128)(2,1)}, f32[264,1024]{1,0:T(8,128)S(1)}) custom-call(bf16[768,320]{1,0:T(8,128)(2,1)S(1)} %shard_map.84.refs_0_, bf16[256,1280]{1,0:T(8,128)(2,1)S(1)} %bitcast.16, bf16[256,1280]{1,0:T(8,128)(2,1)S(1)} %bitcast.17), custom_call_target="tpu_custom_call" | custom-call | flops 1006632960 | bytes 4000000 | tf_op jit(solution)/shard_map/pallas_call | solution.py:263
  45.1 9.6 %collective-permute-start = (bf16[264,1024]{1,0:T(8,128)(2,1)}, bf16[264,1024]{1,0:T(8,128)(2,1)}, u32[]{:S(2)}, u32[]{:S(2)}) collective-permute-start(bf16[264,1024]{1,0:T(8,128)(2,1)} %get-tuple-element.29), channel_id=1, source_target_pairs={{0,31},{1,0},{2,1},{3,2},{4,3},{5,4},{6,5},{7,6},{8,7},{9,8},{10,9... | collective-permute-start | bytes 1622024 | tf_op jit(solution)/shard_map/ppermute | solution.py:129
  54.7 1.9 %collective-permute-start.4 = (bf16[240,1024]{1,0:T(8,128)(2,1)}, bf16[240,1024]{1,0:T(8,128)(2,1)}, u32[]{:S(2)}, u32[]{:S(2)}) collective-permute-start(bf16[240,1024]{1,0:T(8,128)(2,1)} %get-tuple-element.36), channel_id=1, source_target_pairs={{0,1},{1,2},{2,3},{3,4},{4,5},{5,6},{6,7},{7,8},{8,9},{9,10},{10,1... | collective-permute-start | bytes 1474568 | tf_op jit(solution)/shard_map/ppermute | solution.py:129
  56.6 4.3 %shard_map.89 = bf16[256,2560]{1,0:T(8,128)(2,1)} custom-call(bf16[320,768]{1,0:T(8,128)(2,1)S(1)} %copy-done.8, bf16[768,2048]{1,0:T(8,128)(2,1)S(1)} %bitcast.13), custom_call_target="tpu_custom_call" | custom-call | flops 2013265920 | bytes 6000000 | tf_op jit(solution)/shard_map/pallas_call | solution.py:251
  62.0 4.3 %shard_map.87 = (bf16[264,1024]{1,0:T(8,128)(2,1)S(1)}, bf16[240,1024]{1,0:T(8,128)(2,1)S(1)}, f32[264,1024]{1,0:T(8,128)S(1)}) custom-call(bf16[768,320]{1,0:T(8,128)(2,1)S(1)} %copy-done.14, bf16[256,1280]{1,0:T(8,128)(2,1)} %bitcast.6.refs_1_.refs_2_.refs_3_.refs_4_, bf16[256,1280]{1,0:T(8,128)(2,1)} %bitcast.6.refs_1_.refs_2_.refs_3_.refs_4_), custom_call_target="tpu_custom_call" | custom-call | flops 1006632960 | bytes 4000000 | tf_op jit(solution)/shard_map/pallas_call | solution.py:263
  66.3 1.9 %collective-permute-start.2 = (bf16[240,1024]{1,0:T(8,128)(2,1)S(1)}, bf16[240,1024]{1,0:T(8,128)(2,1)S(1)}, u32[]{:S(2)}, u32[]{:S(2)}) collective-permute-start(bf16[240,1024]{1,0:T(8,128)(2,1)S(1)} %get-tuple-element.33), channel_id=1, source_target_pairs={{0,1},{1,2},{2,3},{3,4},{4,5},{5,6},{6,7},{7,8},{8,9},{9,10},{10,1... | collective-permute-start | bytes 1474568 | tf_op jit(solution)/shard_map/ppermute | solution.py:129
  68.3 5.1 %collective-permute-start.1 = (bf16[264,1024]{1,0:T(8,128)(2,1)S(1)}, bf16[264,1024]{1,0:T(8,128)(2,1)S(1)}, u32[]{:S(2)}, u32[]{:S(2)}) collective-permute-start(bf16[264,1024]{1,0:T(8,128)(2,1)S(1)} %get-tuple-element.32), channel_id=1, source_target_pairs={{0,31},{1,0},{2,1},{3,2},{4,3},{5,4},{6,5},{7,6},{8,7},{9,8},{10,9... | collective-permute-start | bytes 1622024 | tf_op jit(solution)/shard_map/ppermute | solution.py:129
  73.4 1.8 %add_convert_fusion.1 = (bf16[24,1024]{1,0:T(8,128)(2,1)S(1)}, f32[24,1024]{1,0:T(8,128)}, f32[24,1024]{1,0:T(8,128)}, f32[24,1024]{1,0:T(8,128)}, bf16[24,1024]{1,0:T(8,128)(2,1)S(1)}) fusion(f32[264,1024]{1,0:T(8,128)S(1)} %copy-done.4, bf16[240,1024]{1,0:T(8,128)(2,1)} %collective-permute-done.4, bf16[264,1024]{1,0:T(8,128)(2,1)} %collective-permute-done), kind=kLoop, calls=%fused_computation.34 | loop fusion | flops 491520 | bytes 1327104 | tf_op jit(solution)/shard_map/convert
  75.2 1.9 %convert_add_fusion.3 = (f32[24,1024]{1,0:T(8,128)S(1)}, f32[24,1024]{1,0:T(8,128)S(1)}, f32[24,1024]{1,0:T(8,128)S(1)}, f32[24,1024]{1,0:T(8,128)S(1)}, f32[24,1024]{1,0:T(8,128)}, /*index=5*/f32[24,1024]{1,0:T(8,128)}) fusion(f32[264,1024]{1,0:T(8,128)S(1)} %copy-done.4, bf16[240,1024]{1,0:T(8,128)(2,1)} %collective-permute-done.4, ...), kind=kLoop, calls=%fused_computation.24 | loop fusion | flops 589824 | bytes 1769472 | tf_op jit(solution)/shard_map/add | solution.py:139
  77.1 5.9 %shard_map.88 = bf16[320,768]{1,0:T(8,128)(2,1)} custom-call(bf16[256,1280]{1,0:T(8,128)(2,1)S(1)} %bitcast.18, bf16[256,1280]{1,0:T(8,128)(2,1)S(1)} %bitcast.19, bf16[768,2048]{1,0:T(8,128)(2,1)S(1)} %bitcast.14, bf16[256,1280]{1,0:T(8,128)(2,1)} %bitcast.6.refs_1_.refs_2_.refs_3_.refs_4_, bf16[256,1280]{1,0:T(8,128)(2,1)} %bitcast.6.refs_1_.refs_2_.refs_3_.refs_4_, ...), custom_call_target="tpu_custom_call" | custom-call | flops 2013265920 | bytes 6000000 | tf_op jit(solution)/shard_map/pallas_call | solution.py:284
  83.0 1.7 %collective-permute-done.1 = bf16[264,1024]{1,0:T(8,128)(2,1)S(1)} collective-permute-done((bf16[264,1024]{1,0:T(8,128)(2,1)S(1)}, bf16[264,1024]{1,0:T(8,128)(2,1)S(1)}, u32[]{:S(2)}, u32[]{:S(2)}) %collective-permute-start.1) | collective-permute-done | bytes 540704 | tf_op jit(solution)/shard_map/ppermute | solution.py:129
  84.9 1.9 %collective-permute-start.3 = (bf16[24,2048]{1,0:T(8,128)(2,1)S(1)}, bf16[24,2048]{1,0:T(8,128)(2,1)S(1)}, u32[]{:S(2)}, u32[]{:S(2)}) collective-permute-start(bf16[24,2048]{1,0:T(8,128)(2,1)S(1)} %pad_maximum_fusion), channel_id=1, source_target_pairs={{0,3},{1,4},{2,5},{3,6},{4,7},{5,8},{6,9},{7,10},{8,11},{9,12},{10... | collective-permute-start | bytes 294920 | tf_op jit(solution)/shard_map/ppermute | solution.py:129
  87.4 6.9 %collective-permute-start.8 = (bf16[24,2048]{1,0:T(8,128)(2,1)}, bf16[24,2048]{1,0:T(8,128)(2,1)}, u32[]{:S(2)}, u32[]{:S(2)}) collective-permute-start(bf16[24,2048]{1,0:T(8,128)(2,1)} %pad_maximum_fusion.1), channel_id=1, source_target_pairs={{0,29},{1,30},{2,31},{3,0},{4,1},{5,2},{6,3},{7,4},{8,5},{9,6},{10... | collective-permute-start | bytes 294920 | tf_op jit(solution)/shard_map/ppermute | solution.py:129
  95.2 7.6 %all-to-all-start.2 = ((bf16[32,8,2560]{2,1,0:T(8,128)(2,1)}), bf16[32,8,2560]{2,1,0:T(8,128)(2,1)S(1)}, u32[]{:S(2)}, u32[]{:S(2)}) async-start(bf16[32,8,2560]{2,1,0:T(8,128)(2,1)} %bitcast.8), calls=%async_computation.2 | async-start | bytes 2621440 | tf_op jit(solution)/shard_map/all_to_all | solution.py:220
  102.9 2.1 %collective-permute-start.5 = (bf16[24,2048]{1,0:T(8,128)(2,1)S(1)}, bf16[24,2048]{1,0:T(8,128)(2,1)S(1)}, u32[]{:S(2)}, u32[]{:S(2)}) collective-permute-start(bf16[24,2048]{1,0:T(8,128)(2,1)S(1)} %fusion), channel_id=1, source_target_pairs={{0,3},{1,4},{2,5},{3,6},{4,7},{5,8},{6,9},{7,10},{8,11},{9,12},{10... | collective-permute-start | bytes 294920 | tf_op jit(solution)/shard_map/ppermute | solution.py:129
  105.9 6.9 %collective-permute-start.9 = (bf16[24,2048]{1,0:T(8,128)(2,1)S(1)}, bf16[24,2048]{1,0:T(8,128)(2,1)S(1)}, u32[]{:S(2)}, u32[]{:S(2)}) collective-permute-start(bf16[24,2048]{1,0:T(8,128)(2,1)S(1)} %fusion.3), channel_id=1, source_target_pairs={{0,29},{1,30},{2,31},{3,0},{4,1},{5,2},{6,3},{7,4},{8,5},{9,6},{10... | collective-permute-start | bytes 294920 | tf_op jit(solution)/shard_map/ppermute | solution.py:129
  112.9 2.1 %collective-permute-done.5 = bf16[24,2048]{1,0:T(8,128)(2,1)S(1)} collective-permute-done((bf16[24,2048]{1,0:T(8,128)(2,1)S(1)}, bf16[24,2048]{1,0:T(8,128)(2,1)S(1)}, u32[]{:S(2)}, u32[]{:S(2)}) %collective-permute-start.5) | collective-permute-done | bytes 98336 | tf_op jit(solution)/shard_map/ppermute | solution.py:129
  115.0 1.9 %collective-permute-start.6 = (bf16[24,2048]{1,0:T(8,128)(2,1)S(1)}, bf16[24,2048]{1,0:T(8,128)(2,1)S(1)}, u32[]{:S(2)}, u32[]{:S(2)}) collective-permute-start(bf16[24,2048]{1,0:T(8,128)(2,1)S(1)} %fusion.1), channel_id=1, source_target_pairs={{0,3},{1,4},{2,5},{3,6},{4,7},{5,8},{6,9},{7,10},{8,11},{9,12},{10... | collective-permute-start | bytes 294920 | tf_op jit(solution)/shard_map/ppermute | solution.py:129
  117.0 2.3 %collective-permute-done.9 = bf16[24,2048]{1,0:T(8,128)(2,1)S(1)} collective-permute-done((bf16[24,2048]{1,0:T(8,128)(2,1)S(1)}, bf16[24,2048]{1,0:T(8,128)(2,1)S(1)}, u32[]{:S(2)}, u32[]{:S(2)}) %collective-permute-start.9) | collective-permute-done | bytes 98336 | tf_op jit(solution)/shard_map/ppermute | solution.py:129
  119.3 7.4 %collective-permute-start.10 = (bf16[24,2048]{1,0:T(8,128)(2,1)S(1)}, bf16[24,2048]{1,0:T(8,128)(2,1)S(1)}, u32[]{:S(2)}, u32[]{:S(2)}) collective-permute-start(bf16[24,2048]{1,0:T(8,128)(2,1)S(1)} %fusion.4), channel_id=1, source_target_pairs={{0,29},{1,30},{2,31},{3,0},{4,1},{5,2},{6,3},{7,4},{8,5},{9,6},{10... | collective-permute-start | bytes 294920 | tf_op jit(solution)/shard_map/ppermute | solution.py:129
  126.9 1.9 %collective-permute-start.7 = (bf16[24,2048]{1,0:T(8,128)(2,1)S(1)}, bf16[24,2048]{1,0:T(8,128)(2,1)S(1)}, u32[]{:S(2)}, u32[]{:S(2)}) collective-permute-start(bf16[24,2048]{1,0:T(8,128)(2,1)S(1)} %fusion.2), channel_id=1, source_target_pairs={{0,3},{1,4},{2,5},{3,6},{4,7},{5,8},{6,9},{7,10},{8,11},{9,12},{10... | collective-permute-start | bytes 294920 | tf_op jit(solution)/shard_map/ppermute | solution.py:129
  128.8 2.9 %collective-permute-done.10 = bf16[24,2048]{1,0:T(8,128)(2,1)S(1)} collective-permute-done((bf16[24,2048]{1,0:T(8,128)(2,1)S(1)}, bf16[24,2048]{1,0:T(8,128)(2,1)S(1)}, u32[]{:S(2)}, u32[]{:S(2)}) %collective-permute-start.10) | collective-permute-done | bytes 98336 | tf_op jit(solution)/shard_map/ppermute | solution.py:129
  131.8 7.4 %collective-permute-start.11 = (bf16[24,2048]{1,0:T(8,128)(2,1)S(1)}, bf16[24,2048]{1,0:T(8,128)(2,1)S(1)}, u32[]{:S(2)}, u32[]{:S(2)}) collective-permute-start(bf16[24,2048]{1,0:T(8,128)(2,1)S(1)} %fusion.5), channel_id=1, source_target_pairs={{0,29},{1,30},{2,31},{3,0},{4,1},{5,2},{6,3},{7,4},{8,5},{9,6},{10... | collective-permute-start | bytes 294920 | tf_op jit(solution)/shard_map/ppermute | solution.py:129
  139.2 1.8 %shard_map.90 = (bf16[128,2048]{1,0:T(8,128)(2,1)}, f32[2,128]{1,0:T(2,128)}) custom-call(s32[2,128]{1,0:T(2,128)S(1)} %bitcast.23, f32[2,128]{1,0:T(2,128)S(1)} %bitcast.25, bf16[128,2048]{1,0:T(8,128)(2,1)S(1)} %copy-done.6, bf16[256,2560]{1,0:T(8,128)(2,1)S(1)} %bitcast.20), custom_call_target="tpu_custom_call" | custom-call | flops 536870912 | bytes 3000000 | tf_op jit(solution)/shard_map/pallas_call | solution.py:298
  141.0 2.4 %collective-permute-done.11 = bf16[24,2048]{1,0:T(8,128)(2,1)S(1)} collective-permute-done((bf16[24,2048]{1,0:T(8,128)(2,1)S(1)}, bf16[24,2048]{1,0:T(8,128)(2,1)S(1)}, u32[]{:S(2)}, u32[]{:S(2)}) %collective-permute-start.11) | collective-permute-done | bytes 98336 | tf_op jit(solution)/shard_map/ppermute | solution.py:129
  143.4 5.4 %collective-permute-start.12 = (bf16[24,2048]{1,0:T(8,128)(2,1)S(1)}, bf16[24,2048]{1,0:T(8,128)(2,1)S(1)}, u32[]{:S(2)}, u32[]{:S(2)}) collective-permute-start(bf16[24,2048]{1,0:T(8,128)(2,1)S(1)} %fusion.8), channel_id=1, source_target_pairs={{0,3},{1,4},{2,5},{3,6},{4,7},{5,8},{6,9},{7,10},{8,11},{9,12},{10... | collective-permute-start | bytes 294920 | tf_op jit(solution)/shard_map/ppermute | solution.py:129
  148.9 3.8 %collective-permute-start.13 = (bf16[24,2048]{1,0:T(8,128)(2,1)S(1)}, bf16[24,2048]{1,0:T(8,128)(2,1)S(1)}, u32[]{:S(2)}, u32[]{:S(2)}) collective-permute-start(bf16[24,2048]{1,0:T(8,128)(2,1)S(1)} %fusion.9), channel_id=1, source_target_pairs={{0,29},{1,30},{2,31},{3,0},{4,1},{5,2},{6,3},{7,4},{8,5},{9,6},{10... | collective-permute-start | bytes 294920 | tf_op jit(solution)/shard_map/ppermute | solution.py:129
  152.7 2.1 %collective-permute-done.12 = bf16[24,2048]{1,0:T(8,128)(2,1)S(1)} collective-permute-done((bf16[24,2048]{1,0:T(8,128)(2,1)S(1)}, bf16[24,2048]{1,0:T(8,128)(2,1)S(1)}, u32[]{:S(2)}, u32[]{:S(2)}) %collective-permute-start.12) | collective-permute-done | bytes 98336 | tf_op jit(solution)/shard_map/ppermute | solution.py:129
  154.8 4.0 %collective-permute-done.13 = bf16[24,2048]{1,0:T(8,128)(2,1)S(1)} collective-permute-done((bf16[24,2048]{1,0:T(8,128)(2,1)S(1)}, bf16[24,2048]{1,0:T(8,128)(2,1)S(1)}, u32[]{:S(2)}, u32[]{:S(2)}) %collective-permute-start.13) | collective-permute-done | bytes 98336 | tf_op jit(solution)/shard_map/ppermute | solution.py:129
  (63 shorter events, 10.2 us)
Async XLA Ops:
  4.8 33.7 %copy-start.7 = (bf16[320,768]{1,0:T(8,128)(2,1)S(1)}, bf16[320,768]{1,0:T(8,128)(2,1)}, u32[]{:S(2)}) copy-start(bf16[320,768]{1,0:T(8,128)(2,1)} %hidden_ref.3) | copy-start | bytes 1474564
  32.4 28.6 %all-to-all-start.1 = ((bf16[32,8,1280]{2,1,0:T(8,128)(2,1)}), bf16[32,8,1280]{2,1,0:T(8,128)(2,1)}, u32[]{:S(2)}, u32[]{:S(2)}) async-start(bf16[32,8,1280]{2,1,0:T(8,128)(2,1)} %bitcast.5), calls=%async_computation.1 | async-start | bytes 1310720 | tf_op jit(solution)/shard_map/all_to_all | solution.py:220
  39.3 1.1 copy-start.1
  40.4 3.6 %copy-start.13 = (bf16[768,320]{1,0:T(8,128)(2,1)}, bf16[768,320]{1,0:T(8,128)(2,1)S(1)}, u32[]{:S(2)}) copy-start(bf16[768,320]{1,0:T(8,128)(2,1)S(1)} %shard_map.84.refs_0_) | copy-start | bytes 1474564
  40.4 16.2 %copy-start = (bf16[1,768,2048]{2,1,0:T(8,128)(2,1)S(1)}, bf16[1,768,2048]{2,1,0:T(8,128)(2,1)}, u32[]{:S(2)}) copy-start(bf16[1,768,2048]{2,1,0:T(8,128)(2,1)} %param.9) | copy-start | bytes 9437188
  40.4 16.2 %copy-start.8 = (bf16[320,768]{1,0:T(8,128)(2,1)S(1)}, bf16[320,768]{1,0:T(8,128)(2,1)}, u32[]{:S(2)}) copy-start(bf16[320,768]{1,0:T(8,128)(2,1)} %hidden_ref.3) | copy-start | bytes 1474564
  45.1 28.3 %collective-permute-start = (bf16[264,1024]{1,0:T(8,128)(2,1)}, bf16[264,1024]{1,0:T(8,128)(2,1)}, u32[]{:S(2)}, u32[]{:S(2)}) collective-permute-start(bf16[264,1024]{1,0:T(8,128)(2,1)} %get-tuple-element.29), channel_id=1, source_target_pairs={{0,31},{1,0},{2,1},{3,2},{4,3},{5,4},{6,5},{7,6},{8,7},{9,8},{10,9... | collective-permute-start | bytes 1622024 | tf_op jit(solution)/shard_map/ppermute | solution.py:129
  54.7 18.7 %collective-permute-start.4 = (bf16[240,1024]{1,0:T(8,128)(2,1)}, bf16[240,1024]{1,0:T(8,128)(2,1)}, u32[]{:S(2)}, u32[]{:S(2)}) collective-permute-start(bf16[240,1024]{1,0:T(8,128)(2,1)} %get-tuple-element.36), channel_id=1, source_target_pairs={{0,1},{1,2},{2,3},{3,4},{4,5},{5,6},{6,7},{7,8},{8,9},{9,10},{10,1... | collective-permute-start | bytes 1474568 | tf_op jit(solution)/shard_map/ppermute | solution.py:129
  61.0 1.1 copy-start.14
  62.0 11.4 %copy-start.4 = (f32[264,1024]{1,0:T(8,128)S(1)}, f32[264,1024]{1,0:T(8,128)}, u32[]{:S(2)}) copy-start(f32[264,1024]{1,0:T(8,128)} %copy-done.3) | copy-start | bytes 3244036
  66.3 16.6 %collective-permute-start.2 = (bf16[240,1024]{1,0:T(8,128)(2,1)S(1)}, bf16[240,1024]{1,0:T(8,128)(2,1)S(1)}, u32[]{:S(2)}, u32[]{:S(2)}) collective-permute-start(bf16[240,1024]{1,0:T(8,128)(2,1)S(1)} %get-tuple-element.33), channel_id=1, source_target_pairs={{0,1},{1,2},{2,3},{3,4},{4,5},{5,6},{6,7},{7,8},{8,9},{9,10},{10,1... | collective-permute-start | bytes 1474568 | tf_op jit(solution)/shard_map/ppermute | solution.py:129
  68.3 16.4 %collective-permute-start.1 = (bf16[264,1024]{1,0:T(8,128)(2,1)S(1)}, bf16[264,1024]{1,0:T(8,128)(2,1)S(1)}, u32[]{:S(2)}, u32[]{:S(2)}) collective-permute-start(bf16[264,1024]{1,0:T(8,128)(2,1)S(1)} %get-tuple-element.32), channel_id=1, source_target_pairs={{0,31},{1,0},{2,1},{3,2},{4,3},{5,4},{6,5},{7,6},{8,7},{9,8},{10,9... | collective-permute-start | bytes 1622024 | tf_op jit(solution)/shard_map/ppermute | solution.py:129
  75.2 1.9 %copy-start.2 = (bf16[32,8,1280]{2,1,0:T(8,128)(2,1)S(1)}, bf16[32,8,1280]{2,1,0:T(8,128)(2,1)}, u32[]{:S(2)}) copy-start(bf16[32,8,1280]{2,1,0:T(8,128)(2,1)} %all_to_all.15) | copy-start | bytes 1966084
  84.9 10.4 %collective-permute-start.3 = (bf16[24,2048]{1,0:T(8,128)(2,1)S(1)}, bf16[24,2048]{1,0:T(8,128)(2,1)S(1)}, u32[]{:S(2)}, u32[]{:S(2)}) collective-permute-start(bf16[24,2048]{1,0:T(8,128)(2,1)S(1)} %pad_maximum_fusion), channel_id=1, source_target_pairs={{0,3},{1,4},{2,5},{3,6},{4,7},{5,8},{6,9},{7,10},{8,11},{9,12},{10... | collective-permute-start | bytes 294920 | tf_op jit(solution)/shard_map/ppermute | solution.py:129
  87.4 17.6 %collective-permute-start.8 = (bf16[24,2048]{1,0:T(8,128)(2,1)}, bf16[24,2048]{1,0:T(8,128)(2,1)}, u32[]{:S(2)}, u32[]{:S(2)}) collective-permute-start(bf16[24,2048]{1,0:T(8,128)(2,1)} %pad_maximum_fusion.1), channel_id=1, source_target_pairs={{0,29},{1,30},{2,31},{3,0},{4,1},{5,2},{6,3},{7,4},{8,5},{9,6},{10... | collective-permute-start | bytes 294920 | tf_op jit(solution)/shard_map/ppermute | solution.py:129
  95.2 7.6 %copy-start.19 = (f32[24,1024]{1,0:T(8,128)S(1)}, f32[24,1024]{1,0:T(8,128)}, u32[]{:S(2)}) copy-start(f32[24,1024]{1,0:T(8,128)} %get-tuple-element.61) | copy-start | bytes 294916
  95.2 9.8 %copy-start.16 = (f32[24,1024]{1,0:T(8,128)S(1)}, f32[24,1024]{1,0:T(8,128)}, u32[]{:S(2)}) copy-start(f32[24,1024]{1,0:T(8,128)} %get-tuple-element.51) | copy-start | bytes 294916
  95.2 19.8 %copy-start.18 = (f32[24,1024]{1,0:T(8,128)S(1)}, f32[24,1024]{1,0:T(8,128)}, u32[]{:S(2)}) copy-start(f32[24,1024]{1,0:T(8,128)} %get-tuple-element.60) | copy-start | bytes 294916
  95.2 43.9 %all-to-all-start.2 = ((bf16[32,8,2560]{2,1,0:T(8,128)(2,1)}), bf16[32,8,2560]{2,1,0:T(8,128)(2,1)S(1)}, u32[]{:S(2)}, u32[]{:S(2)}) async-start(bf16[32,8,2560]{2,1,0:T(8,128)(2,1)} %bitcast.8), calls=%async_computation.2 | async-start | bytes 2621440 | tf_op jit(solution)/shard_map/all_to_all | solution.py:220
  102.8 16.4 %copy-start.15 = (f32[24,1024]{1,0:T(8,128)S(1)}, f32[24,1024]{1,0:T(8,128)}, u32[]{:S(2)}) copy-start(f32[24,1024]{1,0:T(8,128)} %get-tuple-element.50) | copy-start | bytes 294916
  102.8 24.0 %copy-start.17 = (f32[24,1024]{1,0:T(8,128)S(1)}, f32[24,1024]{1,0:T(8,128)}, u32[]{:S(2)}) copy-start(f32[24,1024]{1,0:T(8,128)} %get-tuple-element.59) | copy-start | bytes 294916
  102.9 36.3 %copy-start.6 = (bf16[128,2048]{1,0:T(8,128)(2,1)S(1)}, bf16[128,2048]{1,0:T(8,128)(2,1)}, u32[]{:S(2)}) copy-start(bf16[128,2048]{1,0:T(8,128)(2,1)} %cot_ref.3) | copy-start | bytes 1572868
  102.9 36.3 %copy-start.10 = (s32[128,2]{0,1:T(2,128)S(1)}, s32[128,2]{0,1:T(2,128)}, u32[]{:S(2)}) copy-start(s32[128,2]{0,1:T(2,128)} %param.6) | copy-start | bytes 3076
  102.9 36.3 %copy-start.12 = (f32[128,2]{0,1:T(2,128)S(1)}, f32[128,2]{0,1:T(2,128)}, u32[]{:S(2)}) copy-start(f32[128,2]{0,1:T(2,128)} %param.7) | copy-start | bytes 3076
  102.9 12.1 %collective-permute-start.5 = (bf16[24,2048]{1,0:T(8,128)(2,1)S(1)}, bf16[24,2048]{1,0:T(8,128)(2,1)S(1)}, u32[]{:S(2)}, u32[]{:S(2)}) collective-permute-start(bf16[24,2048]{1,0:T(8,128)(2,1)S(1)} %fusion), channel_id=1, source_target_pairs={{0,3},{1,4},{2,5},{3,6},{4,7},{5,8},{6,9},{7,10},{8,11},{9,12},{10... | collective-permute-start | bytes 294920 | tf_op jit(solution)/shard_map/ppermute | solution.py:129
  105.9 13.3 %collective-permute-start.9 = (bf16[24,2048]{1,0:T(8,128)(2,1)S(1)}, bf16[24,2048]{1,0:T(8,128)(2,1)S(1)}, u32[]{:S(2)}, u32[]{:S(2)}) collective-permute-start(bf16[24,2048]{1,0:T(8,128)(2,1)S(1)} %fusion.3), channel_id=1, source_target_pairs={{0,29},{1,30},{2,31},{3,0},{4,1},{5,2},{6,3},{7,4},{8,5},{9,6},{10... | collective-permute-start | bytes 294920 | tf_op jit(solution)/shard_map/ppermute | solution.py:129
  115.0 11.8 %collective-permute-start.6 = (bf16[24,2048]{1,0:T(8,128)(2,1)S(1)}, bf16[24,2048]{1,0:T(8,128)(2,1)S(1)}, u32[]{:S(2)}, u32[]{:S(2)}) collective-permute-start(bf16[24,2048]{1,0:T(8,128)(2,1)S(1)} %fusion.1), channel_id=1, source_target_pairs={{0,3},{1,4},{2,5},{3,6},{4,7},{5,8},{6,9},{7,10},{8,11},{9,12},{10... | collective-permute-start | bytes 294920 | tf_op jit(solution)/shard_map/ppermute | solution.py:129
  119.3 12.5 %collective-permute-start.10 = (bf16[24,2048]{1,0:T(8,128)(2,1)S(1)}, bf16[24,2048]{1,0:T(8,128)(2,1)S(1)}, u32[]{:S(2)}, u32[]{:S(2)}) collective-permute-start(bf16[24,2048]{1,0:T(8,128)(2,1)S(1)} %fusion.4), channel_id=1, source_target_pairs={{0,29},{1,30},{2,31},{3,0},{4,1},{5,2},{6,3},{7,4},{8,5},{9,6},{10... | collective-permute-start | bytes 294920 | tf_op jit(solution)/shard_map/ppermute | solution.py:129
  126.9 14.1 %collective-permute-start.7 = (bf16[24,2048]{1,0:T(8,128)(2,1)S(1)}, bf16[24,2048]{1,0:T(8,128)(2,1)S(1)}, u32[]{:S(2)}, u32[]{:S(2)}) collective-permute-start(bf16[24,2048]{1,0:T(8,128)(2,1)S(1)} %fusion.2), channel_id=1, source_target_pairs={{0,3},{1,4},{2,5},{3,6},{4,7},{5,8},{6,9},{7,10},{8,11},{9,12},{10... | collective-permute-start | bytes 294920 | tf_op jit(solution)/shard_map/ppermute | solution.py:129
  131.8 11.6 %collective-permute-start.11 = (bf16[24,2048]{1,0:T(8,128)(2,1)S(1)}, bf16[24,2048]{1,0:T(8,128)(2,1)S(1)}, u32[]{:S(2)}, u32[]{:S(2)}) collective-permute-start(bf16[24,2048]{1,0:T(8,128)(2,1)S(1)} %fusion.5), channel_id=1, source_target_pairs={{0,29},{1,30},{2,31},{3,0},{4,1},{5,2},{6,3},{7,4},{8,5},{9,6},{10... | collective-permute-start | bytes 294920 | tf_op jit(solution)/shard_map/ppermute | solution.py:129
  143.4 11.4 %collective-permute-start.12 = (bf16[24,2048]{1,0:T(8,128)(2,1)S(1)}, bf16[24,2048]{1,0:T(8,128)(2,1)S(1)}, u32[]{:S(2)}, u32[]{:S(2)}) collective-permute-start(bf16[24,2048]{1,0:T(8,128)(2,1)S(1)} %fusion.8), channel_id=1, source_target_pairs={{0,3},{1,4},{2,5},{3,6},{4,7},{5,8},{6,9},{7,10},{8,11},{9,12},{10... | collective-permute-start | bytes 294920 | tf_op jit(solution)/shard_map/ppermute | solution.py:129
  148.9 9.9 %collective-permute-start.13 = (bf16[24,2048]{1,0:T(8,128)(2,1)S(1)}, bf16[24,2048]{1,0:T(8,128)(2,1)S(1)}, u32[]{:S(2)}, u32[]{:S(2)}) collective-permute-start(bf16[24,2048]{1,0:T(8,128)(2,1)S(1)} %fusion.9), channel_id=1, source_target_pairs={{0,29},{1,30},{2,31},{3,0},{4,1},{5,2},{6,3},{7,4},{8,5},{9,6},{10... | collective-permute-start | bytes 294920 | tf_op jit(solution)/shard_map/ppermute | solution.py:129
  (4 other events, 3.4 us)

commit v4 on v3

--- a/solution.py
+++ b/solution.py
@@ -103,15 +103,15 @@
     return dot(onehot(in_low | in_left), jnp.concatenate([low, left], axis=0)).astype(BF16)
 
 
-def chunk_order(group, rows):
+def chunk_order(group, sign, rows):
     block = (rows * 2731) >> 16
     offset = jnp.where(block < 11, 14 - 3 * block, jnp.where(block < 21, 46 - 3 * block, 78 - 3 * block))
-    return ((group + offset) & 31) * CHUNK + rows - block * CHUNK
-
-
-def turn_kernel(group_ref, hidden_ref, turned_ref):
+    return ((group + sign * offset) & 31) * CHUNK + rows - block * CHUNK
+
+
+def turn_kernel(place_ref, hidden_ref, turned_ref):
     inner = hidden_ref.shape[1]
-    source = chunk_order(group_ref[0], iota((1, inner), 1))
+    source = chunk_order(place_ref[0], place_ref[1], iota((1, inner), 1))
     select = onehot(iota((inner, inner), 0) == source)
     turned_ref[...] = dot(select, hidden_ref[...], 0, 1).astype(BF16)
 
@@ -125,11 +125,16 @@
 
 
 def shift(block, distance):
-    groups = lax.axis_size("dp")
-    return lax.ppermute(block, "dp", [(i, (i + distance) % groups) for i in range(groups)])
-
-
-def sum_over_groups(halves, expert_rows, combine):
+    peers, groups = lax.axis_size("ep"), lax.axis_size("dp")
+    pairs = [
+        (e * groups + i, e * groups + (i + (distance if e % 2 == 0 else -distance)) % groups)
+        for e in range(peers)
+        for i in range(groups)
+    ]
+    return lax.ppermute(block, ("ep", "dp"), pairs)
+
+
+def sum_over_groups(halves, returned, combine):
     def term(k):
         parts = []
         for from_above, from_below, own in halves:
@@ -143,11 +148,8 @@
     rising, falling = term(0), term(10)
     for k in range(1, 5):
         rising, falling = shift(rising.astype(BF16), 3), shift(falling.astype(BF16), -3)
-        if k == 1:
-            rising, expert_rows = lax.optimization_barrier((rising, expert_rows))
-            combined = combine(expert_rows)
         if k == 4:
-            rising, falling, combined = lax.optimization_barrier((rising, falling, combined))
+            rising, falling, combined = lax.optimization_barrier((rising, falling, combine(returned)))
         rising, falling = rising.astype(F32) + term(k), falling.astype(F32) + term(10 - k)
     rising, falling = shift(rising.astype(BF16), 3), shift(falling.astype(BF16), -3)
     return term(5) + rising.astype(F32) + falling.astype(F32), combined
@@ -240,14 +242,15 @@
     outgoing = call(send_kernel, (half_packed,) * HALVES, 4 * 256 * tokens * features, 2 * 10**6)(
         ids, probs, cotangent
     )
-    group = lax.axis_index("dp").astype(jnp.int32).reshape(1)
+    sign = 1 - 2 * (lax.axis_index("ep") & 1)
+    place = jnp.stack([lax.axis_index("dp"), sign]).astype(jnp.int32)
     turned = call(
         turn_kernel,
         jax.ShapeDtypeStruct((inner, rows), BF16),
         2 * inner * inner * rows,
         10**6,
         in_specs=[pl.BlockSpec(memory_space=pltpu.SMEM), pl.BlockSpec(memory_space=pltpu.VMEM)],
-    )(group, expert_hidden)
+    )(place, expert_hidden)
     expert_rows = call(
         expert_kernel,
         packed,
@@ -275,12 +278,15 @@
         )(turned, arrived, arrived)
 
     first = exchange(outgoing[0], peers)
+    turned, expert_rows, first = lax.optimization_barrier((turned, expert_rows, first))
     first, behind = lax.optimization_barrier((first, outgoing[1]))
     second = exchange(behind, peers)
     down_0, up_0, own_0 = partial(first)
     above_0, below_0 = shift(down_0, -1), shift(up_0, 1)
     down_1, up_1, own_1 = partial(second)
     above_1, below_1 = shift(down_1, -1), shift(up_1, 1)
+    above_0, below_0, own_1, expert_rows = lax.optimization_barrier((above_0, below_0, own_1, expert_rows))
+    returned = exchange(expert_rows, peers)
     hidden_grad = call(
         hidden_grad_kernel,
         jax.ShapeDtypeStruct((rows, inner), BF16),
@@ -292,9 +298,8 @@
         out_specs=whole((rows, inner)),
         scratch_shapes=[pltpu.VMEM((rows, inner), F32)],
     )(first, first, weight, second, second, weight)
-    above_1, below_1, hidden_grad = lax.optimization_barrier((above_1, below_1, hidden_grad))
-
-    def combine(packed_rows):
+
+    def combine(returned):
         return call(
             combine_kernel,
             (
@@ -303,10 +308,10 @@
             ),
             8 * 256 * tokens * features,
             3 * 10**6,
-        )(ids, probs, cotangent, exchange(packed_rows, peers))
+        )(ids, probs, cotangent, returned)
 
     weight_grad, (layer_out, router_grad) = sum_over_groups(
-        ((above_0, below_0, own_0), (above_1, below_1, own_1)), expert_rows, combine
+        ((above_0, below_0, own_0), (above_1, below_1, own_1)), returned, combine
     )
     return (layer_out, router_grad.T, hidden_grad, weight_grad[None])
 

time: 161 us -> 155 us (0.963)
  the two profiles are of different devices: /device:TPU:2 before, /device:TPU:40 now
where the time goes in v4:
time: 155 us; the launch traced here: 154 us
  starting transfers between devices  88.6 us (57%)
  Pallas kernels  23.9 us (15%)
  waiting for transfers between devices  18.2 us (12%)
  local copies, waits for them, and re-layouts  12.7 us (8%)
  other arithmetic  9.55 us (6%)
    ppermute x14, starting transfers between devices, shift(): return lax.ppermute(block, ('ep', 'dp'), pairs)  67.9 us
    all_to_all x3, starting transfers between devices, exchange(): lax.all_to_all(blocks, 'ep', split_axis=0, concat_axis=0, tiled=True)  20.7 us
    ppermute x14, waiting for transfers between devices, shift(): return lax.ppermute(block, ('ep', 'dp'), pairs)  14.4 us
    unnamed x42, local copies, waits for them, and re-layouts  12.7 us
    pallas_call x2, Pallas kernels, partial(): call(lambda *refs: partial_kernel((groups * rows) ** (-0.5), *refs), (jax...  9.35 us
    pallas_call x1, Pallas kernels, shards(): call(hidden_grad_kernel, jax.ShapeDtypeStruct((rows, inner), BF16), 2 * p...  5.91 us
    all_to_all x3, waiting for transfers between devices, exchange(): lax.all_to_all(blocks, 'ep', split_axis=0, concat_axis=0, tiled=True)  3.85 us
    pallas_call x1, Pallas kernels, shards(): call(expert_kernel, packed, 2 * product, 6 * 10 ** 6, grid=(QUARTERS,), i...  3.2 us
  transfers between devices with their start and end apart: 17, of which 6 were waited for; matrix products, arithmetic and copies ran while one was open for 5% of the time, Pallas kernels for 15%

profile of v4, /device:TPU:40, one launch (start us, length us, event | category | flops | bytes accessed | tf_op | source)
XLA Modules:
  0.0 154.0 jit_solution(12800486159886824999)
XLA Ops:
  5.6 7.6 %all-to-all-start = ((bf16[32,8,1280]{2,1,0:T(8,128)(2,1)}), bf16[32,8,1280]{2,1,0:T(8,128)(2,1)}, u32[]{:S(2)}, u32[]{:S(2)}) async-start(bf16[32,8,1280]{2,1,0:T(8,128)(2,1)} %bitcast.19), calls=%async_computation | async-start | bytes 1310720 | tf_op jit(solution)/shard_map/all_to_all | solution.py:222
  14.3 1.4 shard_map.84.refs_0_
  16.5 3.2 %shard_map.85 = bf16[256,2560]{1,0:T(8,128)(2,1)S(1)} custom-call(bf16[320,768]{1,0:T(8,128)(2,1)S(1)} %copy-done.11, bf16[768,2048]{1,0:T(8,128)(2,1)S(1)} %bitcast.14), custom_call_target="tpu_custom_call" | custom-call | flops 2013265920 | bytes 6000000 | tf_op jit(solution)/shard_map/pallas_call | solution.py:254
  20.9 3.8 %all-to-all-done = bf16[32,8,1280]{2,1,0:T(8,128)(2,1)} async-done(((bf16[32,8,1280]{2,1,0:T(8,128)(2,1)}), bf16[32,8,1280]{2,1,0:T(8,128)(2,1)}, u32[]{:S(2)}, u32[]{:S(2)}) %all-to-all-start) | async-done | bytes 655392 | tf_op jit(solution)/shard_map/all_to_all | solution.py:222
  24.7 5.5 %all-to-all-start.1 = ((bf16[32,8,1280]{2,1,0:T(8,128)(2,1)}), bf16[32,8,1280]{2,1,0:T(8,128)(2,1)}, u32[]{:S(2)}, u32[]{:S(2)}) async-start(bf16[32,8,1280]{2,1,0:T(8,128)(2,1)} %bitcast.18), calls=%async_computation.1 | async-start | bytes 1310720 | tf_op jit(solution)/shard_map/all_to_all | solution.py:222
  31.3 4.7 %shard_map.87 = (bf16[264,1024]{1,0:T(8,128)(2,1)}, bf16[240,1024]{1,0:T(8,128)(2,1)}, f32[264,1024]{1,0:T(8,128)S(1)}) custom-call(bf16[768,320]{1,0:T(8,128)(2,1)S(1)} %copy-done.17, bf16[256,1280]{1,0:T(8,128)(2,1)} %bitcast.6.refs_1_.refs_2_.refs_0_, bf16[256,1280]{1,0:T(8,128)(2,1)} %bitcast.6.refs_1_.refs_2_.refs_0_), custom_call_target="tpu_custom_call" | custom-call | flops 1006632960 | bytes 4000000 | tf_op jit(solution)/shard_map/pallas_call | solution.py:266
  37.0 11.8 %collective-permute-start = (bf16[264,1024]{1,0:T(8,128)(2,1)}, bf16[264,1024]{1,0:T(8,128)(2,1)}, u32[]{:S(2)}, u32[]{:S(2)}) collective-permute-start(bf16[264,1024]{1,0:T(8,128)(2,1)} %get-tuple-element.33), channel_id=1, source_target_pairs={{0,31},{1,0},{2,1},{3,2},{4,3},{5,4},{6,5},{7,6},{8,7},{9,8},{10,9... | collective-permute-start | bytes 1622024 | tf_op jit(solution)/shard_map/ppermute | solution.py:134
  48.8 1.9 %collective-permute-start.1 = (bf16[240,1024]{1,0:T(8,128)(2,1)}, bf16[240,1024]{1,0:T(8,128)(2,1)}, u32[]{:S(2)}, u32[]{:S(2)}) collective-permute-start(bf16[240,1024]{1,0:T(8,128)(2,1)} %get-tuple-element.34), channel_id=1, source_target_pairs={{0,1},{1,2},{2,3},{3,4},{4,5},{5,6},{6,7},{7,8},{8,9},{9,10},{10,1... | collective-permute-start | bytes 1474568 | tf_op jit(solution)/shard_map/ppermute | solution.py:134
  51.8 4.7 %shard_map.88 = (bf16[264,1024]{1,0:T(8,128)(2,1)}, bf16[240,1024]{1,0:T(8,128)(2,1)}, f32[264,1024]{1,0:T(8,128)S(1)}) custom-call(bf16[768,320]{1,0:T(8,128)(2,1)S(1)} %copy-done.18, bf16[256,1280]{1,0:T(8,128)(2,1)} %bitcast.8.refs_1_.refs_2_.refs_3_.refs_4_, bf16[256,1280]{1,0:T(8,128)(2,1)} %bitcast.8.refs_1_.refs_2_.refs_3_.refs_4_), custom_call_target="tpu_custom_call" | custom-call | flops 1006632960 | bytes 4000000 | tf_op jit(solution)/shard_map/pallas_call | solution.py:266
  57.5 8.9 %collective-permute-start.2 = (bf16[264,1024]{1,0:T(8,128)(2,1)}, bf16[264,1024]{1,0:T(8,128)(2,1)}, u32[]{:S(2)}, u32[]{:S(2)}) collective-permute-start(bf16[264,1024]{1,0:T(8,128)(2,1)} %get-tuple-element.40), channel_id=1, source_target_pairs={{0,31},{1,0},{2,1},{3,2},{4,3},{5,4},{6,5},{7,6},{8,7},{9,8},{10,9... | collective-permute-start | bytes 1622024 | tf_op jit(solution)/shard_map/ppermute | solution.py:134
  66.4 1.9 %collective-permute-start.4 = (bf16[240,1024]{1,0:T(8,128)(2,1)}, bf16[240,1024]{1,0:T(8,128)(2,1)}, u32[]{:S(2)}, u32[]{:S(2)}) collective-permute-start(bf16[240,1024]{1,0:T(8,128)(2,1)} %get-tuple-element.42), channel_id=1, source_target_pairs={{0,1},{1,2},{2,3},{3,4},{4,5},{5,6},{6,7},{7,8},{8,9},{9,10},{10,1... | collective-permute-start | bytes 1474568 | tf_op jit(solution)/shard_map/ppermute | solution.py:134
  68.3 7.5 %all-to-all-start.2 = ((bf16[32,8,2560]{2,1,0:T(8,128)(2,1)}), bf16[32,8,2560]{2,1,0:T(8,128)(2,1)}, u32[]{:S(2)}, u32[]{:S(2)}) async-start(bf16[32,8,2560]{2,1,0:T(8,128)(2,1)} %bitcast.17), calls=%async_computation.2 | async-start | bytes 2621440 | tf_op jit(solution)/shard_map/all_to_all | solution.py:222
  75.9 1.3 add_convert_fusion.1
  77.5 1.2 convert_add_fusion.3
  80.1 1.9 %collective-permute-start.3 = (bf16[24,2048]{1,0:T(8,128)(2,1)S(1)}, bf16[24,2048]{1,0:T(8,128)(2,1)S(1)}, u32[]{:S(2)}, u32[]{:S(2)}) collective-permute-start(bf16[24,2048]{1,0:T(8,128)(2,1)S(1)} %pad_maximum_fusion), channel_id=1, source_target_pairs={{0,3},{1,4},{2,5},{3,6},{4,7},{5,8},{6,9},{7,10},{8,11},{9,12},{10... | collective-permute-start | bytes 294920 | tf_op jit(solution)/shard_map/ppermute | solution.py:134
  82.0 6.9 %collective-permute-start.8 = (bf16[24,2048]{1,0:T(8,128)(2,1)S(1)}, bf16[24,2048]{1,0:T(8,128)(2,1)S(1)}, u32[]{:S(2)}, u32[]{:S(2)}) collective-permute-start(bf16[24,2048]{1,0:T(8,128)(2,1)S(1)} %pad_maximum_fusion.1), channel_id=1, source_target_pairs={{0,29},{1,30},{2,31},{3,0},{4,1},{5,2},{6,3},{7,4},{8,5},{9,6},{10... | collective-permute-start | bytes 294920 | tf_op jit(solution)/shard_map/ppermute | solution.py:134
  89.0 1.8 %convert_add_fusion.2 = (f32[24,1024]{1,0:T(8,128)}, f32[24,1024]{1,0:T(8,128)}, f32[24,1024]{1,0:T(8,128)S(1)}, f32[24,1024]{1,0:T(8,128)S(1)}, f32[24,1024]{1,0:T(8,128)S(1)}, /*index=5*/f32[24,1024]{1,0:T(8,128)S(1)}) fusion(f32[264,1024]{1,0:T(8,128)S(1)} %copy-done.3, bf16[240,1024]{1,0:T(8,128)(2,1)} %collective-permute-done.4, ...), kind=kLoop, calls=%fused_computation.23 | loop fusion | flops 589824 | bytes 1769472 | tf_op jit(solution)/shard_map/add | solution.py:144
  90.9 1.9 %collective-permute-start.5 = (bf16[24,2048]{1,0:T(8,128)(2,1)S(1)}, bf16[24,2048]{1,0:T(8,128)(2,1)S(1)}, u32[]{:S(2)}, u32[]{:S(2)}) collective-permute-start(bf16[24,2048]{1,0:T(8,128)(2,1)S(1)} %fusion), channel_id=1, source_target_pairs={{0,3},{1,4},{2,5},{3,6},{4,7},{5,8},{6,9},{7,10},{8,11},{9,12},{10... | collective-permute-start | bytes 294920 | tf_op jit(solution)/shard_map/ppermute | solution.py:134
  92.8 2.3 %collective-permute-done.8 = bf16[24,2048]{1,0:T(8,128)(2,1)S(1)} collective-permute-done((bf16[24,2048]{1,0:T(8,128)(2,1)S(1)}, bf16[24,2048]{1,0:T(8,128)(2,1)S(1)}, u32[]{:S(2)}, u32[]{:S(2)}) %collective-permute-start.8) | collective-permute-done | bytes 98336 | tf_op jit(solution)/shard_map/ppermute | solution.py:134
  95.1 7.4 %collective-permute-start.9 = (bf16[24,2048]{1,0:T(8,128)(2,1)S(1)}, bf16[24,2048]{1,0:T(8,128)(2,1)S(1)}, u32[]{:S(2)}, u32[]{:S(2)}) collective-permute-start(bf16[24,2048]{1,0:T(8,128)(2,1)S(1)} %fusion.3), channel_id=1, source_target_pairs={{0,29},{1,30},{2,31},{3,0},{4,1},{5,2},{6,3},{7,4},{8,5},{9,6},{10... | collective-permute-start | bytes 294920 | tf_op jit(solution)/shard_map/ppermute | solution.py:134
  102.6 1.9 %collective-permute-start.6 = (bf16[24,2048]{1,0:T(8,128)(2,1)S(1)}, bf16[24,2048]{1,0:T(8,128)(2,1)S(1)}, u32[]{:S(2)}, u32[]{:S(2)}) collective-permute-start(bf16[24,2048]{1,0:T(8,128)(2,1)S(1)} %fusion.1), channel_id=1, source_target_pairs={{0,3},{1,4},{2,5},{3,6},{4,7},{5,8},{6,9},{7,10},{8,11},{9,12},{10... | collective-permute-start | bytes 294920 | tf_op jit(solution)/shard_map/ppermute | solution.py:134
  104.5 1.2 collective-permute-done.9
  105.7 6.6 %collective-permute-start.10 = (bf16[24,2048]{1,0:T(8,128)(2,1)S(1)}, bf16[24,2048]{1,0:T(8,128)(2,1)S(1)}, u32[]{:S(2)}, u32[]{:S(2)}) collective-permute-start(bf16[24,2048]{1,0:T(8,128)(2,1)S(1)} %fusion.4), channel_id=1, source_target_pairs={{0,29},{1,30},{2,31},{3,0},{4,1},{5,2},{6,3},{7,4},{8,5},{9,6},{10... | collective-permute-start | bytes 294920 | tf_op jit(solution)/shard_map/ppermute | solution.py:134
  113.0 2.3 %collective-permute-start.7 = (bf16[24,2048]{1,0:T(8,128)(2,1)}, bf16[24,2048]{1,0:T(8,128)(2,1)}, u32[]{:S(2)}, u32[]{:S(2)}) collective-permute-start(bf16[24,2048]{1,0:T(8,128)(2,1)} %fusion.2), channel_id=1, source_target_pairs={{0,3},{1,4},{2,5},{3,6},{4,7},{5,8},{6,9},{7,10},{8,11},{9,12},{10... | collective-permute-start | bytes 294920 | tf_op jit(solution)/shard_map/ppermute | solution.py:134
  115.2 3.6 %collective-permute-done.10 = bf16[24,2048]{1,0:T(8,128)(2,1)S(1)} collective-permute-done((bf16[24,2048]{1,0:T(8,128)(2,1)S(1)}, bf16[24,2048]{1,0:T(8,128)(2,1)S(1)}, u32[]{:S(2)}, u32[]{:S(2)}) %collective-permute-start.10) | collective-permute-done | bytes 98336 | tf_op jit(solution)/shard_map/ppermute | solution.py:134
  119.5 5.2 %collective-permute-start.11 = (bf16[24,2048]{1,0:T(8,128)(2,1)}, bf16[24,2048]{1,0:T(8,128)(2,1)}, u32[]{:S(2)}, u32[]{:S(2)}) collective-permute-start(bf16[24,2048]{1,0:T(8,128)(2,1)} %fusion.5), channel_id=1, source_target_pairs={{0,29},{1,30},{2,31},{3,0},{4,1},{5,2},{6,3},{7,4},{8,5},{9,6},{10... | collective-permute-start | bytes 294920 | tf_op jit(solution)/shard_map/ppermute | solution.py:134
  125.7 3.1 %shard_map.89 = (bf16[128,2048]{1,0:T(8,128)(2,1)}, f32[2,128]{1,0:T(2,128)}) custom-call(s32[2,128]{1,0:T(2,128)S(1)} %bitcast.21, f32[2,128]{1,0:T(2,128)S(1)} %bitcast.23, bf16[128,2048]{1,0:T(8,128)(2,1)S(1)} %copy-done.9, bf16[256,2560]{1,0:T(8,128)(2,1)} %bitcast.10.rows_ref), custom_call_target="tpu_custom_call" | custom-call | flops 536870912 | bytes 3000000 | tf_op jit(solution)/shard_map/pallas_call | solution.py:303
  128.9 2.3 %collective-permute-done.11 = bf16[24,2048]{1,0:T(8,128)(2,1)} collective-permute-done((bf16[24,2048]{1,0:T(8,128)(2,1)}, bf16[24,2048]{1,0:T(8,128)(2,1)}, u32[]{:S(2)}, u32[]{:S(2)}) %collective-permute-start.11) | collective-permute-done | bytes 98336 | tf_op jit(solution)/shard_map/ppermute | solution.py:134
  132.1 7.3 %collective-permute-start.12 = (bf16[24,2048]{1,0:T(8,128)(2,1)S(1)}, bf16[24,2048]{1,0:T(8,128)(2,1)S(1)}, u32[]{:S(2)}, u32[]{:S(2)}) collective-permute-start(bf16[24,2048]{1,0:T(8,128)(2,1)S(1)} %fusion.8), channel_id=1, source_target_pairs={{0,3},{1,4},{2,5},{3,6},{4,7},{5,8},{6,9},{7,10},{8,11},{9,12},{10... | collective-permute-start | bytes 294920 | tf_op jit(solution)/shard_map/ppermute | solution.py:134
  140.4 1.9 %collective-permute-start.13 = (bf16[24,2048]{1,0:T(8,128)(2,1)S(1)}, bf16[24,2048]{1,0:T(8,128)(2,1)S(1)}, u32[]{:S(2)}, u32[]{:S(2)}) collective-permute-start(bf16[24,2048]{1,0:T(8,128)(2,1)S(1)} %fusion.9), channel_id=1, source_target_pairs={{0,29},{1,30},{2,31},{3,0},{4,1},{5,2},{6,3},{7,4},{8,5},{9,6},{10... | collective-permute-start | bytes 294920 | tf_op jit(solution)/shard_map/ppermute | solution.py:134
  142.3 5.9 %shard_map.90 = bf16[320,768]{1,0:T(8,128)(2,1)} custom-call(bf16[256,1280]{1,0:T(8,128)(2,1)} %bitcast.6.refs_1_.refs_2_.refs_0_, bf16[256,1280]{1,0:T(8,128)(2,1)} %bitcast.6.refs_1_.refs_2_.refs_0_, bf16[768,2048]{1,0:T(8,128)(2,1)S(1)} %bitcast.15, bf16[256,1280]{1,0:T(8,128)(2,1)} %bitcast.8.refs_1_.refs_2_.refs_3_.refs_4_, ...), custom_call_target="tpu_custom_call" | custom-call | flops 2013265920 | bytes 6000000 | tf_op jit(solution)/shard_map/pallas_call | solution.py:290
  148.2 5.0 %collective-permute-done.13 = bf16[24,2048]{1,0:T(8,128)(2,1)S(1)} collective-permute-done((bf16[24,2048]{1,0:T(8,128)(2,1)S(1)}, bf16[24,2048]{1,0:T(8,128)(2,1)S(1)}, u32[]{:S(2)}, u32[]{:S(2)}) %collective-permute-start.13) | collective-permute-done | bytes 98336 | tf_op jit(solution)/shard_map/ppermute | solution.py:134
  (67 shorter events, 18.7 us)
Async XLA Ops:
  0.6 1.0 copy-start.8
  3.0 13.5 %copy-start = (bf16[1,768,2048]{2,1,0:T(8,128)(2,1)S(1)}, bf16[1,768,2048]{2,1,0:T(8,128)(2,1)}, u32[]{:S(2)}) copy-start(bf16[1,768,2048]{2,1,0:T(8,128)(2,1)} %param.9) | copy-start | bytes 9437188
  5.6 19.1 %all-to-all-start = ((bf16[32,8,1280]{2,1,0:T(8,128)(2,1)}), bf16[32,8,1280]{2,1,0:T(8,128)(2,1)}, u32[]{:S(2)}, u32[]{:S(2)}) async-start(bf16[32,8,1280]{2,1,0:T(8,128)(2,1)} %bitcast.19), calls=%async_computation | async-start | bytes 1310720 | tf_op jit(solution)/shard_map/all_to_all | solution.py:222
  13.3 1.0 copy-start.10
  14.3 2.2 %copy-start.11 = (bf16[320,768]{1,0:T(8,128)(2,1)S(1)}, bf16[320,768]{1,0:T(8,128)(2,1)}, u32[]{:S(2)}) copy-start(bf16[320,768]{1,0:T(8,128)(2,1)} %hidden_ref.3) | copy-start | bytes 1474564
  19.7 1.1 copy-start.1
  24.7 26.1 %all-to-all-start.1 = ((bf16[32,8,1280]{2,1,0:T(8,128)(2,1)}), bf16[32,8,1280]{2,1,0:T(8,128)(2,1)}, u32[]{:S(2)}, u32[]{:S(2)}) async-start(bf16[32,8,1280]{2,1,0:T(8,128)(2,1)} %bitcast.18), calls=%async_computation.1 | async-start | bytes 1310720 | tf_op jit(solution)/shard_map/all_to_all | solution.py:222
  30.3 1.1 copy-start.17
  36.0 1.0 copy-start.4
  37.0 31.3 %collective-permute-start = (bf16[264,1024]{1,0:T(8,128)(2,1)}, bf16[264,1024]{1,0:T(8,128)(2,1)}, u32[]{:S(2)}, u32[]{:S(2)}) collective-permute-start(bf16[264,1024]{1,0:T(8,128)(2,1)} %get-tuple-element.33), channel_id=1, source_target_pairs={{0,31},{1,0},{2,1},{3,2},{4,3},{5,4},{6,5},{7,6},{8,7},{9,8},{10,9... | collective-permute-start | bytes 1622024 | tf_op jit(solution)/shard_map/ppermute | solution.py:134
  48.8 19.5 %collective-permute-start.1 = (bf16[240,1024]{1,0:T(8,128)(2,1)}, bf16[240,1024]{1,0:T(8,128)(2,1)}, u32[]{:S(2)}, u32[]{:S(2)}) collective-permute-start(bf16[240,1024]{1,0:T(8,128)(2,1)} %get-tuple-element.34), channel_id=1, source_target_pairs={{0,1},{1,2},{2,3},{3,4},{4,5},{5,6},{6,7},{7,8},{8,9},{9,10},{10,1... | collective-permute-start | bytes 1474568 | tf_op jit(solution)/shard_map/ppermute | solution.py:134
  50.8 1.1 copy-start.18
  57.5 21.3 %collective-permute-start.2 = (bf16[264,1024]{1,0:T(8,128)(2,1)}, bf16[264,1024]{1,0:T(8,128)(2,1)}, u32[]{:S(2)}, u32[]{:S(2)}) collective-permute-start(bf16[264,1024]{1,0:T(8,128)(2,1)} %get-tuple-element.40), channel_id=1, source_target_pairs={{0,31},{1,0},{2,1},{3,2},{4,3},{5,4},{6,5},{7,6},{8,7},{9,8},{10,9... | collective-permute-start | bytes 1622024 | tf_op jit(solution)/shard_map/ppermute | solution.py:134
  66.4 12.4 %collective-permute-start.4 = (bf16[240,1024]{1,0:T(8,128)(2,1)}, bf16[240,1024]{1,0:T(8,128)(2,1)}, u32[]{:S(2)}, u32[]{:S(2)}) collective-permute-start(bf16[240,1024]{1,0:T(8,128)(2,1)} %get-tuple-element.42), channel_id=1, source_target_pairs={{0,1},{1,2},{2,3},{3,4},{4,5},{5,6},{6,7},{7,8},{8,9},{9,10},{10,1... | collective-permute-start | bytes 1474568 | tf_op jit(solution)/shard_map/ppermute | solution.py:134
  68.3 56.3 %all-to-all-start.2 = ((bf16[32,8,2560]{2,1,0:T(8,128)(2,1)}), bf16[32,8,2560]{2,1,0:T(8,128)(2,1)}, u32[]{:S(2)}, u32[]{:S(2)}) async-start(bf16[32,8,2560]{2,1,0:T(8,128)(2,1)} %bitcast.17), calls=%async_computation.2 | async-start | bytes 2621440 | tf_op jit(solution)/shard_map/all_to_all | solution.py:222
  75.9 1.6 %copy-start.5 = (f32[264,1024]{1,0:T(8,128)S(1)}, f32[264,1024]{1,0:T(8,128)}, u32[]{:S(2)}) copy-start(f32[264,1024]{1,0:T(8,128)} %copy-done.4) | copy-start | bytes 3244036
  77.5 1.5 copy-start.3
  80.1 10.7 %collective-permute-start.3 = (bf16[24,2048]{1,0:T(8,128)(2,1)S(1)}, bf16[24,2048]{1,0:T(8,128)(2,1)S(1)}, u32[]{:S(2)}, u32[]{:S(2)}) collective-permute-start(bf16[24,2048]{1,0:T(8,128)(2,1)S(1)} %pad_maximum_fusion), channel_id=1, source_target_pairs={{0,3},{1,4},{2,5},{3,6},{4,7},{5,8},{6,9},{7,10},{8,11},{9,12},{10... | collective-permute-start | bytes 294920 | tf_op jit(solution)/shard_map/ppermute | solution.py:134
  82.0 13.0 %collective-permute-start.8 = (bf16[24,2048]{1,0:T(8,128)(2,1)S(1)}, bf16[24,2048]{1,0:T(8,128)(2,1)S(1)}, u32[]{:S(2)}, u32[]{:S(2)}) collective-permute-start(bf16[24,2048]{1,0:T(8,128)(2,1)S(1)} %pad_maximum_fusion.1), channel_id=1, source_target_pairs={{0,29},{1,30},{2,31},{3,0},{4,1},{5,2},{6,3},{7,4},{8,5},{9,6},{10... | collective-permute-start | bytes 294920 | tf_op jit(solution)/shard_map/ppermute | solution.py:134
  90.8 33.8 %copy-start.13 = (s32[128,2]{0,1:T(2,128)S(1)}, s32[128,2]{0,1:T(2,128)}, u32[]{:S(2)}) copy-start(s32[128,2]{0,1:T(2,128)} %param.6) | copy-start | bytes 3076
  90.8 33.8 %copy-start.15 = (f32[128,2]{0,1:T(2,128)S(1)}, f32[128,2]{0,1:T(2,128)}, u32[]{:S(2)}) copy-start(f32[128,2]{0,1:T(2,128)} %param.7) | copy-start | bytes 3076
  90.9 11.7 %collective-permute-start.5 = (bf16[24,2048]{1,0:T(8,128)(2,1)S(1)}, bf16[24,2048]{1,0:T(8,128)(2,1)S(1)}, u32[]{:S(2)}, u32[]{:S(2)}) collective-permute-start(bf16[24,2048]{1,0:T(8,128)(2,1)S(1)} %fusion), channel_id=1, source_target_pairs={{0,3},{1,4},{2,5},{3,6},{4,7},{5,8},{6,9},{7,10},{8,11},{9,12},{10... | collective-permute-start | bytes 294920 | tf_op jit(solution)/shard_map/ppermute | solution.py:134
  95.1 10.6 %collective-permute-start.9 = (bf16[24,2048]{1,0:T(8,128)(2,1)S(1)}, bf16[24,2048]{1,0:T(8,128)(2,1)S(1)}, u32[]{:S(2)}, u32[]{:S(2)}) collective-permute-start(bf16[24,2048]{1,0:T(8,128)(2,1)S(1)} %fusion.3), channel_id=1, source_target_pairs={{0,29},{1,30},{2,31},{3,0},{4,1},{5,2},{6,3},{7,4},{8,5},{9,6},{10... | collective-permute-start | bytes 294920 | tf_op jit(solution)/shard_map/ppermute | solution.py:134
  102.6 9.7 %collective-permute-start.6 = (bf16[24,2048]{1,0:T(8,128)(2,1)S(1)}, bf16[24,2048]{1,0:T(8,128)(2,1)S(1)}, u32[]{:S(2)}, u32[]{:S(2)}) collective-permute-start(bf16[24,2048]{1,0:T(8,128)(2,1)S(1)} %fusion.1), channel_id=1, source_target_pairs={{0,3},{1,4},{2,5},{3,6},{4,7},{5,8},{6,9},{7,10},{8,11},{9,12},{10... | collective-permute-start | bytes 294920 | tf_op jit(solution)/shard_map/ppermute | solution.py:134
  105.7 13.1 %collective-permute-start.10 = (bf16[24,2048]{1,0:T(8,128)(2,1)S(1)}, bf16[24,2048]{1,0:T(8,128)(2,1)S(1)}, u32[]{:S(2)}, u32[]{:S(2)}) collective-permute-start(bf16[24,2048]{1,0:T(8,128)(2,1)S(1)} %fusion.4), channel_id=1, source_target_pairs={{0,29},{1,30},{2,31},{3,0},{4,1},{5,2},{6,3},{7,4},{8,5},{9,6},{10... | collective-permute-start | bytes 294920 | tf_op jit(solution)/shard_map/ppermute | solution.py:134
  113.0 15.9 %collective-permute-start.7 = (bf16[24,2048]{1,0:T(8,128)(2,1)}, bf16[24,2048]{1,0:T(8,128)(2,1)}, u32[]{:S(2)}, u32[]{:S(2)}) collective-permute-start(bf16[24,2048]{1,0:T(8,128)(2,1)} %fusion.2), channel_id=1, source_target_pairs={{0,3},{1,4},{2,5},{3,6},{4,7},{5,8},{6,9},{7,10},{8,11},{9,12},{10... | collective-permute-start | bytes 294920 | tf_op jit(solution)/shard_map/ppermute | solution.py:134
  119.5 11.7 %collective-permute-start.11 = (bf16[24,2048]{1,0:T(8,128)(2,1)}, bf16[24,2048]{1,0:T(8,128)(2,1)}, u32[]{:S(2)}, u32[]{:S(2)}) collective-permute-start(bf16[24,2048]{1,0:T(8,128)(2,1)} %fusion.5), channel_id=1, source_target_pairs={{0,29},{1,30},{2,31},{3,0},{4,1},{5,2},{6,3},{7,4},{8,5},{9,6},{10... | collective-permute-start | bytes 294920 | tf_op jit(solution)/shard_map/ppermute | solution.py:134
  124.7 1.0 copy-start.9
  125.7 5.4 %copy-start.20 = (f32[24,1024]{1,0:T(8,128)S(1)}, f32[24,1024]{1,0:T(8,128)}, u32[]{:S(2)}) copy-start(f32[24,1024]{1,0:T(8,128)} %get-tuple-element.56) | copy-start | bytes 294916
  125.7 13.7 %copy-start.19 = (f32[24,1024]{1,0:T(8,128)S(1)}, f32[24,1024]{1,0:T(8,128)}, u32[]{:S(2)}) copy-start(f32[24,1024]{1,0:T(8,128)} %get-tuple-element.57) | copy-start | bytes 294916
  132.1 16.1 %collective-permute-start.12 = (bf16[24,2048]{1,0:T(8,128)(2,1)S(1)}, bf16[24,2048]{1,0:T(8,128)(2,1)S(1)}, u32[]{:S(2)}, u32[]{:S(2)}) collective-permute-start(bf16[24,2048]{1,0:T(8,128)(2,1)S(1)} %fusion.8), channel_id=1, source_target_pairs={{0,3},{1,4},{2,5},{3,6},{4,7},{5,8},{6,9},{7,10},{8,11},{9,12},{10... | collective-permute-start | bytes 294920 | tf_op jit(solution)/shard_map/ppermute | solution.py:134
  140.4 12.9 %collective-permute-start.13 = (bf16[24,2048]{1,0:T(8,128)(2,1)S(1)}, bf16[24,2048]{1,0:T(8,128)(2,1)S(1)}, u32[]{:S(2)}, u32[]{:S(2)}) collective-permute-start(bf16[24,2048]{1,0:T(8,128)(2,1)S(1)} %fusion.9), channel_id=1, source_target_pairs={{0,29},{1,30},{2,31},{3,0},{4,1},{5,2},{6,3},{7,4},{8,5},{9,6},{10... | collective-permute-start | bytes 294920 | tf_op jit(solution)/shard_map/ppermute | solution.py:134
  (6 other events, 4.9 us)

commit v5 on v4

--- a/solution.py
+++ b/solution.py
@@ -10,7 +10,7 @@
 QUARTERS = 4
 HALVES = 2
 CHUNK = 24
-VMEM_BYTES = 48 * 1024 * 1024
+VMEM_BYTES = 20 * 1024 * 1024
 
 
 def iota(shape, dim):
@@ -110,15 +110,22 @@
 
 
 def turn_kernel(place_ref, hidden_ref, turned_ref):
-    inner = hidden_ref.shape[1]
+    rows, inner = hidden_ref.shape
     source = chunk_order(place_ref[0], place_ref[1], iota((1, inner), 1))
     select = onehot(iota((inner, inner), 0) == source)
-    turned_ref[...] = dot(select, hidden_ref[...], 0, 1).astype(BF16)
-
-
-def partial_kernel(scale, turned_ref, low_ref, left_ref, down_ref, up_ref, own_ref):
-    rows = natural_rows(low_ref[...], left_ref[...], pl.program_id(0), turned_ref.shape[1])
-    product = dot(turned_ref[...], rows) * scale
+    turned = dot(select, hidden_ref[...], 0, 1).astype(BF16)
+    row, column = iota((rows, 256), 0), iota((rows, 256), 1)
+    peer, place = column >> 3, column & 7
+    turned_ref[:, 0:256] = dot(turned, onehot(row == peer * 10 + place)).astype(BF16)
+    left = dot(turned, onehot(row == peer * 10 + 8 + (place >> 2)))
+    for q in range(QUARTERS):
+        mine = (iota((inner, 256), 1) & 3) == q
+        turned_ref[:, (q + 1) * 256 : (q + 2) * 256] = jnp.where(mine, left, 0.0).astype(BF16)
+
+
+def partial_kernel(scale, turned_ref, turned_left_ref, low_ref, left_ref, down_ref, up_ref, own_ref):
+    product = dot(turned_ref[...], low_ref[...]) + dot(turned_left_ref[...], left_ref[...])
+    product = product * scale
     down_ref[...] = product[: 11 * CHUNK].astype(BF16)
     up_ref[...] = product[11 * CHUNK : 21 * CHUNK].astype(BF16)
     own_ref[...] = product[21 * CHUNK :]
@@ -205,11 +212,11 @@
         )
 
 
-def call(kernel, out_shape, flops, bytes_accessed, **options):
+def call(kernel, out_shape, flops, bytes_accessed, vmem=VMEM_BYTES, **options):
     return pl.pallas_call(
         kernel,
         out_shape=out_shape,
-        compiler_params=pltpu.CompilerParams(vmem_limit_bytes=VMEM_BYTES),
+        compiler_params=pltpu.CompilerParams(vmem_limit_bytes=vmem),
         cost_estimate=pl.CostEstimate(
             flops=flops, bytes_accessed=bytes_accessed, transcendentals=0
         ),
@@ -239,14 +246,18 @@
     half_packed = jax.ShapeDtypeStruct((256, half + narrow), BF16)
     block = lambda height, at: pl.BlockSpec((height, narrow), lambda q: (0, at(q)))
     half_low, half_left = block(256, lambda q: q), block(256, lambda q: QUARTERS)
-    outgoing = call(send_kernel, (half_packed,) * HALVES, 4 * 256 * tokens * features, 2 * 10**6)(
-        ids, probs, cotangent
-    )
+    outgoing = call(
+        send_kernel,
+        (half_packed,) * HALVES,
+        4 * 256 * tokens * features,
+        2 * 10**6,
+        60 * 1024 * 1024,
+    )(ids, probs, cotangent)
     sign = 1 - 2 * (lax.axis_index("ep") & 1)
     place = jnp.stack([lax.axis_index("dp"), sign]).astype(jnp.int32)
     turned = call(
         turn_kernel,
-        jax.ShapeDtypeStruct((inner, rows), BF16),
+        jax.ShapeDtypeStruct((inner, 256 * (QUARTERS + 1)), BF16),
         2 * inner * inner * rows,
         10**6,
         in_specs=[pl.BlockSpec(memory_space=pltpu.SMEM), pl.BlockSpec(memory_space=pltpu.VMEM)],
@@ -273,9 +284,14 @@
             product,
             4 * 10**6,
             grid=(QUARTERS,),
-            in_specs=[whole((inner, rows)), half_low, half_left],
+            in_specs=[
+                pl.BlockSpec((inner, 256), lambda q: (0, 0)),
+                pl.BlockSpec((inner, 256), lambda q: (0, q + 1)),
+                half_low,
+                half_left,
+            ],
             out_specs=tuple(block(n * CHUNK, lambda q: q) for n in (11, 10, 11)),
-        )(turned, arrived, arrived)
+        )(turned, turned, arrived, arrived)
 
     first = exchange(outgoing[0], peers)
     turned, expert_rows, first = lax.optimization_barrier((turned, expert_rows, first))

time: 155 us -> 147 us (0.948)
  the two profiles are of different devices: /device:TPU:40 before, /device:TPU:34 now
where the time goes in v5:
time: 147 us; the launch traced here: 146 us
  starting transfers between devices  94.9 us (65%)
  Pallas kernels  19.7 us (13%)
  waiting for transfers between devices  14.2 us (10%)
  other arithmetic  9.27 us (6%)
  local copies, waits for them, and re-layouts  7.17 us (5%)
    ppermute x14, starting transfers between devices, shift(): return lax.ppermute(block, ('ep', 'dp'), pairs)  74.1 us
    all_to_all x3, starting transfers between devices, exchange(): lax.all_to_all(blocks, 'ep', split_axis=0, concat_axis=0, tiled=True)  20.8 us
    ppermute x14, waiting for transfers between devices, shift(): return lax.ppermute(block, ('ep', 'dp'), pairs)  11.5 us
    unnamed x26, local copies, waits for them, and re-layouts  7.17 us
    pallas_call x1, Pallas kernels, shards(): call(hidden_grad_kernel, jax.ShapeDtypeStruct((rows, inner), BF16), 2 * p...  5.08 us
    pallas_call x2, Pallas kernels, partial(): call(lambda *refs: partial_kernel((groups * rows) ** (-0.5), *refs), (jax...  4.98 us
    pallas_call x1, Pallas kernels, shards(): call(expert_kernel, packed, 2 * product, 6 * 10 ** 6, grid=(QUARTERS,), i...  3.19 us
    add x2, other arithmetic, term(): total += from_below[(k - 1) * CHUNK:k * CHUNK].astype(F32)  2.96 us
  transfers between devices with their start and end apart: 17, of which 9 were waited for; matrix products, arithmetic and copies ran while one was open for 5% of the time, Pallas kernels for 12%

profile of v5, /device:TPU:34, one launch (start us, length us, event | category | flops | bytes accessed | tf_op | source)
XLA Modules:
  0.0 146.4 jit_solution(10411869752394160374)
XLA Ops:
  0.6 2.9 %shard_map.86 = (bf16[256,1280]{1,0:T(8,128)(2,1)}, bf16[256,1280]{1,0:T(8,128)(2,1)}) custom-call(s32[2,128]{1,0:T(2,128)} %bitcast.27, f32[2,128]{1,0:T(2,128)} %bitcast.29, bf16[128,2048]{1,0:T(8,128)(2,1)} %cot_ref.3), custom_call_target="tpu_custom_call" | custom-call | flops 268435456 | bytes 2000000 | tf_op jit(solution)/shard_map/pallas_call | solution.py:249
  3.5 7.6 %all-to-all-start = ((bf16[32,8,1280]{2,1,0:T(8,128)(2,1)}), bf16[32,8,1280]{2,1,0:T(8,128)(2,1)S(1)}, u32[]{:S(2)}, u32[]{:S(2)}) async-start(bf16[32,8,1280]{2,1,0:T(8,128)(2,1)} %bitcast.32), calls=%async_computation | async-start | bytes 1310720 | tf_op jit(solution)/shard_map/all_to_all | solution.py:229
  11.2 1.8 %shard_map.84.refs_0_.refs_1_ = bf16[768,1280]{1,0:T(8,128)(2,1)S(1)} custom-call(s32[2]{0:T(128)S(1)} %pad_add_fusion.place_ref, bf16[320,768]{1,0:T(8,128)(2,1)S(1)} %copy-done.7), custom_call_target="tpu_custom_call" | custom-call | flops 377487360 | bytes 1000000 | tf_op jit(solution)/shard_map/pallas_call | solution.py:258
  13.0 1.9 %copy-done = bf16[1,768,2048]{2,1,0:T(8,128)(2,1)S(1)} copy-done((bf16[1,768,2048]{2,1,0:T(8,128)(2,1)S(1)}, bf16[1,768,2048]{2,1,0:T(8,128)(2,1)}, u32[]{:S(2)}) %copy-start) | copy-done | bytes 3145752
  14.9 3.2 %shard_map.85 = bf16[256,2560]{1,0:T(8,128)(2,1)S(1)} custom-call(bf16[320,768]{1,0:T(8,128)(2,1)S(1)} %copy-done.7, bf16[768,2048]{1,0:T(8,128)(2,1)S(1)} %bitcast.22), custom_call_target="tpu_custom_call" | custom-call | flops 2013265920 | bytes 6000000 | tf_op jit(solution)/shard_map/pallas_call | solution.py:265
  19.2 2.8 %all-to-all-done = bf16[32,8,1280]{2,1,0:T(8,128)(2,1)S(1)} async-done(((bf16[32,8,1280]{2,1,0:T(8,128)(2,1)}), bf16[32,8,1280]{2,1,0:T(8,128)(2,1)S(1)}, u32[]{:S(2)}, u32[]{:S(2)}) %all-to-all-start) | async-done | bytes 655392 | tf_op jit(solution)/shard_map/all_to_all | solution.py:229
  22.0 5.8 %all-to-all-start.1 = ((bf16[32,8,1280]{2,1,0:T(8,128)(2,1)}), bf16[32,8,1280]{2,1,0:T(8,128)(2,1)S(1)}, u32[]{:S(2)}, u32[]{:S(2)}) async-start(bf16[32,8,1280]{2,1,0:T(8,128)(2,1)} %bitcast.31), calls=%async_computation.1 | async-start | bytes 1310720 | tf_op jit(solution)/shard_map/all_to_all | solution.py:229
  27.8 2.5 %shard_map.87 = (bf16[264,1024]{1,0:T(8,128)(2,1)}, bf16[240,1024]{1,0:T(8,128)(2,1)}, f32[264,1024]{1,0:T(8,128)S(1)}) custom-call(bf16[768,1280]{1,0:T(8,128)(2,1)S(1)} %shard_map.84.refs_0_.refs_1_, bf16[768,1280]{1,0:T(8,128)(2,1)S(1)} %shard_map.84.refs_0_.refs_1_, bf16[256,1280]{1,0:T(8,128)(2,1)S(1)} %bitcast.14, bf16[256,1280]{1,0:T(8,128)(2,1)S(1)} %bitcast.15), custom_call_target="tpu_custom_call" | custom-call | flops 1006632960 | bytes 4000000 | tf_op jit(solution)/shard_map/pallas_call | solution.py:277
  31.3 11.2 %collective-permute-start = (bf16[264,1024]{1,0:T(8,128)(2,1)}, bf16[264,1024]{1,0:T(8,128)(2,1)}, u32[]{:S(2)}, u32[]{:S(2)}) collective-permute-start(bf16[264,1024]{1,0:T(8,128)(2,1)} %get-tuple-element.33), channel_id=1, source_target_pairs={{0,31},{1,0},{2,1},{3,2},{4,3},{5,4},{6,5},{7,6},{8,7},{9,8},{10,9... | collective-permute-start | bytes 1622024 | tf_op jit(solution)/shard_map/ppermute | solution.py:141
  42.5 1.9 %collective-permute-start.1 = (bf16[240,1024]{1,0:T(8,128)(2,1)}, bf16[240,1024]{1,0:T(8,128)(2,1)}, u32[]{:S(2)}, u32[]{:S(2)}) collective-permute-start(bf16[240,1024]{1,0:T(8,128)(2,1)} %get-tuple-element.34), channel_id=1, source_target_pairs={{0,1},{1,2},{2,3},{3,4},{4,5},{5,6},{6,7},{7,8},{8,9},{9,10},{10,1... | collective-permute-start | bytes 1474568 | tf_op jit(solution)/shard_map/ppermute | solution.py:141
  44.4 2.5 %shard_map.88 = (bf16[264,1024]{1,0:T(8,128)(2,1)}, bf16[240,1024]{1,0:T(8,128)(2,1)}, f32[264,1024]{1,0:T(8,128)S(1)}) custom-call(bf16[768,1280]{1,0:T(8,128)(2,1)S(1)} %shard_map.84.refs_0_.refs_1_, bf16[768,1280]{1,0:T(8,128)(2,1)S(1)} %shard_map.84.refs_0_.refs_1_, bf16[256,1280]{1,0:T(8,128)(2,1)S(1)} %bitcast.18, bf16[256,1280]{1,0:T(8,128)(2,1)S(1)} %bitcast.19), custom_call_target="tpu_custom_call" | custom-call | flops 1006632960 | bytes 4000000 | tf_op jit(solution)/shard_map/pallas_call | solution.py:277
  47.9 9.5 %collective-permute-start.2 = (bf16[264,1024]{1,0:T(8,128)(2,1)}, bf16[264,1024]{1,0:T(8,128)(2,1)S(1)}, u32[]{:S(2)}, u32[]{:S(2)}) collective-permute-start(bf16[264,1024]{1,0:T(8,128)(2,1)} %get-tuple-element.40), channel_id=1, source_target_pairs={{0,31},{1,0},{2,1},{3,2},{4,3},{5,4},{6,5},{7,6},{8,7},{9,8},{10,9... | collective-permute-start | bytes 1622024 | tf_op jit(solution)/shard_map/ppermute | solution.py:141
  57.4 1.9 %collective-permute-start.4 = (bf16[240,1024]{1,0:T(8,128)(2,1)}, bf16[240,1024]{1,0:T(8,128)(2,1)}, u32[]{:S(2)}, u32[]{:S(2)}) collective-permute-start(bf16[240,1024]{1,0:T(8,128)(2,1)} %get-tuple-element.42), channel_id=1, source_target_pairs={{0,1},{1,2},{2,3},{3,4},{4,5},{5,6},{6,7},{7,8},{8,9},{9,10},{10,1... | collective-permute-start | bytes 1474568 | tf_op jit(solution)/shard_map/ppermute | solution.py:141
  59.7 7.4 %all-to-all-start.2 = ((bf16[32,8,2560]{2,1,0:T(8,128)(2,1)}), bf16[32,8,2560]{2,1,0:T(8,128)(2,1)S(1)}, u32[]{:S(2)}, u32[]{:S(2)}) async-start(bf16[32,8,2560]{2,1,0:T(8,128)(2,1)} %bitcast.25), calls=%async_computation.2 | async-start | bytes 2621440 | tf_op jit(solution)/shard_map/all_to_all | solution.py:229
  67.1 1.3 add_convert_fusion.1
  71.2 1.9 %collective-permute-start.3 = (bf16[24,2048]{1,0:T(8,128)(2,1)S(1)}, bf16[24,2048]{1,0:T(8,128)(2,1)S(1)}, u32[]{:S(2)}, u32[]{:S(2)}) collective-permute-start(bf16[24,2048]{1,0:T(8,128)(2,1)S(1)} %pad_maximum_fusion), channel_id=1, source_target_pairs={{0,3},{1,4},{2,5},{3,6},{4,7},{5,8},{6,9},{7,10},{8,11},{9,12},{10... | collective-permute-start | bytes 294920 | tf_op jit(solution)/shard_map/ppermute | solution.py:141
  73.1 8.3 %collective-permute-start.8 = (bf16[24,2048]{1,0:T(8,128)(2,1)S(1)}, bf16[24,2048]{1,0:T(8,128)(2,1)S(1)}, u32[]{:S(2)}, u32[]{:S(2)}) collective-permute-start(bf16[24,2048]{1,0:T(8,128)(2,1)S(1)} %pad_maximum_fusion.1), channel_id=1, source_target_pairs={{0,29},{1,30},{2,31},{3,0},{4,1},{5,2},{6,3},{7,4},{8,5},{9,6},{10... | collective-permute-start | bytes 294920 | tf_op jit(solution)/shard_map/ppermute | solution.py:141
  81.4 1.7 %convert_add_fusion.2 = (f32[24,1024]{1,0:T(8,128)}, f32[24,1024]{1,0:T(8,128)}, f32[24,1024]{1,0:T(8,128)S(1)}, f32[24,1024]{1,0:T(8,128)S(1)}, f32[24,1024]{1,0:T(8,128)S(1)}, /*index=5*/f32[24,1024]{1,0:T(8,128)S(1)}) fusion(f32[264,1024]{1,0:T(8,128)S(1)} %copy-done.4, bf16[240,1024]{1,0:T(8,128)(2,1)} %collective-permute-done.4, ...), kind=kLoop, calls=%fused_computation.23 | loop fusion | flops 589824 | bytes 1769472 | tf_op jit(solution)/shard_map/add | solution.py:151
  83.1 2.1 %collective-permute-start.5 = (bf16[24,2048]{1,0:T(8,128)(2,1)S(1)}, bf16[24,2048]{1,0:T(8,128)(2,1)S(1)}, u32[]{:S(2)}, u32[]{:S(2)}) collective-permute-start(bf16[24,2048]{1,0:T(8,128)(2,1)S(1)} %fusion), channel_id=1, source_target_pairs={{0,3},{1,4},{2,5},{3,6},{4,7},{5,8},{6,9},{7,10},{8,11},{9,12},{10... | collective-permute-start | bytes 294920 | tf_op jit(solution)/shard_map/ppermute | solution.py:141
  86.3 7.5 %collective-permute-start.9 = (bf16[24,2048]{1,0:T(8,128)(2,1)S(1)}, bf16[24,2048]{1,0:T(8,128)(2,1)S(1)}, u32[]{:S(2)}, u32[]{:S(2)}) collective-permute-start(bf16[24,2048]{1,0:T(8,128)(2,1)S(1)} %fusion.3), channel_id=1, source_target_pairs={{0,29},{1,30},{2,31},{3,0},{4,1},{5,2},{6,3},{7,4},{8,5},{9,6},{10... | collective-permute-start | bytes 294920 | tf_op jit(solution)/shard_map/ppermute | solution.py:141
  93.8 1.9 %collective-permute-start.6 = (bf16[24,2048]{1,0:T(8,128)(2,1)S(1)}, bf16[24,2048]{1,0:T(8,128)(2,1)S(1)}, u32[]{:S(2)}, u32[]{:S(2)}) collective-permute-start(bf16[24,2048]{1,0:T(8,128)(2,1)S(1)} %fusion.1), channel_id=1, source_target_pairs={{0,3},{1,4},{2,5},{3,6},{4,7},{5,8},{6,9},{7,10},{8,11},{9,12},{10... | collective-permute-start | bytes 294920 | tf_op jit(solution)/shard_map/ppermute | solution.py:141
  97.0 6.7 %collective-permute-start.10 = (bf16[24,2048]{1,0:T(8,128)(2,1)S(1)}, bf16[24,2048]{1,0:T(8,128)(2,1)S(1)}, u32[]{:S(2)}, u32[]{:S(2)}) collective-permute-start(bf16[24,2048]{1,0:T(8,128)(2,1)S(1)} %fusion.4), channel_id=1, source_target_pairs={{0,29},{1,30},{2,31},{3,0},{4,1},{5,2},{6,3},{7,4},{8,5},{9,6},{10... | collective-permute-start | bytes 294920 | tf_op jit(solution)/shard_map/ppermute | solution.py:141
  103.7 2.7 %collective-permute-done.6 = bf16[24,2048]{1,0:T(8,128)(2,1)S(1)} collective-permute-done((bf16[24,2048]{1,0:T(8,128)(2,1)S(1)}, bf16[24,2048]{1,0:T(8,128)(2,1)S(1)}, u32[]{:S(2)}, u32[]{:S(2)}) %collective-permute-start.6) | collective-permute-done | bytes 98336 | tf_op jit(solution)/shard_map/ppermute | solution.py:141
  107.1 1.9 %collective-permute-start.7 = (bf16[24,2048]{1,0:T(8,128)(2,1)}, bf16[24,2048]{1,0:T(8,128)(2,1)}, u32[]{:S(2)}, u32[]{:S(2)}) collective-permute-start(bf16[24,2048]{1,0:T(8,128)(2,1)} %fusion.2), channel_id=1, source_target_pairs={{0,3},{1,4},{2,5},{3,6},{4,7},{5,8},{6,9},{7,10},{8,11},{9,12},{10... | collective-permute-start | bytes 294920 | tf_op jit(solution)/shard_map/ppermute | solution.py:141
  109.6 6.9 %collective-permute-start.11 = (bf16[24,2048]{1,0:T(8,128)(2,1)}, bf16[24,2048]{1,0:T(8,128)(2,1)}, u32[]{:S(2)}, u32[]{:S(2)}) collective-permute-start(bf16[24,2048]{1,0:T(8,128)(2,1)} %fusion.5), channel_id=1, source_target_pairs={{0,29},{1,30},{2,31},{3,0},{4,1},{5,2},{6,3},{7,4},{8,5},{9,6},{10... | collective-permute-start | bytes 294920 | tf_op jit(solution)/shard_map/ppermute | solution.py:141
  116.6 1.8 %shard_map.89 = (bf16[128,2048]{1,0:T(8,128)(2,1)}, f32[2,128]{1,0:T(2,128)}) custom-call(s32[2,128]{1,0:T(2,128)S(1)} %bitcast.28, f32[2,128]{1,0:T(2,128)S(1)} %bitcast.30, bf16[128,2048]{1,0:T(8,128)(2,1)S(1)} %copy-done.8, bf16[256,2560]{1,0:T(8,128)(2,1)S(1)} %bitcast.26), custom_call_target="tpu_custom_call" | custom-call | flops 536870912 | bytes 3000000 | tf_op jit(solution)/shard_map/pallas_call | solution.py:319
  119.1 3.6 %collective-permute-done.11 = bf16[24,2048]{1,0:T(8,128)(2,1)} collective-permute-done((bf16[24,2048]{1,0:T(8,128)(2,1)}, bf16[24,2048]{1,0:T(8,128)(2,1)}, u32[]{:S(2)}, u32[]{:S(2)}) %collective-permute-start.11) | collective-permute-done | bytes 98336 | tf_op jit(solution)/shard_map/ppermute | solution.py:141
  123.7 10.6 %collective-permute-start.12 = (bf16[24,2048]{1,0:T(8,128)(2,1)S(1)}, bf16[24,2048]{1,0:T(8,128)(2,1)S(1)}, u32[]{:S(2)}, u32[]{:S(2)}) collective-permute-start(bf16[24,2048]{1,0:T(8,128)(2,1)S(1)} %fusion.8), channel_id=1, source_target_pairs={{0,3},{1,4},{2,5},{3,6},{4,7},{5,8},{6,9},{7,10},{8,11},{9,12},{10... | collective-permute-start | bytes 294920 | tf_op jit(solution)/shard_map/ppermute | solution.py:141
  135.2 1.9 %collective-permute-start.13 = (bf16[24,2048]{1,0:T(8,128)(2,1)S(1)}, bf16[24,2048]{1,0:T(8,128)(2,1)S(1)}, u32[]{:S(2)}, u32[]{:S(2)}) collective-permute-start(bf16[24,2048]{1,0:T(8,128)(2,1)S(1)} %fusion.9), channel_id=1, source_target_pairs={{0,29},{1,30},{2,31},{3,0},{4,1},{5,2},{6,3},{7,4},{8,5},{9,6},{10... | collective-permute-start | bytes 294920 | tf_op jit(solution)/shard_map/ppermute | solution.py:141
  137.1 1.9 %copy-done.1 = bf16[1,768,2048]{2,1,0:T(8,128)(2,1)S(1)} copy-done((bf16[1,768,2048]{2,1,0:T(8,128)(2,1)S(1)}, bf16[1,768,2048]{2,1,0:T(8,128)(2,1)}, u32[]{:S(2)}) %copy-start.1) | copy-done | bytes 3145752
  139.0 5.1 %shard_map.90 = bf16[320,768]{1,0:T(8,128)(2,1)} custom-call(bf16[256,1280]{1,0:T(8,128)(2,1)S(1)} %bitcast.16, bf16[256,1280]{1,0:T(8,128)(2,1)S(1)} %bitcast.17, bf16[768,2048]{1,0:T(8,128)(2,1)S(1)} %bitcast.23, bf16[256,1280]{1,0:T(8,128)(2,1)S(1)} %bitcast.20, bf16[256,1280]{1,0:T(8,128)(2,1)S(1)} %bitcast.21, bf16[768,2048]{1,0:T(8,128)(2,1)S(1)} %bitcast.24), custom_call_target="tpu_custom_call" | custom-call | flops 2013265920 | bytes 6000000 | tf_op jit(solution)/shard_map/pallas_call | solution.py:306
  144.1 1.6 %collective-permute-done.13 = bf16[24,2048]{1,0:T(8,128)(2,1)S(1)} collective-permute-done((bf16[24,2048]{1,0:T(8,128)(2,1)S(1)}, bf16[24,2048]{1,0:T(8,128)(2,1)S(1)}, u32[]{:S(2)}, u32[]{:S(2)}) %collective-permute-start.13) | collective-permute-done | bytes 98336 | tf_op jit(solution)/shard_map/ppermute | solution.py:141
  (51 shorter events, 13.2 us)
Async XLA Ops:
  0.6 10.6 %copy-start.7 = (bf16[320,768]{1,0:T(8,128)(2,1)S(1)}, bf16[320,768]{1,0:T(8,128)(2,1)}, u32[]{:S(2)}) copy-start(bf16[320,768]{1,0:T(8,128)(2,1)} %hidden_ref.3) | copy-start | bytes 1474564
  3.5 18.5 %all-to-all-start = ((bf16[32,8,1280]{2,1,0:T(8,128)(2,1)}), bf16[32,8,1280]{2,1,0:T(8,128)(2,1)S(1)}, u32[]{:S(2)}, u32[]{:S(2)}) async-start(bf16[32,8,1280]{2,1,0:T(8,128)(2,1)} %bitcast.32), calls=%async_computation | async-start | bytes 1310720 | tf_op jit(solution)/shard_map/all_to_all | solution.py:229
  13.0 1.9 %copy-start = (bf16[1,768,2048]{2,1,0:T(8,128)(2,1)S(1)}, bf16[1,768,2048]{2,1,0:T(8,128)(2,1)}, u32[]{:S(2)}) copy-start(bf16[1,768,2048]{2,1,0:T(8,128)(2,1)} %param.9) | copy-start | bytes 9437188
  18.1 1.1 copy-start.2
  22.0 22.4 %all-to-all-start.1 = ((bf16[32,8,1280]{2,1,0:T(8,128)(2,1)}), bf16[32,8,1280]{2,1,0:T(8,128)(2,1)S(1)}, u32[]{:S(2)}, u32[]{:S(2)}) async-start(bf16[32,8,1280]{2,1,0:T(8,128)(2,1)} %bitcast.31), calls=%async_computation.1 | async-start | bytes 1310720 | tf_op jit(solution)/shard_map/all_to_all | solution.py:229
  30.3 1.0 copy-start.5
  31.3 28.4 %collective-permute-start = (bf16[264,1024]{1,0:T(8,128)(2,1)}, bf16[264,1024]{1,0:T(8,128)(2,1)}, u32[]{:S(2)}, u32[]{:S(2)}) collective-permute-start(bf16[264,1024]{1,0:T(8,128)(2,1)} %get-tuple-element.33), channel_id=1, source_target_pairs={{0,31},{1,0},{2,1},{3,2},{4,3},{5,4},{6,5},{7,6},{8,7},{9,8},{10,9... | collective-permute-start | bytes 1622024 | tf_op jit(solution)/shard_map/ppermute | solution.py:141
  42.5 17.2 %collective-permute-start.1 = (bf16[240,1024]{1,0:T(8,128)(2,1)}, bf16[240,1024]{1,0:T(8,128)(2,1)}, u32[]{:S(2)}, u32[]{:S(2)}) collective-permute-start(bf16[240,1024]{1,0:T(8,128)(2,1)} %get-tuple-element.34), channel_id=1, source_target_pairs={{0,1},{1,2},{2,3},{3,4},{4,5},{5,6},{6,7},{7,8},{8,9},{9,10},{10,1... | collective-permute-start | bytes 1474568 | tf_op jit(solution)/shard_map/ppermute | solution.py:141
  46.9 1.0 copy-start.3
  47.9 22.3 %collective-permute-start.2 = (bf16[264,1024]{1,0:T(8,128)(2,1)}, bf16[264,1024]{1,0:T(8,128)(2,1)S(1)}, u32[]{:S(2)}, u32[]{:S(2)}) collective-permute-start(bf16[264,1024]{1,0:T(8,128)(2,1)} %get-tuple-element.40), channel_id=1, source_target_pairs={{0,31},{1,0},{2,1},{3,2},{4,3},{5,4},{6,5},{7,6},{8,7},{9,8},{10,9... | collective-permute-start | bytes 1622024 | tf_op jit(solution)/shard_map/ppermute | solution.py:141
  57.4 12.8 %collective-permute-start.4 = (bf16[240,1024]{1,0:T(8,128)(2,1)}, bf16[240,1024]{1,0:T(8,128)(2,1)}, u32[]{:S(2)}, u32[]{:S(2)}) collective-permute-start(bf16[240,1024]{1,0:T(8,128)(2,1)} %get-tuple-element.42), channel_id=1, source_target_pairs={{0,1},{1,2},{2,3},{3,4},{4,5},{5,6},{6,7},{7,8},{8,9},{9,10},{10,1... | collective-permute-start | bytes 1474568 | tf_op jit(solution)/shard_map/ppermute | solution.py:141
  59.7 56.9 %all-to-all-start.2 = ((bf16[32,8,2560]{2,1,0:T(8,128)(2,1)}), bf16[32,8,2560]{2,1,0:T(8,128)(2,1)S(1)}, u32[]{:S(2)}, u32[]{:S(2)}) async-start(bf16[32,8,2560]{2,1,0:T(8,128)(2,1)} %bitcast.25), calls=%async_computation.2 | async-start | bytes 2621440 | tf_op jit(solution)/shard_map/all_to_all | solution.py:229
  67.1 1.6 %copy-start.6 = (f32[264,1024]{1,0:T(8,128)S(1)}, f32[264,1024]{1,0:T(8,128)}, u32[]{:S(2)}) copy-start(f32[264,1024]{1,0:T(8,128)} %copy-done.5) | copy-start | bytes 3244036
  68.7 1.5 %copy-start.4 = (f32[264,1024]{1,0:T(8,128)S(1)}, f32[264,1024]{1,0:T(8,128)}, u32[]{:S(2)}) copy-start(f32[264,1024]{1,0:T(8,128)} %copy-done.3) | copy-start | bytes 3244036
  71.2 11.9 %collective-permute-start.3 = (bf16[24,2048]{1,0:T(8,128)(2,1)S(1)}, bf16[24,2048]{1,0:T(8,128)(2,1)S(1)}, u32[]{:S(2)}, u32[]{:S(2)}) collective-permute-start(bf16[24,2048]{1,0:T(8,128)(2,1)S(1)} %pad_maximum_fusion), channel_id=1, source_target_pairs={{0,3},{1,4},{2,5},{3,6},{4,7},{5,8},{6,9},{7,10},{8,11},{9,12},{10... | collective-permute-start | bytes 294920 | tf_op jit(solution)/shard_map/ppermute | solution.py:141
  73.1 13.2 %collective-permute-start.8 = (bf16[24,2048]{1,0:T(8,128)(2,1)S(1)}, bf16[24,2048]{1,0:T(8,128)(2,1)S(1)}, u32[]{:S(2)}, u32[]{:S(2)}) collective-permute-start(bf16[24,2048]{1,0:T(8,128)(2,1)S(1)} %pad_maximum_fusion.1), channel_id=1, source_target_pairs={{0,29},{1,30},{2,31},{3,0},{4,1},{5,2},{6,3},{7,4},{8,5},{9,6},{10... | collective-permute-start | bytes 294920 | tf_op jit(solution)/shard_map/ppermute | solution.py:141
  83.1 33.5 %copy-start.8 = (bf16[128,2048]{1,0:T(8,128)(2,1)S(1)}, bf16[128,2048]{1,0:T(8,128)(2,1)}, u32[]{:S(2)}) copy-start(bf16[128,2048]{1,0:T(8,128)(2,1)} %cot_ref.3) | copy-start | bytes 1572868
  83.1 33.5 %copy-start.9 = (s32[128,2]{0,1:T(2,128)S(1)}, s32[128,2]{0,1:T(2,128)}, u32[]{:S(2)}) copy-start(s32[128,2]{0,1:T(2,128)} %param.6) | copy-start | bytes 3076
  83.1 33.5 %copy-start.10 = (f32[128,2]{0,1:T(2,128)S(1)}, f32[128,2]{0,1:T(2,128)}, u32[]{:S(2)}) copy-start(f32[128,2]{0,1:T(2,128)} %param.7) | copy-start | bytes 3076
  83.1 10.7 %collective-permute-start.5 = (bf16[24,2048]{1,0:T(8,128)(2,1)S(1)}, bf16[24,2048]{1,0:T(8,128)(2,1)S(1)}, u32[]{:S(2)}, u32[]{:S(2)}) collective-permute-start(bf16[24,2048]{1,0:T(8,128)(2,1)S(1)} %fusion), channel_id=1, source_target_pairs={{0,3},{1,4},{2,5},{3,6},{4,7},{5,8},{6,9},{7,10},{8,11},{9,12},{10... | collective-permute-start | bytes 294920 | tf_op jit(solution)/shard_map/ppermute | solution.py:141
  86.3 10.6 %collective-permute-start.9 = (bf16[24,2048]{1,0:T(8,128)(2,1)S(1)}, bf16[24,2048]{1,0:T(8,128)(2,1)S(1)}, u32[]{:S(2)}, u32[]{:S(2)}) collective-permute-start(bf16[24,2048]{1,0:T(8,128)(2,1)S(1)} %fusion.3), channel_id=1, source_target_pairs={{0,29},{1,30},{2,31},{3,0},{4,1},{5,2},{6,3},{7,4},{8,5},{9,6},{10... | collective-permute-start | bytes 294920 | tf_op jit(solution)/shard_map/ppermute | solution.py:141
  93.8 12.6 %collective-permute-start.6 = (bf16[24,2048]{1,0:T(8,128)(2,1)S(1)}, bf16[24,2048]{1,0:T(8,128)(2,1)S(1)}, u32[]{:S(2)}, u32[]{:S(2)}) collective-permute-start(bf16[24,2048]{1,0:T(8,128)(2,1)S(1)} %fusion.1), channel_id=1, source_target_pairs={{0,3},{1,4},{2,5},{3,6},{4,7},{5,8},{6,9},{7,10},{8,11},{9,12},{10... | collective-permute-start | bytes 294920 | tf_op jit(solution)/shard_map/ppermute | solution.py:141
  97.0 12.0 %collective-permute-start.10 = (bf16[24,2048]{1,0:T(8,128)(2,1)S(1)}, bf16[24,2048]{1,0:T(8,128)(2,1)S(1)}, u32[]{:S(2)}, u32[]{:S(2)}) collective-permute-start(bf16[24,2048]{1,0:T(8,128)(2,1)S(1)} %fusion.4), channel_id=1, source_target_pairs={{0,29},{1,30},{2,31},{3,0},{4,1},{5,2},{6,3},{7,4},{8,5},{9,6},{10... | collective-permute-start | bytes 294920 | tf_op jit(solution)/shard_map/ppermute | solution.py:141
  107.1 12.1 %collective-permute-start.7 = (bf16[24,2048]{1,0:T(8,128)(2,1)}, bf16[24,2048]{1,0:T(8,128)(2,1)}, u32[]{:S(2)}, u32[]{:S(2)}) collective-permute-start(bf16[24,2048]{1,0:T(8,128)(2,1)} %fusion.2), channel_id=1, source_target_pairs={{0,3},{1,4},{2,5},{3,6},{4,7},{5,8},{6,9},{7,10},{8,11},{9,12},{10... | collective-permute-start | bytes 294920 | tf_op jit(solution)/shard_map/ppermute | solution.py:141
  109.6 13.1 %collective-permute-start.11 = (bf16[24,2048]{1,0:T(8,128)(2,1)}, bf16[24,2048]{1,0:T(8,128)(2,1)}, u32[]{:S(2)}, u32[]{:S(2)}) collective-permute-start(bf16[24,2048]{1,0:T(8,128)(2,1)} %fusion.5), channel_id=1, source_target_pairs={{0,29},{1,30},{2,31},{3,0},{4,1},{5,2},{6,3},{7,4},{8,5},{9,6},{10... | collective-permute-start | bytes 294920 | tf_op jit(solution)/shard_map/ppermute | solution.py:141
  116.6 6.2 %copy-start.12 = (f32[24,1024]{1,0:T(8,128)S(1)}, f32[24,1024]{1,0:T(8,128)}, u32[]{:S(2)}) copy-start(f32[24,1024]{1,0:T(8,128)} %get-tuple-element.56) | copy-start | bytes 294916
  116.6 17.6 %copy-start.11 = (f32[24,1024]{1,0:T(8,128)S(1)}, f32[24,1024]{1,0:T(8,128)}, u32[]{:S(2)}) copy-start(f32[24,1024]{1,0:T(8,128)} %get-tuple-element.57) | copy-start | bytes 294916
  123.7 20.4 %collective-permute-start.12 = (bf16[24,2048]{1,0:T(8,128)(2,1)S(1)}, bf16[24,2048]{1,0:T(8,128)(2,1)S(1)}, u32[]{:S(2)}, u32[]{:S(2)}) collective-permute-start(bf16[24,2048]{1,0:T(8,128)(2,1)S(1)} %fusion.8), channel_id=1, source_target_pairs={{0,3},{1,4},{2,5},{3,6},{4,7},{5,8},{6,9},{7,10},{8,11},{9,12},{10... | collective-permute-start | bytes 294920 | tf_op jit(solution)/shard_map/ppermute | solution.py:141
  135.2 10.5 %collective-permute-start.13 = (bf16[24,2048]{1,0:T(8,128)(2,1)S(1)}, bf16[24,2048]{1,0:T(8,128)(2,1)S(1)}, u32[]{:S(2)}, u32[]{:S(2)}) collective-permute-start(bf16[24,2048]{1,0:T(8,128)(2,1)S(1)} %fusion.9), channel_id=1, source_target_pairs={{0,29},{1,30},{2,31},{3,0},{4,1},{5,2},{6,3},{7,4},{8,5},{9,6},{10... | collective-permute-start | bytes 294920 | tf_op jit(solution)/shard_map/ppermute | solution.py:141
  137.1 1.9 %copy-start.1 = (bf16[1,768,2048]{2,1,0:T(8,128)(2,1)S(1)}, bf16[1,768,2048]{2,1,0:T(8,128)(2,1)}, u32[]{:S(2)}) copy-start(bf16[1,768,2048]{2,1,0:T(8,128)(2,1)} %param.9) | copy-start | bytes 9437188

commit v6 on v5

--- a/solution.py
+++ b/solution.py
@@ -10,6 +10,7 @@
 QUARTERS = 4
 HALVES = 2
 CHUNK = 24
+SENT = 21 * CHUNK
 VMEM_BYTES = 20 * 1024 * 1024
 
 
@@ -109,26 +110,35 @@
     return ((group + sign * offset) & 31) * CHUNK + rows - block * CHUNK
 
 
-def turn_kernel(place_ref, hidden_ref, turned_ref):
+def turn_kernel(place_ref, hidden_ref, sent_ref, own_ref):
     rows, inner = hidden_ref.shape
     source = chunk_order(place_ref[0], place_ref[1], iota((1, inner), 1))
     select = onehot(iota((inner, inner), 0) == source)
     turned = dot(select, hidden_ref[...], 0, 1).astype(BF16)
     row, column = iota((rows, 256), 0), iota((rows, 256), 1)
     peer, place = column >> 3, column & 7
-    turned_ref[:, 0:256] = dot(turned, onehot(row == peer * 10 + place)).astype(BF16)
+    low = dot(turned, onehot(row == peer * 10 + place))
     left = dot(turned, onehot(row == peer * 10 + 8 + (place >> 2)))
+    sent_ref[:, 0:256] = low[:SENT].astype(BF16)
+    own_ref[:, 0:256] = low[SENT:].astype(BF16)
     for q in range(QUARTERS):
-        mine = (iota((inner, 256), 1) & 3) == q
-        turned_ref[:, (q + 1) * 256 : (q + 2) * 256] = jnp.where(mine, left, 0.0).astype(BF16)
-
-
-def partial_kernel(scale, turned_ref, turned_left_ref, low_ref, left_ref, down_ref, up_ref, own_ref):
+        mine = jnp.where((iota((inner, 256), 1) & 3) == q, left, 0.0)
+        sent_ref[:, (q + 1) * 256 : (q + 2) * 256] = mine[:SENT].astype(BF16)
+        own_ref[:, (q + 1) * 256 : (q + 2) * 256] = mine[SENT:].astype(BF16)
+
+
+def sent_kernel(scale, turned_ref, turned_left_ref, low_ref, left_ref, down_ref, up_ref):
     product = dot(turned_ref[...], low_ref[...]) + dot(turned_left_ref[...], left_ref[...])
     product = product * scale
     down_ref[...] = product[: 11 * CHUNK].astype(BF16)
-    up_ref[...] = product[11 * CHUNK : 21 * CHUNK].astype(BF16)
-    own_ref[...] = product[21 * CHUNK :]
+    up_ref[...] = product[11 * CHUNK :].astype(BF16)
+
+
+def own_kernel(scale, turned_ref, turned_left_ref, *refs):
+    inputs, out_refs = refs[: 2 * HALVES], refs[2 * HALVES :]
+    for low_ref, left_ref, out_ref in zip(inputs[0::2], inputs[1::2], out_refs):
+        product = dot(turned_ref[...], low_ref[...]) + dot(turned_left_ref[...], left_ref[...])
+        out_ref[...] = product * scale
 
 
 def shift(block, distance):
@@ -255,11 +265,14 @@
     )(ids, probs, cotangent)
     sign = 1 - 2 * (lax.axis_index("ep") & 1)
     place = jnp.stack([lax.axis_index("dp"), sign]).astype(jnp.int32)
-    turned = call(
+    turned_sent, turned_own = call(
         turn_kernel,
-        jax.ShapeDtypeStruct((inner, 256 * (QUARTERS + 1)), BF16),
-        2 * inner * inner * rows,
-        10**6,
+        tuple(
+            jax.ShapeDtypeStruct((height, 256 * (QUARTERS + 1)), BF16)
+            for height in (SENT, inner - SENT)
+        ),
+        4 * inner * inner * rows,
+        2 * 10**6,
         in_specs=[pl.BlockSpec(memory_space=pltpu.SMEM), pl.BlockSpec(memory_space=pltpu.VMEM)],
     )(place, expert_hidden)
     expert_rows = call(
@@ -273,35 +286,45 @@
         scratch_shapes=[pltpu.VMEM((512, inner), BF16), pltpu.VMEM((256, width), F32)],
     )(expert_hidden, weight)
 
-    def partial(arrived):
+    scale = (groups * rows) ** (-0.5)
+
+    def turned_blocks(height):
+        first_columns = pl.BlockSpec((height, 256), lambda q: (0, 0))
+        return [first_columns, pl.BlockSpec((height, 256), lambda q: (0, q + 1))]
+
+    def sent(arrived):
         return call(
-            lambda *refs: partial_kernel((groups * rows) ** (-0.5), *refs),
+            lambda *refs: sent_kernel(scale, *refs),
             (
                 jax.ShapeDtypeStruct((11 * CHUNK, half), BF16),
                 jax.ShapeDtypeStruct((10 * CHUNK, half), BF16),
-                jax.ShapeDtypeStruct((11 * CHUNK, half), F32),
             ),
             product,
             4 * 10**6,
             grid=(QUARTERS,),
-            in_specs=[
-                pl.BlockSpec((inner, 256), lambda q: (0, 0)),
-                pl.BlockSpec((inner, 256), lambda q: (0, q + 1)),
-                half_low,
-                half_left,
-            ],
-            out_specs=tuple(block(n * CHUNK, lambda q: q) for n in (11, 10, 11)),
-        )(turned, turned, arrived, arrived)
+            in_specs=turned_blocks(SENT) + [half_low, half_left],
+            out_specs=tuple(block(n * CHUNK, lambda q: q) for n in (11, 10)),
+        )(turned_sent, turned_sent, arrived, arrived)
 
     first = exchange(outgoing[0], peers)
-    turned, expert_rows, first = lax.optimization_barrier((turned, expert_rows, first))
+    turned_sent, expert_rows, first = lax.optimization_barrier((turned_sent, expert_rows, first))
     first, behind = lax.optimization_barrier((first, outgoing[1]))
     second = exchange(behind, peers)
-    down_0, up_0, own_0 = partial(first)
+    down_0, up_0 = sent(first)
     above_0, below_0 = shift(down_0, -1), shift(up_0, 1)
-    down_1, up_1, own_1 = partial(second)
+    down_1, up_1 = sent(second)
     above_1, below_1 = shift(down_1, -1), shift(up_1, 1)
-    above_0, below_0, own_1, expert_rows = lax.optimization_barrier((above_0, below_0, own_1, expert_rows))
+    own_0, own_1 = call(
+        lambda *refs: own_kernel(scale, *refs),
+        (jax.ShapeDtypeStruct((inner - SENT, half), F32),) * HALVES,
+        product,
+        4 * 10**6,
+        52 * 1024 * 1024,
+        grid=(QUARTERS,),
+        in_specs=turned_blocks(inner - SENT) + [half_low, half_left] * HALVES,
+        out_specs=(block(inner - SENT, lambda q: q),) * HALVES,
+    )(turned_own, turned_own, first, first, second, second)
+    above_0, below_0, _, expert_rows = lax.optimization_barrier((above_0, below_0, down_1, expert_rows))
     returned = exchange(expert_rows, peers)
     hidden_grad = call(
         hidden_grad_kernel,

time: 147 us -> 144 us (0.980)
  the two profiles are of different devices: /device:TPU:34 before, /device:TPU:192 now
where the time goes in v6:
time: 144 us; the launch traced here: 143 us
  starting transfers between devices  77.3 us (54%)
  waiting for transfers between devices  27.6 us (19%)
  Pallas kernels  23.4 us (16%)
  other arithmetic  9.27 us (6%)
  local copies, waits for them, and re-layouts  4.07 us (3%)
    ppermute x14, starting transfers between devices, shift(): return lax.ppermute(block, ('ep', 'dp'), pairs)  61.7 us
    ppermute x14, waiting for transfers between devices, shift(): return lax.ppermute(block, ('ep', 'dp'), pairs)  18.8 us
    all_to_all x3, starting transfers between devices, exchange(): lax.all_to_all(blocks, 'ep', split_axis=0, concat_axis=0, tiled=True)  15.7 us
    all_to_all x3, waiting for transfers between devices, exchange(): lax.all_to_all(blocks, 'ep', split_axis=0, concat_axis=0, tiled=True)  8.77 us
    pallas_call x1, Pallas kernels, shards(): call(hidden_grad_kernel, jax.ShapeDtypeStruct((rows, inner), BF16), 2 * p...  5.09 us
    pallas_call x2, Pallas kernels, sent(): call(lambda *refs: sent_kernel(scale, *refs), (jax.ShapeDtypeStruct((11 *...  4.74 us
    pallas_call x1, Pallas kernels, shards(): call(expert_kernel, packed, 2 * product, 6 * 10 ** 6, grid=(QUARTERS,), i...  4.28 us
    unnamed x20, local copies, waits for them, and re-layouts  4.07 us
  transfers between devices with their start and end apart: 17, of which 9 were waited for; matrix products, arithmetic and copies ran while one was open for 5% of the time, Pallas kernels for 14%

profile of v6, /device:TPU:192, one launch (start us, length us, event | category | flops | bytes accessed | tf_op | source)
XLA Modules:
  0.0 142.7 jit_solution(647947546869031229)
XLA Ops:
  0.6 2.9 %shard_map.86 = (bf16[256,1280]{1,0:T(8,128)(2,1)}, bf16[256,1280]{1,0:T(8,128)(2,1)}) custom-call(s32[2,128]{1,0:T(2,128)} %bitcast.30, f32[2,128]{1,0:T(2,128)} %bitcast.32, bf16[128,2048]{1,0:T(8,128)(2,1)} %cot_ref.3), custom_call_target="tpu_custom_call" | custom-call | flops 268435456 | bytes 2000000 | tf_op jit(solution)/shard_map/pallas_call | solution.py:259
  3.5 7.3 %all-to-all-start = ((bf16[32,8,1280]{2,1,0:T(8,128)(2,1)}), bf16[32,8,1280]{2,1,0:T(8,128)(2,1)S(1)}, u32[]{:S(2)}, u32[]{:S(2)}) async-start(bf16[32,8,1280]{2,1,0:T(8,128)(2,1)} %bitcast.35), calls=%async_computation | async-start | bytes 1310720 | tf_op jit(solution)/shard_map/all_to_all | solution.py:239
  10.9 1.8 %shard_map.84 = (bf16[504,1280]{1,0:T(8,128)(2,1)S(1)}, bf16[264,1280]{1,0:T(8,128)(2,1)S(1)}) custom-call(s32[2]{0:T(128)S(1)} %pad_add_fusion.place_ref, bf16[320,768]{1,0:T(8,128)(2,1)S(1)} %copy-done.3), custom_call_target="tpu_custom_call" | custom-call | flops 754974720 | bytes 2000000 | tf_op jit(solution)/shard_map/pallas_call | solution.py:268
  12.7 1.9 %copy-done = bf16[1,768,2048]{2,1,0:T(8,128)(2,1)S(1)} copy-done((bf16[1,768,2048]{2,1,0:T(8,128)(2,1)S(1)}, bf16[1,768,2048]{2,1,0:T(8,128)(2,1)}, u32[]{:S(2)}) %copy-start) | copy-done | bytes 3145752
  14.6 4.3 %shard_map.85 = bf16[256,2560]{1,0:T(8,128)(2,1)} custom-call(bf16[320,768]{1,0:T(8,128)(2,1)S(1)} %copy-done.3, bf16[768,2048]{1,0:T(8,128)(2,1)S(1)} %bitcast.26), custom_call_target="tpu_custom_call" | custom-call | flops 2013265920 | bytes 6000000 | tf_op jit(solution)/shard_map/pallas_call | solution.py:278
  18.9 4.5 %all-to-all-done = bf16[32,8,1280]{2,1,0:T(8,128)(2,1)S(1)} async-done(((bf16[32,8,1280]{2,1,0:T(8,128)(2,1)}), bf16[32,8,1280]{2,1,0:T(8,128)(2,1)S(1)}, u32[]{:S(2)}, u32[]{:S(2)}) %all-to-all-start) | async-done | bytes 655392 | tf_op jit(solution)/shard_map/all_to_all | solution.py:239
  23.4 4.1 %all-to-all-start.1 = ((bf16[32,8,1280]{2,1,0:T(8,128)(2,1)}), bf16[32,8,1280]{2,1,0:T(8,128)(2,1)S(1)}, u32[]{:S(2)}, u32[]{:S(2)}) async-start(bf16[32,8,1280]{2,1,0:T(8,128)(2,1)} %bitcast.34), calls=%async_computation.1 | async-start | bytes 1310720 | tf_op jit(solution)/shard_map/all_to_all | solution.py:239
  27.5 2.4 %shard_map.88 = (bf16[264,1024]{1,0:T(8,128)(2,1)}, bf16[240,1024]{1,0:T(8,128)(2,1)}) custom-call(bf16[504,1280]{1,0:T(8,128)(2,1)S(1)} %get-tuple-element.36.refs_0_.refs_1_, bf16[504,1280]{1,0:T(8,128)(2,1)S(1)} %get-tuple-element.36.refs_0_.refs_1_, bf16[256,1280]{1,0:T(8,128)(2,1)S(1)} %bitcast.14, bf16[256,1280]{1,0:T(8,128)(2,1)S(1)} %bitcast.15), custom_call_target="tpu_custom_call" | custom-call | flops 1006632960 | bytes 4000000 | tf_op jit(solution)/shard_map/pallas_call | solution.py:296
  29.9 2.0 %collective-permute-start = (bf16[264,1024]{1,0:T(8,128)(2,1)}, bf16[264,1024]{1,0:T(8,128)(2,1)}, u32[]{:S(2)}, u32[]{:S(2)}) collective-permute-start(bf16[264,1024]{1,0:T(8,128)(2,1)} %get-tuple-element.37), channel_id=1, source_target_pairs={{0,31},{1,0},{2,1},{3,2},{4,3},{5,4},{6,5},{7,6},{8,7},{9,8},{10,9... | collective-permute-start | bytes 1622024 | tf_op jit(solution)/shard_map/ppermute | solution.py:151
  31.9 3.8 %collective-permute-start.1 = (bf16[240,1024]{1,0:T(8,128)(2,1)}, bf16[240,1024]{1,0:T(8,128)(2,1)}, u32[]{:S(2)}, u32[]{:S(2)}) collective-permute-start(bf16[240,1024]{1,0:T(8,128)(2,1)} %get-tuple-element.38), channel_id=1, source_target_pairs={{0,1},{1,2},{2,3},{3,4},{4,5},{5,6},{6,7},{7,8},{8,9},{9,10},{10,1... | collective-permute-start | bytes 1474568 | tf_op jit(solution)/shard_map/ppermute | solution.py:151
  35.7 4.3 %all-to-all-done.1 = bf16[32,8,1280]{2,1,0:T(8,128)(2,1)S(1)} async-done(((bf16[32,8,1280]{2,1,0:T(8,128)(2,1)}), bf16[32,8,1280]{2,1,0:T(8,128)(2,1)S(1)}, u32[]{:S(2)}, u32[]{:S(2)}) %all-to-all-start.1) | async-done | bytes 655392 | tf_op jit(solution)/shard_map/all_to_all | solution.py:239
  40.0 2.4 %shard_map.89 = (bf16[264,1024]{1,0:T(8,128)(2,1)}, bf16[240,1024]{1,0:T(8,128)(2,1)}) custom-call(bf16[504,1280]{1,0:T(8,128)(2,1)S(1)} %get-tuple-element.36.refs_0_.refs_1_, bf16[504,1280]{1,0:T(8,128)(2,1)S(1)} %get-tuple-element.36.refs_0_.refs_1_, bf16[256,1280]{1,0:T(8,128)(2,1)S(1)} %bitcast.20, bf16[256,1280]{1,0:T(8,128)(2,1)S(1)} %bitcast.21), custom_call_target="tpu_custom_call" | custom-call | flops 1006632960 | bytes 4000000 | tf_op jit(solution)/shard_map/pallas_call | solution.py:296
  42.4 3.8 %collective-permute-start.4 = (bf16[240,1024]{1,0:T(8,128)(2,1)}, bf16[240,1024]{1,0:T(8,128)(2,1)}, u32[]{:S(2)}, u32[]{:S(2)}) collective-permute-start(bf16[240,1024]{1,0:T(8,128)(2,1)} %get-tuple-element.44), channel_id=1, source_target_pairs={{0,1},{1,2},{2,3},{3,4},{4,5},{5,6},{6,7},{7,8},{8,9},{9,10},{10,1... | collective-permute-start | bytes 1474568 | tf_op jit(solution)/shard_map/ppermute | solution.py:151
  46.2 2.0 %collective-permute-start.2 = (bf16[264,1024]{1,0:T(8,128)(2,1)}, bf16[264,1024]{1,0:T(8,128)(2,1)S(1)}, u32[]{:S(2)}, u32[]{:S(2)}) collective-permute-start(bf16[264,1024]{1,0:T(8,128)(2,1)} %get-tuple-element.39), channel_id=1, source_target_pairs={{0,31},{1,0},{2,1},{3,2},{4,3},{5,4},{6,5},{7,6},{8,7},{9,8},{10,9... | collective-permute-start | bytes 1622024 | tf_op jit(solution)/shard_map/ppermute | solution.py:151
  48.2 2.8 %shard_map.87 = (f32[264,1024]{1,0:T(8,128)}, f32[264,1024]{1,0:T(8,128)}) custom-call(bf16[264,1280]{1,0:T(8,128)(2,1)S(1)} %get-tuple-element.28.refs_0_.refs_1_, bf16[264,1280]{1,0:T(8,128)(2,1)S(1)} %get-tuple-element.28.refs_0_.refs_1_, bf16[256,1280]{1,0:T(8,128)(2,1)S(1)} %bitcast.16, bf16[256,1280]{1,0:T(8,128)(2,1)S(1)} %bitcast.17, ...), custom_call_target="tpu_custom_call" | custom-call | flops 1006632960 | bytes 4000000 | tf_op jit(solution)/shard_map/pallas_call | solution.py:317
  51.1 4.2 %all-to-all-start.2 = ((bf16[32,8,2560]{2,1,0:T(8,128)(2,1)}), bf16[32,8,2560]{2,1,0:T(8,128)(2,1)S(1)}, u32[]{:S(2)}, u32[]{:S(2)}) async-start(bf16[32,8,2560]{2,1,0:T(8,128)(2,1)} %bitcast.9), calls=%async_computation.2 | async-start | bytes 2621440 | tf_op jit(solution)/shard_map/all_to_all | solution.py:239
  60.0 7.7 %collective-permute-start.3 = (bf16[24,2048]{1,0:T(8,128)(2,1)S(1)}, bf16[24,2048]{1,0:T(8,128)(2,1)S(1)}, u32[]{:S(2)}, u32[]{:S(2)}) collective-permute-start(bf16[24,2048]{1,0:T(8,128)(2,1)S(1)} %pad_maximum_fusion), channel_id=1, source_target_pairs={{0,3},{1,4},{2,5},{3,6},{4,7},{5,8},{6,9},{7,10},{8,11},{9,12},{10... | collective-permute-start | bytes 294920 | tf_op jit(solution)/shard_map/ppermute | solution.py:151
  67.7 1.9 %collective-permute-start.8 = (bf16[24,2048]{1,0:T(8,128)(2,1)S(1)}, bf16[24,2048]{1,0:T(8,128)(2,1)S(1)}, u32[]{:S(2)}, u32[]{:S(2)}) collective-permute-start(bf16[24,2048]{1,0:T(8,128)(2,1)S(1)} %pad_maximum_fusion.1), channel_id=1, source_target_pairs={{0,29},{1,30},{2,31},{3,0},{4,1},{5,2},{6,3},{7,4},{8,5},{9,6},{10... | collective-permute-start | bytes 294920 | tf_op jit(solution)/shard_map/ppermute | solution.py:151
  71.4 2.1 %collective-permute-done.3 = bf16[24,2048]{1,0:T(8,128)(2,1)S(1)} collective-permute-done((bf16[24,2048]{1,0:T(8,128)(2,1)S(1)}, bf16[24,2048]{1,0:T(8,128)(2,1)S(1)}, u32[]{:S(2)}, u32[]{:S(2)}) %collective-permute-start.3) | collective-permute-done | bytes 98336 | tf_op jit(solution)/shard_map/ppermute | solution.py:151
  73.5 8.5 %collective-permute-start.5 = (bf16[24,2048]{1,0:T(8,128)(2,1)S(1)}, bf16[24,2048]{1,0:T(8,128)(2,1)S(1)}, u32[]{:S(2)}, u32[]{:S(2)}) collective-permute-start(bf16[24,2048]{1,0:T(8,128)(2,1)S(1)} %fusion), channel_id=1, source_target_pairs={{0,3},{1,4},{2,5},{3,6},{4,7},{5,8},{6,9},{7,10},{8,11},{9,12},{10... | collective-permute-start | bytes 294920 | tf_op jit(solution)/shard_map/ppermute | solution.py:151
  82.1 1.9 %collective-permute-start.9 = (bf16[24,2048]{1,0:T(8,128)(2,1)S(1)}, bf16[24,2048]{1,0:T(8,128)(2,1)S(1)}, u32[]{:S(2)}, u32[]{:S(2)}) collective-permute-start(bf16[24,2048]{1,0:T(8,128)(2,1)S(1)} %fusion.3), channel_id=1, source_target_pairs={{0,29},{1,30},{2,31},{3,0},{4,1},{5,2},{6,3},{7,4},{8,5},{9,6},{10... | collective-permute-start | bytes 294920 | tf_op jit(solution)/shard_map/ppermute | solution.py:151
  85.1 7.6 %collective-permute-start.6 = (bf16[24,2048]{1,0:T(8,128)(2,1)S(1)}, bf16[24,2048]{1,0:T(8,128)(2,1)S(1)}, u32[]{:S(2)}, u32[]{:S(2)}) collective-permute-start(bf16[24,2048]{1,0:T(8,128)(2,1)S(1)} %fusion.1), channel_id=1, source_target_pairs={{0,3},{1,4},{2,5},{3,6},{4,7},{5,8},{6,9},{7,10},{8,11},{9,12},{10... | collective-permute-start | bytes 294920 | tf_op jit(solution)/shard_map/ppermute | solution.py:151
  92.7 1.9 %collective-permute-start.10 = (bf16[24,2048]{1,0:T(8,128)(2,1)S(1)}, bf16[24,2048]{1,0:T(8,128)(2,1)S(1)}, u32[]{:S(2)}, u32[]{:S(2)}) collective-permute-start(bf16[24,2048]{1,0:T(8,128)(2,1)S(1)} %fusion.4), channel_id=1, source_target_pairs={{0,29},{1,30},{2,31},{3,0},{4,1},{5,2},{6,3},{7,4},{8,5},{9,6},{10... | collective-permute-start | bytes 294920 | tf_op jit(solution)/shard_map/ppermute | solution.py:151
  94.7 2.3 %collective-permute-done.6 = bf16[24,2048]{1,0:T(8,128)(2,1)S(1)} collective-permute-done((bf16[24,2048]{1,0:T(8,128)(2,1)S(1)}, bf16[24,2048]{1,0:T(8,128)(2,1)S(1)}, u32[]{:S(2)}, u32[]{:S(2)}) %collective-permute-start.6) | collective-permute-done | bytes 98336 | tf_op jit(solution)/shard_map/ppermute | solution.py:151
  97.7 9.4 %collective-permute-start.7 = (bf16[24,2048]{1,0:T(8,128)(2,1)}, bf16[24,2048]{1,0:T(8,128)(2,1)}, u32[]{:S(2)}, u32[]{:S(2)}) collective-permute-start(bf16[24,2048]{1,0:T(8,128)(2,1)} %fusion.2), channel_id=1, source_target_pairs={{0,3},{1,4},{2,5},{3,6},{4,7},{5,8},{6,9},{7,10},{8,11},{9,12},{10... | collective-permute-start | bytes 294920 | tf_op jit(solution)/shard_map/ppermute | solution.py:151
  107.7 1.9 %collective-permute-start.11 = (bf16[24,2048]{1,0:T(8,128)(2,1)}, bf16[24,2048]{1,0:T(8,128)(2,1)}, u32[]{:S(2)}, u32[]{:S(2)}) collective-permute-start(bf16[24,2048]{1,0:T(8,128)(2,1)} %fusion.5), channel_id=1, source_target_pairs={{0,29},{1,30},{2,31},{3,0},{4,1},{5,2},{6,3},{7,4},{8,5},{9,6},{10... | collective-permute-start | bytes 294920 | tf_op jit(solution)/shard_map/ppermute | solution.py:151
  109.7 1.8 %shard_map.90 = (bf16[128,2048]{1,0:T(8,128)(2,1)}, f32[2,128]{1,0:T(2,128)}) custom-call(s32[2,128]{1,0:T(2,128)S(1)} %bitcast.31, f32[2,128]{1,0:T(2,128)S(1)} %bitcast.33, bf16[128,2048]{1,0:T(8,128)(2,1)S(1)} %copy-done.2, bf16[256,2560]{1,0:T(8,128)(2,1)S(1)} %bitcast.29), custom_call_target="tpu_custom_call" | custom-call | flops 536870912 | bytes 3000000 | tf_op jit(solution)/shard_map/pallas_call | solution.py:342
  112.4 9.9 %collective-permute-done.11 = bf16[24,2048]{1,0:T(8,128)(2,1)} collective-permute-done((bf16[24,2048]{1,0:T(8,128)(2,1)}, bf16[24,2048]{1,0:T(8,128)(2,1)}, u32[]{:S(2)}, u32[]{:S(2)}) %collective-permute-start.11) | collective-permute-done | bytes 98336 | tf_op jit(solution)/shard_map/ppermute | solution.py:151
  123.3 7.2 %collective-permute-start.12 = (bf16[24,2048]{1,0:T(8,128)(2,1)S(1)}, bf16[24,2048]{1,0:T(8,128)(2,1)S(1)}, u32[]{:S(2)}, u32[]{:S(2)}) collective-permute-start(bf16[24,2048]{1,0:T(8,128)(2,1)S(1)} %fusion.8), channel_id=1, source_target_pairs={{0,3},{1,4},{2,5},{3,6},{4,7},{5,8},{6,9},{7,10},{8,11},{9,12},{10... | collective-permute-start | bytes 294920 | tf_op jit(solution)/shard_map/ppermute | solution.py:151
  131.4 1.9 %collective-permute-start.13 = (bf16[24,2048]{1,0:T(8,128)(2,1)S(1)}, bf16[24,2048]{1,0:T(8,128)(2,1)S(1)}, u32[]{:S(2)}, u32[]{:S(2)}) collective-permute-start(bf16[24,2048]{1,0:T(8,128)(2,1)S(1)} %fusion.9), channel_id=1, source_target_pairs={{0,29},{1,30},{2,31},{3,0},{4,1},{5,2},{6,3},{7,4},{8,5},{9,6},{10... | collective-permute-start | bytes 294920 | tf_op jit(solution)/shard_map/ppermute | solution.py:151
  133.3 1.9 %copy-done.1 = bf16[1,768,2048]{2,1,0:T(8,128)(2,1)S(1)} copy-done((bf16[1,768,2048]{2,1,0:T(8,128)(2,1)S(1)}, bf16[1,768,2048]{2,1,0:T(8,128)(2,1)}, u32[]{:S(2)}) %copy-start.1) | copy-done | bytes 3145752
  135.2 5.1 %shard_map.91 = bf16[320,768]{1,0:T(8,128)(2,1)} custom-call(bf16[256,1280]{1,0:T(8,128)(2,1)S(1)} %bitcast.18, bf16[256,1280]{1,0:T(8,128)(2,1)S(1)} %bitcast.19, bf16[768,2048]{1,0:T(8,128)(2,1)S(1)} %bitcast.27, bf16[256,1280]{1,0:T(8,128)(2,1)S(1)} %bitcast.24, bf16[256,1280]{1,0:T(8,128)(2,1)S(1)} %bitcast.25, bf16[768,2048]{1,0:T(8,128)(2,1)S(1)} %bitcast.28), custom_call_target="tpu_custom_call" | custom-call | flops 2013265920 | bytes 6000000 | tf_op jit(solution)/shard_map/pallas_call | solution.py:329
  (46 shorter events, 14.0 us)
Async XLA Ops:
  0.6 10.3 %copy-start.3 = (bf16[320,768]{1,0:T(8,128)(2,1)S(1)}, bf16[320,768]{1,0:T(8,128)(2,1)}, u32[]{:S(2)}) copy-start(bf16[320,768]{1,0:T(8,128)(2,1)} %hidden_ref.3) | copy-start | bytes 1474564
  3.5 19.9 %all-to-all-start = ((bf16[32,8,1280]{2,1,0:T(8,128)(2,1)}), bf16[32,8,1280]{2,1,0:T(8,128)(2,1)S(1)}, u32[]{:S(2)}, u32[]{:S(2)}) async-start(bf16[32,8,1280]{2,1,0:T(8,128)(2,1)} %bitcast.35), calls=%async_computation | async-start | bytes 1310720 | tf_op jit(solution)/shard_map/all_to_all | solution.py:239
  12.7 1.9 %copy-start = (bf16[1,768,2048]{2,1,0:T(8,128)(2,1)S(1)}, bf16[1,768,2048]{2,1,0:T(8,128)(2,1)}, u32[]{:S(2)}) copy-start(bf16[1,768,2048]{2,1,0:T(8,128)(2,1)} %param.9) | copy-start | bytes 9437188
  23.4 16.7 %all-to-all-start.1 = ((bf16[32,8,1280]{2,1,0:T(8,128)(2,1)}), bf16[32,8,1280]{2,1,0:T(8,128)(2,1)S(1)}, u32[]{:S(2)}, u32[]{:S(2)}) async-start(bf16[32,8,1280]{2,1,0:T(8,128)(2,1)} %bitcast.34), calls=%async_computation.1 | async-start | bytes 1310720 | tf_op jit(solution)/shard_map/all_to_all | solution.py:239
  29.9 21.2 %collective-permute-start = (bf16[264,1024]{1,0:T(8,128)(2,1)}, bf16[264,1024]{1,0:T(8,128)(2,1)}, u32[]{:S(2)}, u32[]{:S(2)}) collective-permute-start(bf16[264,1024]{1,0:T(8,128)(2,1)} %get-tuple-element.37), channel_id=1, source_target_pairs={{0,31},{1,0},{2,1},{3,2},{4,3},{5,4},{6,5},{7,6},{8,7},{9,8},{10,9... | collective-permute-start | bytes 1622024 | tf_op jit(solution)/shard_map/ppermute | solution.py:151
  31.9 19.2 %collective-permute-start.1 = (bf16[240,1024]{1,0:T(8,128)(2,1)}, bf16[240,1024]{1,0:T(8,128)(2,1)}, u32[]{:S(2)}, u32[]{:S(2)}) collective-permute-start(bf16[240,1024]{1,0:T(8,128)(2,1)} %get-tuple-element.38), channel_id=1, source_target_pairs={{0,1},{1,2},{2,3},{3,4},{4,5},{5,6},{6,7},{7,8},{8,9},{9,10},{10,1... | collective-permute-start | bytes 1474568 | tf_op jit(solution)/shard_map/ppermute | solution.py:151
  42.4 15.8 %collective-permute-start.4 = (bf16[240,1024]{1,0:T(8,128)(2,1)}, bf16[240,1024]{1,0:T(8,128)(2,1)}, u32[]{:S(2)}, u32[]{:S(2)}) collective-permute-start(bf16[240,1024]{1,0:T(8,128)(2,1)} %get-tuple-element.44), channel_id=1, source_target_pairs={{0,1},{1,2},{2,3},{3,4},{4,5},{5,6},{6,7},{7,8},{8,9},{9,10},{10,1... | collective-permute-start | bytes 1474568 | tf_op jit(solution)/shard_map/ppermute | solution.py:151
  46.2 12.8 %collective-permute-start.2 = (bf16[264,1024]{1,0:T(8,128)(2,1)}, bf16[264,1024]{1,0:T(8,128)(2,1)S(1)}, u32[]{:S(2)}, u32[]{:S(2)}) collective-permute-start(bf16[264,1024]{1,0:T(8,128)(2,1)} %get-tuple-element.39), channel_id=1, source_target_pairs={{0,31},{1,0},{2,1},{3,2},{4,3},{5,4},{6,5},{7,6},{8,7},{9,8},{10,9... | collective-permute-start | bytes 1622024 | tf_op jit(solution)/shard_map/ppermute | solution.py:151
  51.1 58.5 %all-to-all-start.2 = ((bf16[32,8,2560]{2,1,0:T(8,128)(2,1)}), bf16[32,8,2560]{2,1,0:T(8,128)(2,1)S(1)}, u32[]{:S(2)}, u32[]{:S(2)}) async-start(bf16[32,8,2560]{2,1,0:T(8,128)(2,1)} %bitcast.9), calls=%async_computation.2 | async-start | bytes 2621440 | tf_op jit(solution)/shard_map/all_to_all | solution.py:239
  55.3 1.6 %copy-start.7 = (f32[264,1024]{1,0:T(8,128)S(1)}, f32[264,1024]{1,0:T(8,128)}, u32[]{:S(2)}) copy-start(f32[264,1024]{1,0:T(8,128)} %get-tuple-element.35) | copy-start | bytes 3244036
  56.9 2.1 %copy-start.6 = (f32[264,1024]{1,0:T(8,128)S(1)}, f32[264,1024]{1,0:T(8,128)}, u32[]{:S(2)}) copy-start(f32[264,1024]{1,0:T(8,128)} %get-tuple-element.42) | copy-start | bytes 3244036
  60.0 13.5 %collective-permute-start.3 = (bf16[24,2048]{1,0:T(8,128)(2,1)S(1)}, bf16[24,2048]{1,0:T(8,128)(2,1)S(1)}, u32[]{:S(2)}, u32[]{:S(2)}) collective-permute-start(bf16[24,2048]{1,0:T(8,128)(2,1)S(1)} %pad_maximum_fusion), channel_id=1, source_target_pairs={{0,3},{1,4},{2,5},{3,6},{4,7},{5,8},{6,9},{7,10},{8,11},{9,12},{10... | collective-permute-start | bytes 294920 | tf_op jit(solution)/shard_map/ppermute | solution.py:151
  67.7 14.3 %collective-permute-start.8 = (bf16[24,2048]{1,0:T(8,128)(2,1)S(1)}, bf16[24,2048]{1,0:T(8,128)(2,1)S(1)}, u32[]{:S(2)}, u32[]{:S(2)}) collective-permute-start(bf16[24,2048]{1,0:T(8,128)(2,1)S(1)} %pad_maximum_fusion.1), channel_id=1, source_target_pairs={{0,29},{1,30},{2,31},{3,0},{4,1},{5,2},{6,3},{7,4},{8,5},{9,6},{10... | collective-permute-start | bytes 294920 | tf_op jit(solution)/shard_map/ppermute | solution.py:151
  73.5 36.2 %copy-start.2 = (bf16[128,2048]{1,0:T(8,128)(2,1)S(1)}, bf16[128,2048]{1,0:T(8,128)(2,1)}, u32[]{:S(2)}) copy-start(bf16[128,2048]{1,0:T(8,128)(2,1)} %cot_ref.3) | copy-start | bytes 1572868
  73.5 36.2 %copy-start.4 = (s32[128,2]{0,1:T(2,128)S(1)}, s32[128,2]{0,1:T(2,128)}, u32[]{:S(2)}) copy-start(s32[128,2]{0,1:T(2,128)} %param.6) | copy-start | bytes 3076
  73.5 36.2 %copy-start.5 = (f32[128,2]{0,1:T(2,128)S(1)}, f32[128,2]{0,1:T(2,128)}, u32[]{:S(2)}) copy-start(f32[128,2]{0,1:T(2,128)} %param.7) | copy-start | bytes 3076
  73.5 11.6 %collective-permute-start.5 = (bf16[24,2048]{1,0:T(8,128)(2,1)S(1)}, bf16[24,2048]{1,0:T(8,128)(2,1)S(1)}, u32[]{:S(2)}, u32[]{:S(2)}) collective-permute-start(bf16[24,2048]{1,0:T(8,128)(2,1)S(1)} %fusion), channel_id=1, source_target_pairs={{0,3},{1,4},{2,5},{3,6},{4,7},{5,8},{6,9},{7,10},{8,11},{9,12},{10... | collective-permute-start | bytes 294920 | tf_op jit(solution)/shard_map/ppermute | solution.py:151
  82.1 10.6 %collective-permute-start.9 = (bf16[24,2048]{1,0:T(8,128)(2,1)S(1)}, bf16[24,2048]{1,0:T(8,128)(2,1)S(1)}, u32[]{:S(2)}, u32[]{:S(2)}) collective-permute-start(bf16[24,2048]{1,0:T(8,128)(2,1)S(1)} %fusion.3), channel_id=1, source_target_pairs={{0,29},{1,30},{2,31},{3,0},{4,1},{5,2},{6,3},{7,4},{8,5},{9,6},{10... | collective-permute-start | bytes 294920 | tf_op jit(solution)/shard_map/ppermute | solution.py:151
  85.1 11.9 %collective-permute-start.6 = (bf16[24,2048]{1,0:T(8,128)(2,1)S(1)}, bf16[24,2048]{1,0:T(8,128)(2,1)S(1)}, u32[]{:S(2)}, u32[]{:S(2)}) collective-permute-start(bf16[24,2048]{1,0:T(8,128)(2,1)S(1)} %fusion.1), channel_id=1, source_target_pairs={{0,3},{1,4},{2,5},{3,6},{4,7},{5,8},{6,9},{7,10},{8,11},{9,12},{10... | collective-permute-start | bytes 294920 | tf_op jit(solution)/shard_map/ppermute | solution.py:151
  92.7 14.3 %collective-permute-start.10 = (bf16[24,2048]{1,0:T(8,128)(2,1)S(1)}, bf16[24,2048]{1,0:T(8,128)(2,1)S(1)}, u32[]{:S(2)}, u32[]{:S(2)}) collective-permute-start(bf16[24,2048]{1,0:T(8,128)(2,1)S(1)} %fusion.4), channel_id=1, source_target_pairs={{0,29},{1,30},{2,31},{3,0},{4,1},{5,2},{6,3},{7,4},{8,5},{9,6},{10... | collective-permute-start | bytes 294920 | tf_op jit(solution)/shard_map/ppermute | solution.py:151
  97.7 14.7 %collective-permute-start.7 = (bf16[24,2048]{1,0:T(8,128)(2,1)}, bf16[24,2048]{1,0:T(8,128)(2,1)}, u32[]{:S(2)}, u32[]{:S(2)}) collective-permute-start(bf16[24,2048]{1,0:T(8,128)(2,1)} %fusion.2), channel_id=1, source_target_pairs={{0,3},{1,4},{2,5},{3,6},{4,7},{5,8},{6,9},{7,10},{8,11},{9,12},{10... | collective-permute-start | bytes 294920 | tf_op jit(solution)/shard_map/ppermute | solution.py:151
  107.7 14.6 %collective-permute-start.11 = (bf16[24,2048]{1,0:T(8,128)(2,1)}, bf16[24,2048]{1,0:T(8,128)(2,1)}, u32[]{:S(2)}, u32[]{:S(2)}) collective-permute-start(bf16[24,2048]{1,0:T(8,128)(2,1)} %fusion.5), channel_id=1, source_target_pairs={{0,29},{1,30},{2,31},{3,0},{4,1},{5,2},{6,3},{7,4},{8,5},{9,6},{10... | collective-permute-start | bytes 294920 | tf_op jit(solution)/shard_map/ppermute | solution.py:151
  109.6 12.7 %copy-start.9 = (f32[24,1024]{1,0:T(8,128)S(1)}, f32[24,1024]{1,0:T(8,128)}, u32[]{:S(2)}) copy-start(f32[24,1024]{1,0:T(8,128)} %get-tuple-element.58) | copy-start | bytes 294916
  109.7 20.8 %copy-start.8 = (f32[24,1024]{1,0:T(8,128)S(1)}, f32[24,1024]{1,0:T(8,128)}, u32[]{:S(2)}) copy-start(f32[24,1024]{1,0:T(8,128)} %get-tuple-element.59) | copy-start | bytes 294916
  123.3 17.1 %collective-permute-start.12 = (bf16[24,2048]{1,0:T(8,128)(2,1)S(1)}, bf16[24,2048]{1,0:T(8,128)(2,1)S(1)}, u32[]{:S(2)}, u32[]{:S(2)}) collective-permute-start(bf16[24,2048]{1,0:T(8,128)(2,1)S(1)} %fusion.8), channel_id=1, source_target_pairs={{0,3},{1,4},{2,5},{3,6},{4,7},{5,8},{6,9},{7,10},{8,11},{9,12},{10... | collective-permute-start | bytes 294920 | tf_op jit(solution)/shard_map/ppermute | solution.py:151
  131.4 10.6 %collective-permute-start.13 = (bf16[24,2048]{1,0:T(8,128)(2,1)S(1)}, bf16[24,2048]{1,0:T(8,128)(2,1)S(1)}, u32[]{:S(2)}, u32[]{:S(2)}) collective-permute-start(bf16[24,2048]{1,0:T(8,128)(2,1)S(1)} %fusion.9), channel_id=1, source_target_pairs={{0,29},{1,30},{2,31},{3,0},{4,1},{5,2},{6,3},{7,4},{8,5},{9,6},{10... | collective-permute-start | bytes 294920 | tf_op jit(solution)/shard_map/ppermute | solution.py:151
  133.3 1.9 %copy-start.1 = (bf16[1,768,2048]{2,1,0:T(8,128)(2,1)S(1)}, bf16[1,768,2048]{2,1,0:T(8,128)(2,1)}, u32[]{:S(2)}) copy-start(bf16[1,768,2048]{2,1,0:T(8,128)(2,1)} %param.9) | copy-start | bytes 9437188

commit v7 on v6

--- a/solution.py
+++ b/solution.py
@@ -166,7 +166,7 @@
     for k in range(1, 5):
         rising, falling = shift(rising.astype(BF16), 3), shift(falling.astype(BF16), -3)
         if k == 4:
-            rising, falling, combined = lax.optimization_barrier((rising, falling, combine(returned)))
+            falling, combined = lax.optimization_barrier((falling, combine(returned)))
         rising, falling = rising.astype(F32) + term(k), falling.astype(F32) + term(10 - k)
     rising, falling = shift(rising.astype(BF16), 3), shift(falling.astype(BF16), -3)
     return term(5) + rising.astype(F32) + falling.astype(F32), combined

time: 144 us -> 142 us (0.986)
  the two profiles are of different devices: /device:TPU:192 before, /device:TPU:36 now
where the time goes in v7:
time: 142 us; the launch traced here: 140 us
  starting transfers between devices  93.3 us (66%)
  Pallas kernels  23.4 us (16%)
  waiting for transfers between devices  9.83 us (7%)
  other arithmetic  8.6 us (6%)
  local copies, waits for them, and re-layouts  4.27 us (3%)
    ppermute x14, starting transfers between devices, shift(): return lax.ppermute(block, ('ep', 'dp'), pairs)  72.5 us
    all_to_all x3, starting transfers between devices, exchange(): lax.all_to_all(blocks, 'ep', split_axis=0, concat_axis=0, tiled=True)  20.8 us
    ppermute x14, waiting for transfers between devices, shift(): return lax.ppermute(block, ('ep', 'dp'), pairs)  6.99 us
    pallas_call x1, Pallas kernels, shards(): call(hidden_grad_kernel, jax.ShapeDtypeStruct((rows, inner), BF16), 2 * p...  5.08 us
    pallas_call x2, Pallas kernels, sent(): call(lambda *refs: sent_kernel(scale, *refs), (jax.ShapeDtypeStruct((11 *...  4.76 us
    unnamed x16, local copies, waits for them, and re-layouts  4.27 us
    pallas_call x1, Pallas kernels, shards(): call(expert_kernel, packed, 2 * product, 6 * 10 ** 6, grid=(QUARTERS,), i...  4.26 us
    pallas_call x1, Pallas kernels, shards(): call(send_kernel, (half_packed,) * HALVES, 4 * 256 * tokens * features, 2...  2.86 us
  transfers between devices with their start and end apart: 17, of which 5 were waited for; matrix products, arithmetic and copies ran while one was open for 5% of the time, Pallas kernels for 15%

profile of v7, /device:TPU:36, one launch (start us, length us, event | category | flops | bytes accessed | tf_op | source)
XLA Modules:
  0.0 140.4 jit_solution(11815169513420116584)
XLA Ops:
  0.6 2.9 %shard_map.86 = (bf16[256,1280]{1,0:T(8,128)(2,1)}, bf16[256,1280]{1,0:T(8,128)(2,1)}) custom-call(s32[2,128]{1,0:T(2,128)} %bitcast.30, f32[2,128]{1,0:T(2,128)} %bitcast.32, bf16[128,2048]{1,0:T(8,128)(2,1)} %cot_ref.3), custom_call_target="tpu_custom_call" | custom-call | flops 268435456 | bytes 2000000 | tf_op jit(solution)/shard_map/pallas_call | solution.py:259
  3.5 7.6 %all-to-all-start = ((bf16[32,8,1280]{2,1,0:T(8,128)(2,1)}), bf16[32,8,1280]{2,1,0:T(8,128)(2,1)S(1)}, u32[]{:S(2)}, u32[]{:S(2)}) async-start(bf16[32,8,1280]{2,1,0:T(8,128)(2,1)} %bitcast.35), calls=%async_computation | async-start | bytes 1310720 | tf_op jit(solution)/shard_map/all_to_all | solution.py:239
  11.2 1.8 %shard_map.84 = (bf16[504,1280]{1,0:T(8,128)(2,1)S(1)}, bf16[264,1280]{1,0:T(8,128)(2,1)S(1)}) custom-call(s32[2]{0:T(128)S(1)} %pad_add_fusion.place_ref, bf16[320,768]{1,0:T(8,128)(2,1)S(1)} %copy-done.3), custom_call_target="tpu_custom_call" | custom-call | flops 754974720 | bytes 2000000 | tf_op jit(solution)/shard_map/pallas_call | solution.py:268
  13.0 1.9 %copy-done = bf16[1,768,2048]{2,1,0:T(8,128)(2,1)S(1)} copy-done((bf16[1,768,2048]{2,1,0:T(8,128)(2,1)S(1)}, bf16[1,768,2048]{2,1,0:T(8,128)(2,1)}, u32[]{:S(2)}) %copy-start) | copy-done | bytes 3145752
  14.9 4.3 %shard_map.85 = bf16[256,2560]{1,0:T(8,128)(2,1)} custom-call(bf16[320,768]{1,0:T(8,128)(2,1)S(1)} %copy-done.3, bf16[768,2048]{1,0:T(8,128)(2,1)S(1)} %bitcast.26), custom_call_target="tpu_custom_call" | custom-call | flops 2013265920 | bytes 6000000 | tf_op jit(solution)/shard_map/pallas_call | solution.py:278
  19.2 2.8 %all-to-all-done = bf16[32,8,1280]{2,1,0:T(8,128)(2,1)S(1)} async-done(((bf16[32,8,1280]{2,1,0:T(8,128)(2,1)}), bf16[32,8,1280]{2,1,0:T(8,128)(2,1)S(1)}, u32[]{:S(2)}, u32[]{:S(2)}) %all-to-all-start) | async-done | bytes 655392 | tf_op jit(solution)/shard_map/all_to_all | solution.py:239
  22.0 5.8 %all-to-all-start.1 = ((bf16[32,8,1280]{2,1,0:T(8,128)(2,1)}), bf16[32,8,1280]{2,1,0:T(8,128)(2,1)S(1)}, u32[]{:S(2)}, u32[]{:S(2)}) async-start(bf16[32,8,1280]{2,1,0:T(8,128)(2,1)} %bitcast.34), calls=%async_computation.1 | async-start | bytes 1310720 | tf_op jit(solution)/shard_map/all_to_all | solution.py:239
  27.8 2.4 %shard_map.88 = (bf16[264,1024]{1,0:T(8,128)(2,1)}, bf16[240,1024]{1,0:T(8,128)(2,1)}) custom-call(bf16[504,1280]{1,0:T(8,128)(2,1)S(1)} %get-tuple-element.35.refs_0_.refs_1_, bf16[504,1280]{1,0:T(8,128)(2,1)S(1)} %get-tuple-element.35.refs_0_.refs_1_, bf16[256,1280]{1,0:T(8,128)(2,1)S(1)} %bitcast.14, bf16[256,1280]{1,0:T(8,128)(2,1)S(1)} %bitcast.15), custom_call_target="tpu_custom_call" | custom-call | flops 1006632960 | bytes 4000000 | tf_op jit(solution)/shard_map/pallas_call | solution.py:296
  30.1 11.2 %collective-permute-start = (bf16[264,1024]{1,0:T(8,128)(2,1)}, bf16[264,1024]{1,0:T(8,128)(2,1)}, u32[]{:S(2)}, u32[]{:S(2)}) collective-permute-start(bf16[264,1024]{1,0:T(8,128)(2,1)} %get-tuple-element.36), channel_id=1, source_target_pairs={{0,31},{1,0},{2,1},{3,2},{4,3},{5,4},{6,5},{7,6},{8,7},{9,8},{10,9... | collective-permute-start | bytes 1622024 | tf_op jit(solution)/shard_map/ppermute | solution.py:151
  41.4 1.9 %collective-permute-start.1 = (bf16[240,1024]{1,0:T(8,128)(2,1)}, bf16[240,1024]{1,0:T(8,128)(2,1)}, u32[]{:S(2)}, u32[]{:S(2)}) collective-permute-start(bf16[240,1024]{1,0:T(8,128)(2,1)} %get-tuple-element.37), channel_id=1, source_target_pairs={{0,1},{1,2},{2,3},{3,4},{4,5},{5,6},{6,7},{7,8},{8,9},{9,10},{10,1... | collective-permute-start | bytes 1474568 | tf_op jit(solution)/shard_map/ppermute | solution.py:151
  43.3 2.4 %shard_map.89 = (bf16[264,1024]{1,0:T(8,128)(2,1)}, bf16[240,1024]{1,0:T(8,128)(2,1)}) custom-call(bf16[504,1280]{1,0:T(8,128)(2,1)S(1)} %get-tuple-element.35.refs_0_.refs_1_, bf16[504,1280]{1,0:T(8,128)(2,1)S(1)} %get-tuple-element.35.refs_0_.refs_1_, bf16[256,1280]{1,0:T(8,128)(2,1)S(1)} %bitcast.20, bf16[256,1280]{1,0:T(8,128)(2,1)S(1)} %bitcast.21), custom_call_target="tpu_custom_call" | custom-call | flops 1006632960 | bytes 4000000 | tf_op jit(solution)/shard_map/pallas_call | solution.py:296
  45.7 1.9 %collective-permute-start.3 = (bf16[240,1024]{1,0:T(8,128)(2,1)}, bf16[240,1024]{1,0:T(8,128)(2,1)}, u32[]{:S(2)}, u32[]{:S(2)}) collective-permute-start(bf16[240,1024]{1,0:T(8,128)(2,1)} %get-tuple-element.43), channel_id=1, source_target_pairs={{0,1},{1,2},{2,3},{3,4},{4,5},{5,6},{6,7},{7,8},{8,9},{9,10},{10,1... | collective-permute-start | bytes 1474568 | tf_op jit(solution)/shard_map/ppermute | solution.py:151
  47.6 9.5 %collective-permute-start.2 = (bf16[264,1024]{1,0:T(8,128)(2,1)}, bf16[264,1024]{1,0:T(8,128)(2,1)S(1)}, u32[]{:S(2)}, u32[]{:S(2)}) collective-permute-start(bf16[264,1024]{1,0:T(8,128)(2,1)} %get-tuple-element.38), channel_id=1, source_target_pairs={{0,31},{1,0},{2,1},{3,2},{4,3},{5,4},{6,5},{7,6},{8,7},{9,8},{10,9... | collective-permute-start | bytes 1622024 | tf_op jit(solution)/shard_map/ppermute | solution.py:151
  57.1 2.8 %shard_map.87 = (f32[264,1024]{1,0:T(8,128)}, f32[264,1024]{1,0:T(8,128)}) custom-call(bf16[264,1280]{1,0:T(8,128)(2,1)S(1)} %get-tuple-element.27.refs_0_.refs_1_, bf16[264,1280]{1,0:T(8,128)(2,1)S(1)} %get-tuple-element.27.refs_0_.refs_1_, bf16[256,1280]{1,0:T(8,128)(2,1)S(1)} %bitcast.16, bf16[256,1280]{1,0:T(8,128)(2,1)S(1)} %bitcast.17, ...), custom_call_target="tpu_custom_call" | custom-call | flops 1006632960 | bytes 4000000 | tf_op jit(solution)/shard_map/pallas_call | solution.py:317
  59.9 7.4 %all-to-all-start.2 = ((bf16[32,8,2560]{2,1,0:T(8,128)(2,1)}), bf16[32,8,2560]{2,1,0:T(8,128)(2,1)S(1)}, u32[]{:S(2)}, u32[]{:S(2)}) async-start(bf16[32,8,2560]{2,1,0:T(8,128)(2,1)} %bitcast.9), calls=%async_computation.2 | async-start | bytes 2621440 | tf_op jit(solution)/shard_map/all_to_all | solution.py:239
  67.3 1.3 add_convert_fusion.3
  71.4 1.9 %collective-permute-start.8 = (bf16[24,2048]{1,0:T(8,128)(2,1)S(1)}, bf16[24,2048]{1,0:T(8,128)(2,1)S(1)}, u32[]{:S(2)}, u32[]{:S(2)}) collective-permute-start(bf16[24,2048]{1,0:T(8,128)(2,1)S(1)} %pad_maximum_fusion.1), channel_id=1, source_target_pairs={{0,3},{1,4},{2,5},{3,6},{4,7},{5,8},{6,9},{7,10},{8,11},{9,12},{10... | collective-permute-start | bytes 294920 | tf_op jit(solution)/shard_map/ppermute | solution.py:151
  73.4 6.9 %collective-permute-start.4 = (bf16[24,2048]{1,0:T(8,128)(2,1)S(1)}, bf16[24,2048]{1,0:T(8,128)(2,1)S(1)}, u32[]{:S(2)}, u32[]{:S(2)}) collective-permute-start(bf16[24,2048]{1,0:T(8,128)(2,1)S(1)} %pad_maximum_fusion), channel_id=1, source_target_pairs={{0,29},{1,30},{2,31},{3,0},{4,1},{5,2},{6,3},{7,4},{8,5},{9,6},{10... | collective-permute-start | bytes 294920 | tf_op jit(solution)/shard_map/ppermute | solution.py:151
  81.4 1.9 %collective-permute-start.9 = (bf16[24,2048]{1,0:T(8,128)(2,1)S(1)}, bf16[24,2048]{1,0:T(8,128)(2,1)S(1)}, u32[]{:S(2)}, u32[]{:S(2)}) collective-permute-start(bf16[24,2048]{1,0:T(8,128)(2,1)S(1)} %fusion.5), channel_id=1, source_target_pairs={{0,3},{1,4},{2,5},{3,6},{4,7},{5,8},{6,9},{7,10},{8,11},{9,12},{10... | collective-permute-start | bytes 294920 | tf_op jit(solution)/shard_map/ppermute | solution.py:151
  83.6 7.4 %collective-permute-start.5 = (bf16[24,2048]{1,0:T(8,128)(2,1)S(1)}, bf16[24,2048]{1,0:T(8,128)(2,1)S(1)}, u32[]{:S(2)}, u32[]{:S(2)}) collective-permute-start(bf16[24,2048]{1,0:T(8,128)(2,1)S(1)} %fusion), channel_id=1, source_target_pairs={{0,29},{1,30},{2,31},{3,0},{4,1},{5,2},{6,3},{7,4},{8,5},{9,6},{10... | collective-permute-start | bytes 294920 | tf_op jit(solution)/shard_map/ppermute | solution.py:151
  91.6 1.9 %collective-permute-start.10 = (bf16[24,2048]{1,0:T(8,128)(2,1)S(1)}, bf16[24,2048]{1,0:T(8,128)(2,1)S(1)}, u32[]{:S(2)}, u32[]{:S(2)}) collective-permute-start(bf16[24,2048]{1,0:T(8,128)(2,1)S(1)} %fusion.6), channel_id=1, source_target_pairs={{0,3},{1,4},{2,5},{3,6},{4,7},{5,8},{6,9},{7,10},{8,11},{9,12},{10... | collective-permute-start | bytes 294920 | tf_op jit(solution)/shard_map/ppermute | solution.py:151
  93.5 3.8 %collective-permute-done.5 = bf16[24,2048]{1,0:T(8,128)(2,1)S(1)} collective-permute-done((bf16[24,2048]{1,0:T(8,128)(2,1)S(1)}, bf16[24,2048]{1,0:T(8,128)(2,1)S(1)}, u32[]{:S(2)}, u32[]{:S(2)}) %collective-permute-start.5) | collective-permute-done | bytes 98336 | tf_op jit(solution)/shard_map/ppermute | solution.py:151
  97.3 7.5 %collective-permute-start.6 = (bf16[24,2048]{1,0:T(8,128)(2,1)S(1)}, bf16[24,2048]{1,0:T(8,128)(2,1)S(1)}, u32[]{:S(2)}, u32[]{:S(2)}) collective-permute-start(bf16[24,2048]{1,0:T(8,128)(2,1)S(1)} %fusion.1), channel_id=1, source_target_pairs={{0,29},{1,30},{2,31},{3,0},{4,1},{5,2},{6,3},{7,4},{8,5},{9,6},{10... | collective-permute-start | bytes 294920 | tf_op jit(solution)/shard_map/ppermute | solution.py:151
  104.8 1.9 %collective-permute-start.11 = (bf16[24,2048]{1,0:T(8,128)(2,1)S(1)}, bf16[24,2048]{1,0:T(8,128)(2,1)S(1)}, u32[]{:S(2)}, u32[]{:S(2)}) collective-permute-start(bf16[24,2048]{1,0:T(8,128)(2,1)S(1)} %fusion.7), channel_id=1, source_target_pairs={{0,3},{1,4},{2,5},{3,6},{4,7},{5,8},{6,9},{7,10},{8,11},{9,12},{10... | collective-permute-start | bytes 294920 | tf_op jit(solution)/shard_map/ppermute | solution.py:151
  106.7 2.4 %collective-permute-done.6 = bf16[24,2048]{1,0:T(8,128)(2,1)S(1)} collective-permute-done((bf16[24,2048]{1,0:T(8,128)(2,1)S(1)}, bf16[24,2048]{1,0:T(8,128)(2,1)S(1)}, u32[]{:S(2)}, u32[]{:S(2)}) %collective-permute-start.6) | collective-permute-done | bytes 98336 | tf_op jit(solution)/shard_map/ppermute | solution.py:151
  109.8 7.5 %collective-permute-start.7 = (bf16[24,2048]{1,0:T(8,128)(2,1)}, bf16[24,2048]{1,0:T(8,128)(2,1)}, u32[]{:S(2)}, u32[]{:S(2)}) collective-permute-start(bf16[24,2048]{1,0:T(8,128)(2,1)} %fusion.2), channel_id=1, source_target_pairs={{0,29},{1,30},{2,31},{3,0},{4,1},{5,2},{6,3},{7,4},{8,5},{9,6},{10... | collective-permute-start | bytes 294920 | tf_op jit(solution)/shard_map/ppermute | solution.py:151
  118.0 1.9 %collective-permute-start.12 = (bf16[24,2048]{1,0:T(8,128)(2,1)}, bf16[24,2048]{1,0:T(8,128)(2,1)}, u32[]{:S(2)}, u32[]{:S(2)}) collective-permute-start(bf16[24,2048]{1,0:T(8,128)(2,1)} %fusion.8), channel_id=1, source_target_pairs={{0,3},{1,4},{2,5},{3,6},{4,7},{5,8},{6,9},{7,10},{8,11},{9,12},{10... | collective-permute-start | bytes 294920 | tf_op jit(solution)/shard_map/ppermute | solution.py:151
  119.9 1.8 %shard_map.90 = (bf16[128,2048]{1,0:T(8,128)(2,1)}, f32[2,128]{1,0:T(2,128)}) custom-call(s32[2,128]{1,0:T(2,128)S(1)} %bitcast.31, f32[2,128]{1,0:T(2,128)S(1)} %bitcast.33, bf16[128,2048]{1,0:T(8,128)(2,1)S(1)} %copy-done.2, bf16[256,2560]{1,0:T(8,128)(2,1)S(1)} %bitcast.29), custom_call_target="tpu_custom_call" | custom-call | flops 536870912 | bytes 3000000 | tf_op jit(solution)/shard_map/pallas_call | solution.py:342
  122.7 9.1 %collective-permute-start.13 = (bf16[24,2048]{1,0:T(8,128)(2,1)S(1)}, bf16[24,2048]{1,0:T(8,128)(2,1)S(1)}, u32[]{:S(2)}, u32[]{:S(2)}) collective-permute-start(bf16[24,2048]{1,0:T(8,128)(2,1)S(1)} %fusion.9), channel_id=1, source_target_pairs={{0,29},{1,30},{2,31},{3,0},{4,1},{5,2},{6,3},{7,4},{8,5},{9,6},{10... | collective-permute-start | bytes 294920 | tf_op jit(solution)/shard_map/ppermute | solution.py:151
  131.8 1.9 %copy-done.1 = bf16[1,768,2048]{2,1,0:T(8,128)(2,1)S(1)} copy-done((bf16[1,768,2048]{2,1,0:T(8,128)(2,1)S(1)}, bf16[1,768,2048]{2,1,0:T(8,128)(2,1)}, u32[]{:S(2)}) %copy-start.1) | copy-done | bytes 3145752
  133.7 5.1 %shard_map.91 = bf16[320,768]{1,0:T(8,128)(2,1)} custom-call(bf16[256,1280]{1,0:T(8,128)(2,1)S(1)} %bitcast.18, bf16[256,1280]{1,0:T(8,128)(2,1)S(1)} %bitcast.19, bf16[768,2048]{1,0:T(8,128)(2,1)S(1)} %bitcast.27, bf16[256,1280]{1,0:T(8,128)(2,1)S(1)} %bitcast.24, bf16[256,1280]{1,0:T(8,128)(2,1)S(1)} %bitcast.25, bf16[768,2048]{1,0:T(8,128)(2,1)S(1)} %bitcast.28), custom_call_target="tpu_custom_call" | custom-call | flops 2013265920 | bytes 6000000 | tf_op jit(solution)/shard_map/pallas_call | solution.py:329
  138.8 1.6 %fusion.4 = f32[1,24,2048]{2,1,0:T(8,128)} fusion(f32[24,1024]{1,0:T(8,128)S(1)} %get-tuple-element.61, f32[24,1024]{1,0:T(8,128)S(1)} %get-tuple-element.55, bf16[24,2048]{1,0:T(8,128)(2,1)S(1)} %collective-permute-done.13, bf16[24,2048]{1,0:T(8,128)(2,1)} %collective-permute-done.12), kind=kLoop, calls=%fused_computation.8 | loop fusion | flops 245760 | bytes 589824 | tf_op jit(solution)/shard_map/broadcast_in_dim | solution.py:355
  (42 shorter events, 7.0 us)
Async XLA Ops:
  0.6 10.6 %copy-start.3 = (bf16[320,768]{1,0:T(8,128)(2,1)S(1)}, bf16[320,768]{1,0:T(8,128)(2,1)}, u32[]{:S(2)}) copy-start(bf16[320,768]{1,0:T(8,128)(2,1)} %hidden_ref.3) | copy-start | bytes 1474564
  3.5 18.5 %all-to-all-start = ((bf16[32,8,1280]{2,1,0:T(8,128)(2,1)}), bf16[32,8,1280]{2,1,0:T(8,128)(2,1)S(1)}, u32[]{:S(2)}, u32[]{:S(2)}) async-start(bf16[32,8,1280]{2,1,0:T(8,128)(2,1)} %bitcast.35), calls=%async_computation | async-start | bytes 1310720 | tf_op jit(solution)/shard_map/all_to_all | solution.py:239
  13.0 1.9 %copy-start = (bf16[1,768,2048]{2,1,0:T(8,128)(2,1)S(1)}, bf16[1,768,2048]{2,1,0:T(8,128)(2,1)}, u32[]{:S(2)}) copy-start(bf16[1,768,2048]{2,1,0:T(8,128)(2,1)} %param.9) | copy-start | bytes 9437188
  22.0 21.3 %all-to-all-start.1 = ((bf16[32,8,1280]{2,1,0:T(8,128)(2,1)}), bf16[32,8,1280]{2,1,0:T(8,128)(2,1)S(1)}, u32[]{:S(2)}, u32[]{:S(2)}) async-start(bf16[32,8,1280]{2,1,0:T(8,128)(2,1)} %bitcast.34), calls=%async_computation.1 | async-start | bytes 1310720 | tf_op jit(solution)/shard_map/all_to_all | solution.py:239
  30.1 29.8 %collective-permute-start = (bf16[264,1024]{1,0:T(8,128)(2,1)}, bf16[264,1024]{1,0:T(8,128)(2,1)}, u32[]{:S(2)}, u32[]{:S(2)}) collective-permute-start(bf16[264,1024]{1,0:T(8,128)(2,1)} %get-tuple-element.36), channel_id=1, source_target_pairs={{0,31},{1,0},{2,1},{3,2},{4,3},{5,4},{6,5},{7,6},{8,7},{9,8},{10,9... | collective-permute-start | bytes 1622024 | tf_op jit(solution)/shard_map/ppermute | solution.py:151
  41.4 18.6 %collective-permute-start.1 = (bf16[240,1024]{1,0:T(8,128)(2,1)}, bf16[240,1024]{1,0:T(8,128)(2,1)}, u32[]{:S(2)}, u32[]{:S(2)}) collective-permute-start(bf16[240,1024]{1,0:T(8,128)(2,1)} %get-tuple-element.37), channel_id=1, source_target_pairs={{0,1},{1,2},{2,3},{3,4},{4,5},{5,6},{6,7},{7,8},{8,9},{9,10},{10,1... | collective-permute-start | bytes 1474568 | tf_op jit(solution)/shard_map/ppermute | solution.py:151
  45.7 24.5 %collective-permute-start.3 = (bf16[240,1024]{1,0:T(8,128)(2,1)}, bf16[240,1024]{1,0:T(8,128)(2,1)}, u32[]{:S(2)}, u32[]{:S(2)}) collective-permute-start(bf16[240,1024]{1,0:T(8,128)(2,1)} %get-tuple-element.43), channel_id=1, source_target_pairs={{0,1},{1,2},{2,3},{3,4},{4,5},{5,6},{6,7},{7,8},{8,9},{9,10},{10,1... | collective-permute-start | bytes 1474568 | tf_op jit(solution)/shard_map/ppermute | solution.py:151
  47.6 22.6 %collective-permute-start.2 = (bf16[264,1024]{1,0:T(8,128)(2,1)}, bf16[264,1024]{1,0:T(8,128)(2,1)S(1)}, u32[]{:S(2)}, u32[]{:S(2)}) collective-permute-start(bf16[264,1024]{1,0:T(8,128)(2,1)} %get-tuple-element.38), channel_id=1, source_target_pairs={{0,31},{1,0},{2,1},{3,2},{4,3},{5,4},{6,5},{7,6},{8,7},{9,8},{10,9... | collective-permute-start | bytes 1622024 | tf_op jit(solution)/shard_map/ppermute | solution.py:151
  59.9 60.0 %all-to-all-start.2 = ((bf16[32,8,2560]{2,1,0:T(8,128)(2,1)}), bf16[32,8,2560]{2,1,0:T(8,128)(2,1)S(1)}, u32[]{:S(2)}, u32[]{:S(2)}) async-start(bf16[32,8,2560]{2,1,0:T(8,128)(2,1)} %bitcast.9), calls=%async_computation.2 | async-start | bytes 2621440 | tf_op jit(solution)/shard_map/all_to_all | solution.py:239
  67.3 1.6 %copy-start.7 = (f32[264,1024]{1,0:T(8,128)S(1)}, f32[264,1024]{1,0:T(8,128)}, u32[]{:S(2)}) copy-start(f32[264,1024]{1,0:T(8,128)} %get-tuple-element.34) | copy-start | bytes 3244036
  68.9 1.5 %copy-start.6 = (f32[264,1024]{1,0:T(8,128)S(1)}, f32[264,1024]{1,0:T(8,128)}, u32[]{:S(2)}) copy-start(f32[264,1024]{1,0:T(8,128)} %get-tuple-element.42) | copy-start | bytes 3244036
  71.4 9.9 %collective-permute-start.8 = (bf16[24,2048]{1,0:T(8,128)(2,1)S(1)}, bf16[24,2048]{1,0:T(8,128)(2,1)S(1)}, u32[]{:S(2)}, u32[]{:S(2)}) collective-permute-start(bf16[24,2048]{1,0:T(8,128)(2,1)S(1)} %pad_maximum_fusion.1), channel_id=1, source_target_pairs={{0,3},{1,4},{2,5},{3,6},{4,7},{5,8},{6,9},{7,10},{8,11},{9,12},{10... | collective-permute-start | bytes 294920 | tf_op jit(solution)/shard_map/ppermute | solution.py:151
  73.4 10.2 %collective-permute-start.4 = (bf16[24,2048]{1,0:T(8,128)(2,1)S(1)}, bf16[24,2048]{1,0:T(8,128)(2,1)S(1)}, u32[]{:S(2)}, u32[]{:S(2)}) collective-permute-start(bf16[24,2048]{1,0:T(8,128)(2,1)S(1)} %pad_maximum_fusion), channel_id=1, source_target_pairs={{0,29},{1,30},{2,31},{3,0},{4,1},{5,2},{6,3},{7,4},{8,5},{9,6},{10... | collective-permute-start | bytes 294920 | tf_op jit(solution)/shard_map/ppermute | solution.py:151
  81.4 10.2 %collective-permute-start.9 = (bf16[24,2048]{1,0:T(8,128)(2,1)S(1)}, bf16[24,2048]{1,0:T(8,128)(2,1)S(1)}, u32[]{:S(2)}, u32[]{:S(2)}) collective-permute-start(bf16[24,2048]{1,0:T(8,128)(2,1)S(1)} %fusion.5), channel_id=1, source_target_pairs={{0,3},{1,4},{2,5},{3,6},{4,7},{5,8},{6,9},{7,10},{8,11},{9,12},{10... | collective-permute-start | bytes 294920 | tf_op jit(solution)/shard_map/ppermute | solution.py:151
  83.6 36.3 %copy-start.2 = (bf16[128,2048]{1,0:T(8,128)(2,1)S(1)}, bf16[128,2048]{1,0:T(8,128)(2,1)}, u32[]{:S(2)}) copy-start(bf16[128,2048]{1,0:T(8,128)(2,1)} %cot_ref.3) | copy-start | bytes 1572868
  83.6 36.3 %copy-start.4 = (s32[128,2]{0,1:T(2,128)S(1)}, s32[128,2]{0,1:T(2,128)}, u32[]{:S(2)}) copy-start(s32[128,2]{0,1:T(2,128)} %param.6) | copy-start | bytes 3076
  83.6 36.3 %copy-start.5 = (f32[128,2]{0,1:T(2,128)S(1)}, f32[128,2]{0,1:T(2,128)}, u32[]{:S(2)}) copy-start(f32[128,2]{0,1:T(2,128)} %param.7) | copy-start | bytes 3076
  83.6 13.7 %collective-permute-start.5 = (bf16[24,2048]{1,0:T(8,128)(2,1)S(1)}, bf16[24,2048]{1,0:T(8,128)(2,1)S(1)}, u32[]{:S(2)}, u32[]{:S(2)}) collective-permute-start(bf16[24,2048]{1,0:T(8,128)(2,1)S(1)} %fusion), channel_id=1, source_target_pairs={{0,29},{1,30},{2,31},{3,0},{4,1},{5,2},{6,3},{7,4},{8,5},{9,6},{10... | collective-permute-start | bytes 294920 | tf_op jit(solution)/shard_map/ppermute | solution.py:151
  91.6 13.2 %collective-permute-start.10 = (bf16[24,2048]{1,0:T(8,128)(2,1)S(1)}, bf16[24,2048]{1,0:T(8,128)(2,1)S(1)}, u32[]{:S(2)}, u32[]{:S(2)}) collective-permute-start(bf16[24,2048]{1,0:T(8,128)(2,1)S(1)} %fusion.6), channel_id=1, source_target_pairs={{0,3},{1,4},{2,5},{3,6},{4,7},{5,8},{6,9},{7,10},{8,11},{9,12},{10... | collective-permute-start | bytes 294920 | tf_op jit(solution)/shard_map/ppermute | solution.py:151
  97.3 11.8 %collective-permute-start.6 = (bf16[24,2048]{1,0:T(8,128)(2,1)S(1)}, bf16[24,2048]{1,0:T(8,128)(2,1)S(1)}, u32[]{:S(2)}, u32[]{:S(2)}) collective-permute-start(bf16[24,2048]{1,0:T(8,128)(2,1)S(1)} %fusion.1), channel_id=1, source_target_pairs={{0,29},{1,30},{2,31},{3,0},{4,1},{5,2},{6,3},{7,4},{8,5},{9,6},{10... | collective-permute-start | bytes 294920 | tf_op jit(solution)/shard_map/ppermute | solution.py:151
  104.8 12.5 %collective-permute-start.11 = (bf16[24,2048]{1,0:T(8,128)(2,1)S(1)}, bf16[24,2048]{1,0:T(8,128)(2,1)S(1)}, u32[]{:S(2)}, u32[]{:S(2)}) collective-permute-start(bf16[24,2048]{1,0:T(8,128)(2,1)S(1)} %fusion.7), channel_id=1, source_target_pairs={{0,3},{1,4},{2,5},{3,6},{4,7},{5,8},{6,9},{7,10},{8,11},{9,12},{10... | collective-permute-start | bytes 294920 | tf_op jit(solution)/shard_map/ppermute | solution.py:151
  109.8 12.0 %collective-permute-start.7 = (bf16[24,2048]{1,0:T(8,128)(2,1)}, bf16[24,2048]{1,0:T(8,128)(2,1)}, u32[]{:S(2)}, u32[]{:S(2)}) collective-permute-start(bf16[24,2048]{1,0:T(8,128)(2,1)} %fusion.2), channel_id=1, source_target_pairs={{0,29},{1,30},{2,31},{3,0},{4,1},{5,2},{6,3},{7,4},{8,5},{9,6},{10... | collective-permute-start | bytes 294920 | tf_op jit(solution)/shard_map/ppermute | solution.py:151
  118.0 20.8 %collective-permute-start.12 = (bf16[24,2048]{1,0:T(8,128)(2,1)}, bf16[24,2048]{1,0:T(8,128)(2,1)}, u32[]{:S(2)}, u32[]{:S(2)}) collective-permute-start(bf16[24,2048]{1,0:T(8,128)(2,1)} %fusion.8), channel_id=1, source_target_pairs={{0,3},{1,4},{2,5},{3,6},{4,7},{5,8},{6,9},{7,10},{8,11},{9,12},{10... | collective-permute-start | bytes 294920 | tf_op jit(solution)/shard_map/ppermute | solution.py:151
  122.7 16.1 %collective-permute-start.13 = (bf16[24,2048]{1,0:T(8,128)(2,1)S(1)}, bf16[24,2048]{1,0:T(8,128)(2,1)S(1)}, u32[]{:S(2)}, u32[]{:S(2)}) collective-permute-start(bf16[24,2048]{1,0:T(8,128)(2,1)S(1)} %fusion.9), channel_id=1, source_target_pairs={{0,29},{1,30},{2,31},{3,0},{4,1},{5,2},{6,3},{7,4},{8,5},{9,6},{10... | collective-permute-start | bytes 294920 | tf_op jit(solution)/shard_map/ppermute | solution.py:151
  131.8 1.9 %copy-start.1 = (bf16[1,768,2048]{2,1,0:T(8,128)(2,1)S(1)}, bf16[1,768,2048]{2,1,0:T(8,128)(2,1)}, u32[]{:S(2)}) copy-start(bf16[1,768,2048]{2,1,0:T(8,128)(2,1)} %param.9) | copy-start | bytes 9437188

commit v8 on v7

--- a/solution.py
+++ b/solution.py
@@ -331,6 +331,7 @@
         jax.ShapeDtypeStruct((rows, inner), BF16),
         2 * product,
         6 * 10**6,
+        56 * 1024 * 1024,
         grid=(QUARTERS,),
         in_specs=[half_low, half_left, block(inner, lambda q: q)]
         + [half_low, half_left, block(inner, lambda q: QUARTERS + q)],

time: 142 us -> 140 us (0.986)
  the two profiles are of different devices: /device:TPU:36 before, /device:TPU:64 now
where the time goes in v8:
time: 140 us; the launch traced here: 139 us
  starting transfers between devices  84.9 us (61%)
  Pallas kernels  23.6 us (17%)
  waiting for transfers between devices  20.9 us (15%)
  other arithmetic  5.54 us (4%)
  local copies, waits for them, and re-layouts  3.21 us (2%)
    ppermute x14, starting transfers between devices, shift(): return lax.ppermute(block, ('ep', 'dp'), pairs)  65.9 us
    all_to_all x3, starting transfers between devices, exchange(): lax.all_to_all(blocks, 'ep', split_axis=0, concat_axis=0, tiled=True)  19 us
    ppermute x14, waiting for transfers between devices, shift(): return lax.ppermute(block, ('ep', 'dp'), pairs)  12.1 us
    all_to_all x3, waiting for transfers between devices, exchange(): lax.all_to_all(blocks, 'ep', split_axis=0, concat_axis=0, tiled=True)  8.76 us
    pallas_call x1, Pallas kernels, shards(): call(hidden_grad_kernel, jax.ShapeDtypeStruct((rows, inner), BF16), 2 * p...  6.28 us
    pallas_call x2, Pallas kernels, sent(): call(lambda *refs: sent_kernel(scale, *refs), (jax.ShapeDtypeStruct((11 *...  4.74 us
    unnamed x20, local copies, waits for them, and re-layouts  3.21 us
    pallas_call x1, Pallas kernels, shards(): call(expert_kernel, packed, 2 * product, 6 * 10 ** 6, grid=(QUARTERS,), i...  3.19 us
  transfers between devices with their start and end apart: 17, of which 6 were waited for; matrix products, arithmetic and copies ran while one was open for 3% of the time, Pallas kernels for 15%

profile of v8, /device:TPU:64, one launch (start us, length us, event | category | flops | bytes accessed | tf_op | source)
XLA Modules:
  0.0 139.1 jit_solution(10213180467737458584)
XLA Ops:
  0.6 2.9 %shard_map.86 = (bf16[256,1280]{1,0:T(8,128)(2,1)}, bf16[256,1280]{1,0:T(8,128)(2,1)}) custom-call(s32[2,128]{1,0:T(2,128)} %bitcast.31, f32[2,128]{1,0:T(2,128)} %bitcast.33, bf16[128,2048]{1,0:T(8,128)(2,1)} %cot_ref.3), custom_call_target="tpu_custom_call" | custom-call | flops 268435456 | bytes 2000000 | tf_op jit(solution)/shard_map/pallas_call | solution.py:259
  3.5 7.3 %all-to-all-start = ((bf16[32,8,1280]{2,1,0:T(8,128)(2,1)}), bf16[32,8,1280]{2,1,0:T(8,128)(2,1)S(1)}, u32[]{:S(2)}, u32[]{:S(2)}) async-start(bf16[32,8,1280]{2,1,0:T(8,128)(2,1)} %bitcast.36), calls=%async_computation | async-start | bytes 1310720 | tf_op jit(solution)/shard_map/all_to_all | solution.py:239
  10.9 1.8 %shard_map.84 = (bf16[504,1280]{1,0:T(8,128)(2,1)S(1)}, bf16[264,1280]{1,0:T(8,128)(2,1)S(1)}) custom-call(s32[2]{0:T(128)S(1)} %pad_add_fusion.place_ref, bf16[320,768]{1,0:T(8,128)(2,1)S(1)} %copy-done.5), custom_call_target="tpu_custom_call" | custom-call | flops 754974720 | bytes 2000000 | tf_op jit(solution)/shard_map/pallas_call | solution.py:268
  12.7 1.9 %copy-done.2 = bf16[1,768,2048]{2,1,0:T(8,128)(2,1)S(1)} copy-done((bf16[1,768,2048]{2,1,0:T(8,128)(2,1)S(1)}, bf16[1,768,2048]{2,1,0:T(8,128)(2,1)}, u32[]{:S(2)}) %copy-start.2) | copy-done | bytes 3145752
  14.6 3.2 %shard_map.85 = bf16[256,2560]{1,0:T(8,128)(2,1)S(1)} custom-call(bf16[320,768]{1,0:T(8,128)(2,1)S(1)} %copy-done.5, bf16[768,2048]{1,0:T(8,128)(2,1)S(1)} %bitcast.28), custom_call_target="tpu_custom_call" | custom-call | flops 2013265920 | bytes 6000000 | tf_op jit(solution)/shard_map/pallas_call | solution.py:278
  18.9 4.5 %all-to-all-done = bf16[32,8,1280]{2,1,0:T(8,128)(2,1)S(1)} async-done(((bf16[32,8,1280]{2,1,0:T(8,128)(2,1)}), bf16[32,8,1280]{2,1,0:T(8,128)(2,1)S(1)}, u32[]{:S(2)}, u32[]{:S(2)}) %all-to-all-start) | async-done | bytes 655392 | tf_op jit(solution)/shard_map/all_to_all | solution.py:239
  23.4 4.1 %all-to-all-start.1 = ((bf16[32,8,1280]{2,1,0:T(8,128)(2,1)}), bf16[32,8,1280]{2,1,0:T(8,128)(2,1)S(1)}, u32[]{:S(2)}, u32[]{:S(2)}) async-start(bf16[32,8,1280]{2,1,0:T(8,128)(2,1)} %bitcast.35), calls=%async_computation.1 | async-start | bytes 1310720 | tf_op jit(solution)/shard_map/all_to_all | solution.py:239
  27.5 2.4 %shard_map.88 = (bf16[264,1024]{1,0:T(8,128)(2,1)}, bf16[240,1024]{1,0:T(8,128)(2,1)}) custom-call(bf16[504,1280]{1,0:T(8,128)(2,1)S(1)} %get-tuple-element.35.refs_0_.refs_1_, bf16[504,1280]{1,0:T(8,128)(2,1)S(1)} %get-tuple-element.35.refs_0_.refs_1_, bf16[256,1280]{1,0:T(8,128)(2,1)S(1)} %bitcast.14, bf16[256,1280]{1,0:T(8,128)(2,1)S(1)} %bitcast.15), custom_call_target="tpu_custom_call" | custom-call | flops 1006632960 | bytes 4000000 | tf_op jit(solution)/shard_map/pallas_call | solution.py:296
  29.9 2.0 %collective-permute-start = (bf16[264,1024]{1,0:T(8,128)(2,1)}, bf16[264,1024]{1,0:T(8,128)(2,1)}, u32[]{:S(2)}, u32[]{:S(2)}) collective-permute-start(bf16[264,1024]{1,0:T(8,128)(2,1)} %get-tuple-element.36), channel_id=1, source_target_pairs={{0,31},{1,0},{2,1},{3,2},{4,3},{5,4},{6,5},{7,6},{8,7},{9,8},{10,9... | collective-permute-start | bytes 1622024 | tf_op jit(solution)/shard_map/ppermute | solution.py:151
  31.9 3.8 %collective-permute-start.1 = (bf16[240,1024]{1,0:T(8,128)(2,1)}, bf16[240,1024]{1,0:T(8,128)(2,1)}, u32[]{:S(2)}, u32[]{:S(2)}) collective-permute-start(bf16[240,1024]{1,0:T(8,128)(2,1)} %get-tuple-element.37), channel_id=1, source_target_pairs={{0,1},{1,2},{2,3},{3,4},{4,5},{5,6},{6,7},{7,8},{8,9},{9,10},{10,1... | collective-permute-start | bytes 1474568 | tf_op jit(solution)/shard_map/ppermute | solution.py:151
  35.7 4.3 %all-to-all-done.1 = bf16[32,8,1280]{2,1,0:T(8,128)(2,1)S(1)} async-done(((bf16[32,8,1280]{2,1,0:T(8,128)(2,1)}), bf16[32,8,1280]{2,1,0:T(8,128)(2,1)S(1)}, u32[]{:S(2)}, u32[]{:S(2)}) %all-to-all-start.1) | async-done | bytes 655392 | tf_op jit(solution)/shard_map/all_to_all | solution.py:239
  40.0 2.4 %shard_map.89 = (bf16[264,1024]{1,0:T(8,128)(2,1)}, bf16[240,1024]{1,0:T(8,128)(2,1)}) custom-call(bf16[504,1280]{1,0:T(8,128)(2,1)S(1)} %get-tuple-element.35.refs_0_.refs_1_, bf16[504,1280]{1,0:T(8,128)(2,1)S(1)} %get-tuple-element.35.refs_0_.refs_1_, bf16[256,1280]{1,0:T(8,128)(2,1)S(1)} %bitcast.20, bf16[256,1280]{1,0:T(8,128)(2,1)S(1)} %bitcast.21), custom_call_target="tpu_custom_call" | custom-call | flops 1006632960 | bytes 4000000 | tf_op jit(solution)/shard_map/pallas_call | solution.py:296
  42.4 3.8 %collective-permute-start.3 = (bf16[240,1024]{1,0:T(8,128)(2,1)}, bf16[240,1024]{1,0:T(8,128)(2,1)}, u32[]{:S(2)}, u32[]{:S(2)}) collective-permute-start(bf16[240,1024]{1,0:T(8,128)(2,1)} %get-tuple-element.43), channel_id=1, source_target_pairs={{0,1},{1,2},{2,3},{3,4},{4,5},{5,6},{6,7},{7,8},{8,9},{9,10},{10,1... | collective-permute-start | bytes 1474568 | tf_op jit(solution)/shard_map/ppermute | solution.py:151
  46.2 3.1 %collective-permute-start.2 = (bf16[264,1024]{1,0:T(8,128)(2,1)}, bf16[264,1024]{1,0:T(8,128)(2,1)}, u32[]{:S(2)}, u32[]{:S(2)}) collective-permute-start(bf16[264,1024]{1,0:T(8,128)(2,1)} %get-tuple-element.38), channel_id=1, source_target_pairs={{0,31},{1,0},{2,1},{3,2},{4,3},{5,4},{6,5},{7,6},{8,7},{9,8},{10,9... | collective-permute-start | bytes 1622024 | tf_op jit(solution)/shard_map/ppermute | solution.py:151
  49.4 2.8 %shard_map.87 = (f32[264,1024]{1,0:T(8,128)}, f32[264,1024]{1,0:T(8,128)}) custom-call(bf16[264,1280]{1,0:T(8,128)(2,1)S(1)} %get-tuple-element.27.refs_0_.refs_1_, bf16[264,1280]{1,0:T(8,128)(2,1)S(1)} %get-tuple-element.27.refs_0_.refs_1_, bf16[256,1280]{1,0:T(8,128)(2,1)S(1)} %bitcast.16, bf16[256,1280]{1,0:T(8,128)(2,1)S(1)} %bitcast.17, ...), custom_call_target="tpu_custom_call" | custom-call | flops 1006632960 | bytes 4000000 | tf_op jit(solution)/shard_map/pallas_call | solution.py:317
  52.2 7.5 %all-to-all-start.2 = ((bf16[32,8,2560]{2,1,0:T(8,128)(2,1)}), bf16[32,8,2560]{2,1,0:T(8,128)(2,1)S(1)}, u32[]{:S(2)}, u32[]{:S(2)}) async-start(bf16[32,8,2560]{2,1,0:T(8,128)(2,1)} %bitcast.29), calls=%async_computation.2 | async-start | bytes 2621440 | tf_op jit(solution)/shard_map/all_to_all | solution.py:239
  60.9 1.3 convert_add_fusion.9
  63.4 4.5 %collective-permute-start.8 = (bf16[24,2048]{1,0:T(8,128)(2,1)S(1)}, bf16[24,2048]{1,0:T(8,128)(2,1)S(1)}, u32[]{:S(2)}, u32[]{:S(2)}) collective-permute-start(bf16[24,2048]{1,0:T(8,128)(2,1)S(1)} %pad_maximum_fusion.1), channel_id=1, source_target_pairs={{0,3},{1,4},{2,5},{3,6},{4,7},{5,8},{6,9},{7,10},{8,11},{9,12},{10... | collective-permute-start | bytes 294920 | tf_op jit(solution)/shard_map/ppermute | solution.py:151
  68.0 13.0 %collective-permute-start.4 = (bf16[24,2048]{1,0:T(8,128)(2,1)S(1)}, bf16[24,2048]{1,0:T(8,128)(2,1)S(1)}, u32[]{:S(2)}, u32[]{:S(2)}) collective-permute-start(bf16[24,2048]{1,0:T(8,128)(2,1)S(1)} %pad_maximum_fusion), channel_id=1, source_target_pairs={{0,29},{1,30},{2,31},{3,0},{4,1},{5,2},{6,3},{7,4},{8,5},{9,6},{10... | collective-permute-start | bytes 294920 | tf_op jit(solution)/shard_map/ppermute | solution.py:151
  83.1 1.9 %collective-permute-start.9 = (bf16[24,2048]{1,0:T(8,128)(2,1)S(1)}, bf16[24,2048]{1,0:T(8,128)(2,1)S(1)}, u32[]{:S(2)}, u32[]{:S(2)}) collective-permute-start(bf16[24,2048]{1,0:T(8,128)(2,1)S(1)} %fusion.5), channel_id=1, source_target_pairs={{0,3},{1,4},{2,5},{3,6},{4,7},{5,8},{6,9},{7,10},{8,11},{9,12},{10... | collective-permute-start | bytes 294920 | tf_op jit(solution)/shard_map/ppermute | solution.py:151
  85.1 7.1 %collective-permute-start.5 = (bf16[24,2048]{1,0:T(8,128)(2,1)S(1)}, bf16[24,2048]{1,0:T(8,128)(2,1)S(1)}, u32[]{:S(2)}, u32[]{:S(2)}) collective-permute-start(bf16[24,2048]{1,0:T(8,128)(2,1)S(1)} %fusion), channel_id=1, source_target_pairs={{0,29},{1,30},{2,31},{3,0},{4,1},{5,2},{6,3},{7,4},{8,5},{9,6},{10... | collective-permute-start | bytes 294920 | tf_op jit(solution)/shard_map/ppermute | solution.py:151
  92.2 2.6 %collective-permute-done.9 = bf16[24,2048]{1,0:T(8,128)(2,1)S(1)} collective-permute-done((bf16[24,2048]{1,0:T(8,128)(2,1)S(1)}, bf16[24,2048]{1,0:T(8,128)(2,1)S(1)}, u32[]{:S(2)}, u32[]{:S(2)}) %collective-permute-start.9) | collective-permute-done | bytes 98336 | tf_op jit(solution)/shard_map/ppermute | solution.py:151
  94.8 1.9 %collective-permute-start.10 = (bf16[24,2048]{1,0:T(8,128)(2,1)S(1)}, bf16[24,2048]{1,0:T(8,128)(2,1)S(1)}, u32[]{:S(2)}, u32[]{:S(2)}) collective-permute-start(bf16[24,2048]{1,0:T(8,128)(2,1)S(1)} %fusion.6), channel_id=1, source_target_pairs={{0,3},{1,4},{2,5},{3,6},{4,7},{5,8},{6,9},{7,10},{8,11},{9,12},{10... | collective-permute-start | bytes 294920 | tf_op jit(solution)/shard_map/ppermute | solution.py:151
  96.8 7.1 %collective-permute-start.6 = (bf16[24,2048]{1,0:T(8,128)(2,1)S(1)}, bf16[24,2048]{1,0:T(8,128)(2,1)S(1)}, u32[]{:S(2)}, u32[]{:S(2)}) collective-permute-start(bf16[24,2048]{1,0:T(8,128)(2,1)S(1)} %fusion.1), channel_id=1, source_target_pairs={{0,29},{1,30},{2,31},{3,0},{4,1},{5,2},{6,3},{7,4},{8,5},{9,6},{10... | collective-permute-start | bytes 294920 | tf_op jit(solution)/shard_map/ppermute | solution.py:151
  103.8 4.7 %collective-permute-done.10 = bf16[24,2048]{1,0:T(8,128)(2,1)S(1)} collective-permute-done((bf16[24,2048]{1,0:T(8,128)(2,1)S(1)}, bf16[24,2048]{1,0:T(8,128)(2,1)S(1)}, u32[]{:S(2)}, u32[]{:S(2)}) %collective-permute-start.10) | collective-permute-done | bytes 98336 | tf_op jit(solution)/shard_map/ppermute | solution.py:151
  108.6 1.9 %collective-permute-start.11 = (bf16[24,2048]{1,0:T(8,128)(2,1)S(1)}, bf16[24,2048]{1,0:T(8,128)(2,1)S(1)}, u32[]{:S(2)}, u32[]{:S(2)}) collective-permute-start(bf16[24,2048]{1,0:T(8,128)(2,1)S(1)} %fusion.7), channel_id=1, source_target_pairs={{0,3},{1,4},{2,5},{3,6},{4,7},{5,8},{6,9},{7,10},{8,11},{9,12},{10... | collective-permute-start | bytes 294920 | tf_op jit(solution)/shard_map/ppermute | solution.py:151
  110.6 6.9 %collective-permute-start.7 = (bf16[24,2048]{1,0:T(8,128)(2,1)S(1)}, bf16[24,2048]{1,0:T(8,128)(2,1)S(1)}, u32[]{:S(2)}, u32[]{:S(2)}) collective-permute-start(bf16[24,2048]{1,0:T(8,128)(2,1)S(1)} %fusion.2), channel_id=1, source_target_pairs={{0,29},{1,30},{2,31},{3,0},{4,1},{5,2},{6,3},{7,4},{8,5},{9,6},{10... | collective-permute-start | bytes 294920 | tf_op jit(solution)/shard_map/ppermute | solution.py:151
  117.5 3.8 %collective-permute-done.11 = bf16[24,2048]{1,0:T(8,128)(2,1)S(1)} collective-permute-done((bf16[24,2048]{1,0:T(8,128)(2,1)S(1)}, bf16[24,2048]{1,0:T(8,128)(2,1)S(1)}, u32[]{:S(2)}, u32[]{:S(2)}) %collective-permute-start.11) | collective-permute-done | bytes 98336 | tf_op jit(solution)/shard_map/ppermute | solution.py:151
  121.3 1.9 %collective-permute-start.12 = (bf16[24,2048]{1,0:T(8,128)(2,1)S(1)}, bf16[24,2048]{1,0:T(8,128)(2,1)S(1)}, u32[]{:S(2)}, u32[]{:S(2)}) collective-permute-start(bf16[24,2048]{1,0:T(8,128)(2,1)S(1)} %fusion.8), channel_id=1, source_target_pairs={{0,3},{1,4},{2,5},{3,6},{4,7},{5,8},{6,9},{7,10},{8,11},{9,12},{10... | collective-permute-start | bytes 294920 | tf_op jit(solution)/shard_map/ppermute | solution.py:151
  123.3 1.8 %shard_map.90 = (bf16[128,2048]{1,0:T(8,128)(2,1)}, f32[2,128]{1,0:T(2,128)}) custom-call(s32[2,128]{1,0:T(2,128)S(1)} %bitcast.32, f32[2,128]{1,0:T(2,128)S(1)} %bitcast.34, bf16[128,2048]{1,0:T(8,128)(2,1)S(1)} %copy-done.4, bf16[256,2560]{1,0:T(8,128)(2,1)S(1)} %bitcast.30), custom_call_target="tpu_custom_call" | custom-call | flops 536870912 | bytes 3000000 | tf_op jit(solution)/shard_map/pallas_call | solution.py:343
  125.1 6.9 %collective-permute-start.13 = (bf16[24,2048]{1,0:T(8,128)(2,1)S(1)}, bf16[24,2048]{1,0:T(8,128)(2,1)S(1)}, u32[]{:S(2)}, u32[]{:S(2)}) collective-permute-start(bf16[24,2048]{1,0:T(8,128)(2,1)S(1)} %fusion.9), channel_id=1, source_target_pairs={{0,29},{1,30},{2,31},{3,0},{4,1},{5,2},{6,3},{7,4},{8,5},{9,6},{10... | collective-permute-start | bytes 294920 | tf_op jit(solution)/shard_map/ppermute | solution.py:151
  132.1 6.3 %shard_map.91 = bf16[320,768]{1,0:T(8,128)(2,1)} custom-call(bf16[256,1280]{1,0:T(8,128)(2,1)} %bitcast.18, bf16[256,1280]{1,0:T(8,128)(2,1)} %bitcast.19, bf16[768,2048]{1,0:T(8,128)(2,1)} %bitcast.26, bf16[256,1280]{1,0:T(8,128)(2,1)} %bitcast.24, bf16[256,1280]{1,0:T(8,128)(2,1)} %bitcast.25, bf16[768,2048]{1,0:T(8,128)(2,1)} %bitcast.27), custom_call_target="tpu_custom_call" | custom-call | flops 2013265920 | bytes 6000000 | tf_op jit(solution)/shard_map/pallas_call | solution.py:329
  (46 shorter events, 6.6 us)
Async XLA Ops:
  0.6 10.3 %copy-start.5 = (bf16[320,768]{1,0:T(8,128)(2,1)S(1)}, bf16[320,768]{1,0:T(8,128)(2,1)}, u32[]{:S(2)}) copy-start(bf16[320,768]{1,0:T(8,128)(2,1)} %hidden_ref.3) | copy-start | bytes 1474564
  3.5 19.9 %all-to-all-start = ((bf16[32,8,1280]{2,1,0:T(8,128)(2,1)}), bf16[32,8,1280]{2,1,0:T(8,128)(2,1)S(1)}, u32[]{:S(2)}, u32[]{:S(2)}) async-start(bf16[32,8,1280]{2,1,0:T(8,128)(2,1)} %bitcast.36), calls=%async_computation | async-start | bytes 1310720 | tf_op jit(solution)/shard_map/all_to_all | solution.py:239
  12.7 1.9 %copy-start.2 = (bf16[1,768,2048]{2,1,0:T(8,128)(2,1)S(1)}, bf16[1,768,2048]{2,1,0:T(8,128)(2,1)}, u32[]{:S(2)}) copy-start(bf16[1,768,2048]{2,1,0:T(8,128)(2,1)} %param.9) | copy-start | bytes 9437188
  17.8 1.1 copy-start.3
  23.4 26.0 %copy-start = (bf16[32,8,1280]{2,1,0:T(8,128)(2,1)}, bf16[32,8,1280]{2,1,0:T(8,128)(2,1)S(1)}, u32[]{:S(2)}) copy-start(bf16[32,8,1280]{2,1,0:T(8,128)(2,1)S(1)} %all-to-all-done) | copy-start | bytes 1966084
  23.4 16.7 %all-to-all-start.1 = ((bf16[32,8,1280]{2,1,0:T(8,128)(2,1)}), bf16[32,8,1280]{2,1,0:T(8,128)(2,1)S(1)}, u32[]{:S(2)}, u32[]{:S(2)}) async-start(bf16[32,8,1280]{2,1,0:T(8,128)(2,1)} %bitcast.35), calls=%async_computation.1 | async-start | bytes 1310720 | tf_op jit(solution)/shard_map/all_to_all | solution.py:239
  29.9 22.3 %collective-permute-start = (bf16[264,1024]{1,0:T(8,128)(2,1)}, bf16[264,1024]{1,0:T(8,128)(2,1)}, u32[]{:S(2)}, u32[]{:S(2)}) collective-permute-start(bf16[264,1024]{1,0:T(8,128)(2,1)} %get-tuple-element.36), channel_id=1, source_target_pairs={{0,31},{1,0},{2,1},{3,2},{4,3},{5,4},{6,5},{7,6},{8,7},{9,8},{10,9... | collective-permute-start | bytes 1622024 | tf_op jit(solution)/shard_map/ppermute | solution.py:151
  31.9 20.3 %collective-permute-start.1 = (bf16[240,1024]{1,0:T(8,128)(2,1)}, bf16[240,1024]{1,0:T(8,128)(2,1)}, u32[]{:S(2)}, u32[]{:S(2)}) collective-permute-start(bf16[240,1024]{1,0:T(8,128)(2,1)} %get-tuple-element.37), channel_id=1, source_target_pairs={{0,1},{1,2},{2,3},{3,4},{4,5},{5,6},{6,7},{7,8},{8,9},{9,10},{10,1... | collective-permute-start | bytes 1474568 | tf_op jit(solution)/shard_map/ppermute | solution.py:151
  40.0 9.3 %copy-start.1 = (bf16[32,8,1280]{2,1,0:T(8,128)(2,1)}, bf16[32,8,1280]{2,1,0:T(8,128)(2,1)S(1)}, u32[]{:S(2)}) copy-start(bf16[32,8,1280]{2,1,0:T(8,128)(2,1)S(1)} %all-to-all-done.1) | copy-start | bytes 1966084
  42.4 19.7 %collective-permute-start.3 = (bf16[240,1024]{1,0:T(8,128)(2,1)}, bf16[240,1024]{1,0:T(8,128)(2,1)}, u32[]{:S(2)}, u32[]{:S(2)}) collective-permute-start(bf16[240,1024]{1,0:T(8,128)(2,1)} %get-tuple-element.43), channel_id=1, source_target_pairs={{0,1},{1,2},{2,3},{3,4},{4,5},{5,6},{6,7},{7,8},{8,9},{9,10},{10,1... | collective-permute-start | bytes 1474568 | tf_op jit(solution)/shard_map/ppermute | solution.py:151
  46.2 15.9 %collective-permute-start.2 = (bf16[264,1024]{1,0:T(8,128)(2,1)}, bf16[264,1024]{1,0:T(8,128)(2,1)}, u32[]{:S(2)}, u32[]{:S(2)}) collective-permute-start(bf16[264,1024]{1,0:T(8,128)(2,1)} %get-tuple-element.38), channel_id=1, source_target_pairs={{0,31},{1,0},{2,1},{3,2},{4,3},{5,4},{6,5},{7,6},{8,7},{9,8},{10,9... | collective-permute-start | bytes 1622024 | tf_op jit(solution)/shard_map/ppermute | solution.py:151
  52.2 7.5 %copy-start.9 = (f32[264,1024]{1,0:T(8,128)S(1)}, f32[264,1024]{1,0:T(8,128)}, u32[]{:S(2)}) copy-start(f32[264,1024]{1,0:T(8,128)} %get-tuple-element.34) | copy-start | bytes 3244036
  52.2 71.0 %all-to-all-start.2 = ((bf16[32,8,2560]{2,1,0:T(8,128)(2,1)}), bf16[32,8,2560]{2,1,0:T(8,128)(2,1)S(1)}, u32[]{:S(2)}, u32[]{:S(2)}) async-start(bf16[32,8,2560]{2,1,0:T(8,128)(2,1)} %bitcast.29), calls=%async_computation.2 | async-start | bytes 2621440 | tf_op jit(solution)/shard_map/all_to_all | solution.py:239
  60.8 1.5 %copy-start.8 = (f32[264,1024]{1,0:T(8,128)S(1)}, f32[264,1024]{1,0:T(8,128)}, u32[]{:S(2)}) copy-start(f32[264,1024]{1,0:T(8,128)} %get-tuple-element.42) | copy-start | bytes 3244036
  63.4 19.6 %collective-permute-start.8 = (bf16[24,2048]{1,0:T(8,128)(2,1)S(1)}, bf16[24,2048]{1,0:T(8,128)(2,1)S(1)}, u32[]{:S(2)}, u32[]{:S(2)}) collective-permute-start(bf16[24,2048]{1,0:T(8,128)(2,1)S(1)} %pad_maximum_fusion.1), channel_id=1, source_target_pairs={{0,3},{1,4},{2,5},{3,6},{4,7},{5,8},{6,9},{7,10},{8,11},{9,12},{10... | collective-permute-start | bytes 294920 | tf_op jit(solution)/shard_map/ppermute | solution.py:151
  68.0 17.1 %collective-permute-start.4 = (bf16[24,2048]{1,0:T(8,128)(2,1)S(1)}, bf16[24,2048]{1,0:T(8,128)(2,1)S(1)}, u32[]{:S(2)}, u32[]{:S(2)}) collective-permute-start(bf16[24,2048]{1,0:T(8,128)(2,1)S(1)} %pad_maximum_fusion), channel_id=1, source_target_pairs={{0,29},{1,30},{2,31},{3,0},{4,1},{5,2},{6,3},{7,4},{8,5},{9,6},{10... | collective-permute-start | bytes 294920 | tf_op jit(solution)/shard_map/ppermute | solution.py:151
  83.1 11.7 %collective-permute-start.9 = (bf16[24,2048]{1,0:T(8,128)(2,1)S(1)}, bf16[24,2048]{1,0:T(8,128)(2,1)S(1)}, u32[]{:S(2)}, u32[]{:S(2)}) collective-permute-start(bf16[24,2048]{1,0:T(8,128)(2,1)S(1)} %fusion.5), channel_id=1, source_target_pairs={{0,3},{1,4},{2,5},{3,6},{4,7},{5,8},{6,9},{7,10},{8,11},{9,12},{10... | collective-permute-start | bytes 294920 | tf_op jit(solution)/shard_map/ppermute | solution.py:151
  85.1 38.2 %copy-start.4 = (bf16[128,2048]{1,0:T(8,128)(2,1)S(1)}, bf16[128,2048]{1,0:T(8,128)(2,1)}, u32[]{:S(2)}) copy-start(bf16[128,2048]{1,0:T(8,128)(2,1)} %cot_ref.3) | copy-start | bytes 1572868
  85.1 38.2 %copy-start.6 = (s32[128,2]{0,1:T(2,128)S(1)}, s32[128,2]{0,1:T(2,128)}, u32[]{:S(2)}) copy-start(s32[128,2]{0,1:T(2,128)} %param.6) | copy-start | bytes 3076
  85.1 38.2 %copy-start.7 = (f32[128,2]{0,1:T(2,128)S(1)}, f32[128,2]{0,1:T(2,128)}, u32[]{:S(2)}) copy-start(f32[128,2]{0,1:T(2,128)} %param.7) | copy-start | bytes 3076
  85.1 11.6 %collective-permute-start.5 = (bf16[24,2048]{1,0:T(8,128)(2,1)S(1)}, bf16[24,2048]{1,0:T(8,128)(2,1)S(1)}, u32[]{:S(2)}, u32[]{:S(2)}) collective-permute-start(bf16[24,2048]{1,0:T(8,128)(2,1)S(1)} %fusion), channel_id=1, source_target_pairs={{0,29},{1,30},{2,31},{3,0},{4,1},{5,2},{6,3},{7,4},{8,5},{9,6},{10... | collective-permute-start | bytes 294920 | tf_op jit(solution)/shard_map/ppermute | solution.py:151
  94.8 13.8 %collective-permute-start.10 = (bf16[24,2048]{1,0:T(8,128)(2,1)S(1)}, bf16[24,2048]{1,0:T(8,128)(2,1)S(1)}, u32[]{:S(2)}, u32[]{:S(2)}) collective-permute-start(bf16[24,2048]{1,0:T(8,128)(2,1)S(1)} %fusion.6), channel_id=1, source_target_pairs={{0,3},{1,4},{2,5},{3,6},{4,7},{5,8},{6,9},{7,10},{8,11},{9,12},{10... | collective-permute-start | bytes 294920 | tf_op jit(solution)/shard_map/ppermute | solution.py:151
  96.8 13.8 %collective-permute-start.6 = (bf16[24,2048]{1,0:T(8,128)(2,1)S(1)}, bf16[24,2048]{1,0:T(8,128)(2,1)S(1)}, u32[]{:S(2)}, u32[]{:S(2)}) collective-permute-start(bf16[24,2048]{1,0:T(8,128)(2,1)S(1)} %fusion.1), channel_id=1, source_target_pairs={{0,29},{1,30},{2,31},{3,0},{4,1},{5,2},{6,3},{7,4},{8,5},{9,6},{10... | collective-permute-start | bytes 294920 | tf_op jit(solution)/shard_map/ppermute | solution.py:151
  108.6 12.7 %collective-permute-start.11 = (bf16[24,2048]{1,0:T(8,128)(2,1)S(1)}, bf16[24,2048]{1,0:T(8,128)(2,1)S(1)}, u32[]{:S(2)}, u32[]{:S(2)}) collective-permute-start(bf16[24,2048]{1,0:T(8,128)(2,1)S(1)} %fusion.7), channel_id=1, source_target_pairs={{0,3},{1,4},{2,5},{3,6},{4,7},{5,8},{6,9},{7,10},{8,11},{9,12},{10... | collective-permute-start | bytes 294920 | tf_op jit(solution)/shard_map/ppermute | solution.py:151
  110.6 14.5 %collective-permute-start.7 = (bf16[24,2048]{1,0:T(8,128)(2,1)S(1)}, bf16[24,2048]{1,0:T(8,128)(2,1)S(1)}, u32[]{:S(2)}, u32[]{:S(2)}) collective-permute-start(bf16[24,2048]{1,0:T(8,128)(2,1)S(1)} %fusion.2), channel_id=1, source_target_pairs={{0,29},{1,30},{2,31},{3,0},{4,1},{5,2},{6,3},{7,4},{8,5},{9,6},{10... | collective-permute-start | bytes 294920 | tf_op jit(solution)/shard_map/ppermute | solution.py:151
  121.3 17.1 %collective-permute-start.12 = (bf16[24,2048]{1,0:T(8,128)(2,1)S(1)}, bf16[24,2048]{1,0:T(8,128)(2,1)S(1)}, u32[]{:S(2)}, u32[]{:S(2)}) collective-permute-start(bf16[24,2048]{1,0:T(8,128)(2,1)S(1)} %fusion.8), channel_id=1, source_target_pairs={{0,3},{1,4},{2,5},{3,6},{4,7},{5,8},{6,9},{7,10},{8,11},{9,12},{10... | collective-permute-start | bytes 294920 | tf_op jit(solution)/shard_map/ppermute | solution.py:151
  125.1 13.2 %collective-permute-start.13 = (bf16[24,2048]{1,0:T(8,128)(2,1)S(1)}, bf16[24,2048]{1,0:T(8,128)(2,1)S(1)}, u32[]{:S(2)}, u32[]{:S(2)}) collective-permute-start(bf16[24,2048]{1,0:T(8,128)(2,1)S(1)} %fusion.9), channel_id=1, source_target_pairs={{0,29},{1,30},{2,31},{3,0},{4,1},{5,2},{6,3},{7,4},{8,5},{9,6},{10... | collective-permute-start | bytes 294920 | tf_op jit(solution)/shard_map/ppermute | solution.py:151
